TPU v7x, 256 devices: a whole 4x4x8 slice. The times are simulated.
256 devices in a mesh: frame: 32 (over x_hi, z, core), space: 8 (over y, x_lo).
Axes of the slice: x: 4 (x_hi: 2, x_lo: 2; x = x_hi * 2 + x_lo), y: 4, z: 8, core: 2. Of those that a mesh axis runs over, the one named last changes fastest.
Arguments:
- frames_in: bfloat16 [128, 16, 64, 320], P('frame', 'space'), may hold values from -15 to 15
- kernel_space: bfloat16 [3, 3, 320, 320], replicated, may hold values from -0.109375 to 0.109375
- kernel_time: bfloat16 [3, 320, 320], replicated, may hold values from -0.1875 to 0.1875
- norm_gain: float32 [320], replicated, may hold values from 0.5 to 1.5
- proj_in: bfloat16 [320, 1280], replicated, may hold values from -0.3125 to 0.3125
- proj_query: bfloat16 [1280, 640], replicated, may hold values from -0.15625 to 0.15625
- proj_key: bfloat16 [1280, 640], replicated, may hold values from -0.15625 to 0.15625
- proj_value: bfloat16 [1280, 640], replicated, may hold values from -0.15625 to 0.15625
- proj_out: bfloat16 [640, 1280], replicated, may hold values from -0.25 to 0.25
- frame_bias: float32 [10, 32, 32], replicated, may hold values from -400 to 400
- cotangent: bfloat16 [32, 8, 32, 1280], P('frame', 'space'), may hold values from -24 to 24
Outputs:
- coarse_out: bfloat16 [32, 8, 32, 1280], P('frame', 'space')
- grad_frames: bfloat16 [128, 16, 64, 320], P('frame', 'space')
- grad_gain: float32 [320], replicated
All inputs are finite; a program needn't handle non-finite values.
Results may differ from a plain program's by a relative error of at most 0.015.
Values may be sent and summed in bfloat16 or wider, within the bound.
No kernel may reach another device: no remote copies, remote signals or barrier semaphores. Data moves between devices by JAX's collectives and lax.ppermute only.
A program may use at most 64 MiB of HBM per device.

v0:
```python
import math

import jax
import jax.numpy as jnp
from jax import lax
from jax.sharding import PartitionSpec as P

HEADS = 10
GROUPS = 32


def with_halo(cells, sides, width):
    for axis, dim in sides:
        count = lax.axis_size(axis)
        ends = count - 1
        head = lax.slice_in_dim(cells, 0, width, axis=dim)
        tail = lax.slice_in_dim(cells, cells.shape[dim] - width, cells.shape[dim], axis=dim)
        cells = jnp.concatenate(
            [
                lax.ppermute(tail, axis, [(i, (i + 1) % count) for i in range(ends)]),
                cells,
                lax.ppermute(head, axis, [((i + 1) % count, i) for i in range(ends)]),
            ],
            axis=dim,
        )
    return cells


def dot_transposed(matrix, weight):
    return lax.dot_general(
        matrix, weight, (((1,), (1,)), ((), ())), preferred_element_type=jnp.float32
    )


def project(tensor, weight):
    flat = tensor.reshape(-1, tensor.shape[-1])
    return jnp.dot(flat, weight, preferred_element_type=jnp.float32).reshape(
        tensor.shape[:-1] + (weight.shape[1],)
    )


def project_back(tensor, weight):
    flat = tensor.reshape(-1, tensor.shape[-1])
    return dot_transposed(flat, weight).reshape(tensor.shape[:-1] + (weight.shape[0],))


def space_conv(padded, kernel, transpose):
    frames, padded_rows, padded_cols, channels = padded.shape
    row_count = padded_rows - 2
    col_count = padded_cols - 2
    running = jnp.zeros((frames * row_count * col_count, channels), jnp.float32)
    for row_off in range(3):
        for col_off in range(3):
            if transpose:
                window = padded[
                    :, 2 - row_off : 2 - row_off + row_count, 2 - col_off : 2 - col_off + col_count
                ]
                running = running + dot_transposed(
                    window.reshape(-1, channels), kernel[row_off, col_off]
                )
            else:
                window = padded[:, row_off : row_off + row_count, col_off : col_off + col_count]
                running = running + jnp.dot(
                    window.reshape(-1, channels),
                    kernel[row_off, col_off],
                    preferred_element_type=jnp.float32,
                )
    return running.reshape(frames, row_count, col_count, channels)


def time_conv(padded, kernel, transpose):
    frames = padded.shape[0] - 2
    channels = padded.shape[3]
    running = jnp.zeros((frames * padded.shape[1] * padded.shape[2], channels), jnp.float32)
    for tap_index in range(3):
        if transpose:
            window = padded[2 - tap_index : 2 - tap_index + frames].reshape(-1, channels)
            running = running + dot_transposed(window, kernel[tap_index])
        else:
            window = padded[tap_index : tap_index + frames].reshape(-1, channels)
            running = running + jnp.dot(
                window, kernel[tap_index], preferred_element_type=jnp.float32
            )
    return running.reshape((frames,) + padded.shape[1:])


def group_reduce(tensor):
    per_channel = jnp.sum(tensor, axis=(1, 2))
    return jnp.sum(per_channel.reshape(tensor.shape[0], GROUPS, -1), axis=2)


def spread(statistic, channels):
    return jnp.repeat(statistic, channels // GROUPS, axis=1)[:, None, None, :]


def pool(tensor):
    frames, row_count, col_count, channels = tensor.shape
    return jnp.mean(
        tensor.reshape(frames // 4, 4, row_count // 2, 2, col_count // 2, 2, channels),
        axis=(1, 3, 5),
    )


def unpool(tensor):
    coarse_frames, half_rows, half_cols, channels = tensor.shape
    grown = jnp.broadcast_to(
        tensor[:, None, :, None, :, None, :],
        (coarse_frames, 4, half_rows, 2, half_cols, 2, channels),
    )
    return grown.reshape(coarse_frames * 4, half_rows * 2, half_cols * 2, channels) / 16.0


def split_heads(tensor):
    return tensor.reshape(tensor.shape[0], tensor.shape[1], HEADS, -1)


def probabilities(queries, keys_in, bias):
    factor = 1.0 / math.sqrt(queries.shape[-1] // HEADS)
    scores = (
        jnp.einsum(
            "ipnd,jpnd->pnij",
            split_heads(queries),
            split_heads(keys_in),
            preferred_element_type=jnp.float32,
        )
        * factor
        + bias[None]
    )
    row_max = jnp.max(scores, axis=-1, keepdims=True)
    expd = jnp.exp(scores - row_max)
    return (expd / jnp.sum(expd, axis=-1, keepdims=True), factor)


def attend(queries, keys_in, values_in, bias):
    weights, factor = probabilities(queries, keys_in, bias)
    rounded = weights.astype(jnp.bfloat16)
    blended = jnp.einsum(
        "pnij,jpnd->ipnd", rounded, split_heads(values_in), preferred_element_type=jnp.float32
    )
    return blended.reshape(queries.shape).astype(jnp.bfloat16)


def attend_back(queries, keys_in, values_in, bias, grad_out):
    weights, factor = probabilities(queries, keys_in, bias)
    rounded = weights.astype(jnp.bfloat16)
    grad_heads = split_heads(grad_out)
    grad_weights = jnp.einsum(
        "ipnd,jpnd->pnij", grad_heads, split_heads(values_in), preferred_element_type=jnp.float32
    )
    grad_values = jnp.einsum(
        "pnij,ipnd->jpnd", rounded, grad_heads, preferred_element_type=jnp.float32
    )
    grad_scores = weights * (grad_weights - jnp.sum(weights * grad_weights, axis=-1, keepdims=True))
    grad_rounded = grad_scores.astype(jnp.bfloat16)
    grad_queries = (
        jnp.einsum(
            "pnij,jpnd->ipnd",
            grad_rounded,
            split_heads(keys_in),
            preferred_element_type=jnp.float32,
        )
        * factor
    )
    grad_keys = (
        jnp.einsum(
            "pnij,ipnd->jpnd",
            grad_rounded,
            split_heads(queries),
            preferred_element_type=jnp.float32,
        )
        * factor
    )
    out_shape = queries.shape
    return (
        grad_queries.reshape(out_shape).astype(jnp.bfloat16),
        grad_keys.reshape(out_shape).astype(jnp.bfloat16),
        grad_values.reshape(out_shape).astype(jnp.bfloat16),
    )


def pad_columns(tensor):
    return jnp.pad(tensor, ((0, 0), (0, 0), (1, 1), (0, 0)))


def row_rims(tensor):
    extended = with_halo(tensor, (("space", 1),), 1)
    return pad_columns(extended)


def frame_rims(tensor):
    return with_halo(tensor, (("frame", 0),), 1)


def group_totals(first_term, second_term):
    return lax.psum((group_reduce(first_term), group_reduce(second_term)), "space")


def coarse_grads(
    cot_rows, grad_queries, grad_keys, grad_values, proj_in, proj_query, proj_key, proj_value
):
    grad_coarse = (
        cot_rows.astype(jnp.float32)
        + project_back(grad_queries, proj_query)
        + project_back(grad_keys, proj_key)
        + project_back(grad_values, proj_value)
    ).astype(jnp.bfloat16)
    return project_back(grad_coarse, proj_in).astype(jnp.bfloat16)


def local(
    frames_in,
    kernel_space,
    kernel_time,
    norm_gain,
    proj_in,
    proj_query,
    proj_key,
    proj_value,
    proj_out,
    frame_bias,
    cotangent,
):
    frames, row_count, width, channels = frames_in.shape
    cell_count = row_count * lax.axis_size("space") * width * (channels // GROUPS)
    spatial = space_conv(row_rims(frames_in), kernel_space, False).astype(jnp.bfloat16)
    temporal = time_conv(frame_rims(spatial), kernel_time, False)
    group_sum, group_square = group_totals(temporal, temporal * temporal)
    group_mean = group_sum / cell_count
    inv_std = lax.rsqrt(group_square / cell_count - group_mean * group_mean + 1e-05)
    normed = (temporal - spread(group_mean, channels)) * spread(inv_std, channels)
    gated = normed * norm_gain
    sigmoid_val = jax.nn.sigmoid(gated)
    fine_out = frames_in.astype(jnp.float32) + gated * sigmoid_val
    pooled = pool(fine_out).astype(jnp.bfloat16)
    coarse_frames, half_rows, half_cols = pooled.shape[:3]
    pixels = half_rows * half_cols
    pooled = pooled.reshape(coarse_frames, pixels, channels)
    cot_rows = cotangent.reshape(coarse_frames, pixels, -1)
    coarse_in = lax.optimization_barrier(project(pooled, proj_in).astype(jnp.bfloat16))
    queries = project(coarse_in, proj_query).astype(jnp.bfloat16)
    keys_out = project(coarse_in, proj_key).astype(jnp.bfloat16)
    values_out = project(coarse_in, proj_value).astype(jnp.bfloat16)
    query_px, key_px, value_px = (
        lax.all_to_all(queries, "frame", split_axis=1, concat_axis=0, tiled=True),
        lax.all_to_all(keys_out, "frame", split_axis=1, concat_axis=0, tiled=True),
        lax.all_to_all(values_out, "frame", split_axis=1, concat_axis=0, tiled=True),
    )
    blended = attend(query_px, key_px, value_px, frame_bias)
    blended_frames = lax.all_to_all(blended, "frame", split_axis=0, concat_axis=1, tiled=True)
    coarse_out = (coarse_in.astype(jnp.float32) + project(blended_frames, proj_out)).astype(
        jnp.bfloat16
    )
    grad_heads = project_back(cot_rows, proj_out).astype(jnp.bfloat16)
    grad_pixels = lax.all_to_all(grad_heads, "frame", split_axis=1, concat_axis=0, tiled=True)
    grad_q_px, grad_k_px, grad_v_px = attend_back(
        query_px, key_px, value_px, frame_bias, grad_pixels
    )
    grad_queries, grad_keys, grad_values = (
        lax.all_to_all(grad_q_px, "frame", split_axis=0, concat_axis=1, tiled=True),
        lax.all_to_all(grad_k_px, "frame", split_axis=0, concat_axis=1, tiled=True),
        lax.all_to_all(grad_v_px, "frame", split_axis=0, concat_axis=1, tiled=True),
    )
    grad_pooled = coarse_grads(
        cot_rows, grad_queries, grad_keys, grad_values, proj_in, proj_query, proj_key, proj_value
    )
    grad_pooled = lax.optimization_barrier(grad_pooled)
    grad_fine = unpool(
        grad_pooled.astype(jnp.float32).reshape(coarse_frames, half_rows, half_cols, channels)
    )
    grad_gated = grad_fine * sigmoid_val * (1.0 + gated * (1.0 - sigmoid_val))
    grad_gain = lax.psum(jnp.sum(grad_gated * normed, axis=(0, 1, 2)), ("frame", "space"))
    grad_normed = grad_gated * norm_gain
    first_total, second_total = group_totals(grad_normed, grad_normed * normed)
    grad_temporal = (
        spread(inv_std, channels)
        * (
            grad_normed
            - spread(first_total / cell_count, channels)
            - normed * spread(second_total / cell_count, channels)
        )
    ).astype(jnp.bfloat16)
    grad_spatial = time_conv(frame_rims(grad_temporal), kernel_time, True).astype(jnp.bfloat16)
    grad_frames = (grad_fine + space_conv(row_rims(grad_spatial), kernel_space, True)).astype(
        jnp.bfloat16
    )
    return (coarse_out.reshape(cotangent.shape), grad_frames, grad_gain)


def solution(mesh):
    in_specs = (
        P("frame", "space", None, None),
        P(),
        P(),
        P(),
        P(),
        P(),
        P(),
        P(),
        P(),
        P(),
        P("frame", "space", None, None),
    )
    out_specs = (P("frame", "space", None, None), P("frame", "space", None, None), P())
    return jax.shard_map(local, mesh=mesh, in_specs=in_specs, out_specs=out_specs, check_vma=False)
```

profile of v0, /device:TPU:1, one launch (start us, length us, event | category | flops | bytes accessed | tf_op | source)
XLA Modules:
  0.0 360.0 jit_solution(5539269563116250990)
XLA Ops:
  5.1 12.6 %all-to-all-start.4 = ((bf16[32,2,320]{2,1,0:T(2,128)(2,1)}), bf16[32,2,320]{2,1,0:T(2,128)(2,1)S(1)}, u32[]{:S(2)}, u32[]{:S(2)}) async-start(bf16[32,2,320]{2,1,0:T(2,128)(2,1)} %reshape.461), calls=%async_computation.4 | async-start | bytes 98304 | tf_op jit(solution)/shard_map/all_to_all | solution.py:254
  22.1 5.0 %all-to-all-done.4 = bf16[32,2,320]{2,1,0:T(2,128)(2,1)S(1)} async-done(((bf16[32,2,320]{2,1,0:T(2,128)(2,1)}), bf16[32,2,320]{2,1,0:T(2,128)(2,1)S(1)}, u32[]{:S(2)}, u32[]{:S(2)}) %all-to-all-start.4) | async-done | bytes 40992 | tf_op jit(solution)/shard_map/all_to_all | solution.py:254
  28.2 3.1 collective-permute-done.1
  38.4 2.9 collective-permute-start.3
  41.3 3.2 collective-permute-start.2
  51.5 13.5 %all-reduce.3 = (f32[4,32]{1,0:T(4,128)S(1)}, f32[4,32]{1,0:T(4,128)S(1)}) all-reduce(f32[4,32]{1,0:T(4,128)S(1)} %reduce_sum.122, f32[4,32]{1,0:T(4,128)S(1)} %reduce_sum.120), channel_id=1, replica_groups=mesh['frame'=32,'space'=8] {'space'}, use_global_device_ids=true, to_apply=%region_5.6 | all-reduce | flops 256 | bytes 2048 | tf_op jit(solution)/shard_map/psum | solution.py:195
  71.7 15.6 %all-to-all-start.1 = ((bf16[32,2,320]{2,1,0:T(2,128)(2,1)}), bf16[32,2,320]{2,1,0:T(2,128)(2,1)S(1)}, u32[]{:S(2)}, u32[]{:S(2)}) async-start(bf16[32,2,320]{2,1,0:T(2,128)(2,1)} %reshape.457), calls=%async_computation.1 | async-start | bytes 98304 | tf_op jit(solution)/shard_map/all_to_all | solution.py:244
  112.5 9.8 %all-to-all-start.2 = ((bf16[32,2,320]{2,1,0:T(2,128)(2,1)}), bf16[32,2,320]{2,1,0:T(2,128)(2,1)S(1)}, u32[]{:S(2)}, u32[]{:S(2)}) async-start(bf16[32,2,320]{2,1,0:T(2,128)(2,1)} %reshape.455), calls=%async_computation.2 | async-start | bytes 98304 | tf_op jit(solution)/shard_map/all_to_all | solution.py:245
  123.3 8.5 %all-to-all-done.2 = bf16[32,2,320]{2,1,0:T(2,128)(2,1)S(1)} async-done(((bf16[32,2,320]{2,1,0:T(2,128)(2,1)}), bf16[32,2,320]{2,1,0:T(2,128)(2,1)S(1)}, u32[]{:S(2)}, u32[]{:S(2)}) %all-to-all-start.2) | async-done | bytes 40992 | tf_op jit(solution)/shard_map/all_to_all | solution.py:245
  131.8 4.5 %all-to-all-start = ((bf16[32,2,320]{2,1,0:T(2,128)(2,1)}), bf16[32,2,320]{2,1,0:T(2,128)(2,1)S(1)}, u32[]{:S(2)}, u32[]{:S(2)}) async-start(bf16[32,2,320]{2,1,0:T(2,128)(2,1)} %reshape.453), calls=%async_computation | async-start | bytes 98304 | tf_op jit(solution)/shard_map/all_to_all | solution.py:246
  136.7 9.3 %all-to-all-done = bf16[32,2,320]{2,1,0:T(2,128)(2,1)S(1)} async-done(((bf16[32,2,320]{2,1,0:T(2,128)(2,1)}), bf16[32,2,320]{2,1,0:T(2,128)(2,1)S(1)}, u32[]{:S(2)}, u32[]{:S(2)}) %all-to-all-start) | async-done | bytes 40992 | tf_op jit(solution)/shard_map/all_to_all | solution.py:246
  156.7 4.5 %all-to-all-start.5 = ((bf16[32,2,320]{2,1,0:T(2,128)(2,1)}), bf16[32,2,320]{2,1,0:T(2,128)(2,1)S(1)}, u32[]{:S(2)}, u32[]{:S(2)}) async-start(bf16[32,2,320]{2,1,0:T(2,128)(2,1)} %reshape.463), calls=%async_computation.5 | async-start | bytes 98304 | tf_op jit(solution)/shard_map/all_to_all | solution.py:259
  170.8 8.6 %all-to-all-start.6 = ((bf16[32,2,320]{2,1,0:T(2,128)(2,1)}), bf16[32,2,320]{2,1,0:T(2,128)(2,1)S(1)}, u32[]{:S(2)}, u32[]{:S(2)}) async-start(bf16[32,2,320]{2,1,0:T(2,128)(2,1)} %reshape.465), calls=%async_computation.6 | async-start | bytes 98304 | tf_op jit(solution)/shard_map/all_to_all | solution.py:260
  181.0 7.8 %all-to-all-done.6 = bf16[32,2,320]{2,1,0:T(2,128)(2,1)S(1)} async-done(((bf16[32,2,320]{2,1,0:T(2,128)(2,1)}), bf16[32,2,320]{2,1,0:T(2,128)(2,1)S(1)}, u32[]{:S(2)}, u32[]{:S(2)}) %all-to-all-start.6) | async-done | bytes 40992 | tf_op jit(solution)/shard_map/all_to_all | solution.py:260
  188.8 5.2 %all-to-all-start.7 = ((bf16[32,2,320]{2,1,0:T(2,128)(2,1)}), bf16[32,2,320]{2,1,0:T(2,128)(2,1)}, u32[]{:S(2)}, u32[]{:S(2)}) async-start(bf16[32,2,320]{2,1,0:T(2,128)(2,1)} %reshape.467), calls=%async_computation.7 | async-start | bytes 98304 | tf_op jit(solution)/shard_map/all_to_all | solution.py:261
  196.8 6.9 %all-to-all-done.7 = bf16[32,2,320]{2,1,0:T(2,128)(2,1)} async-done(((bf16[32,2,320]{2,1,0:T(2,128)(2,1)}), bf16[32,2,320]{2,1,0:T(2,128)(2,1)}, u32[]{:S(2)}, u32[]{:S(2)}) %all-to-all-start.7) | async-done | bytes 40992 | tf_op jit(solution)/shard_map/all_to_all | solution.py:261
  203.7 5.2 %all-to-all-start.3 = ((bf16[32,2,320]{2,1,0:T(2,128)(2,1)}), bf16[32,2,320]{2,1,0:T(2,128)(2,1)}, u32[]{:S(2)}, u32[]{:S(2)}) async-start(bf16[32,2,320]{2,1,0:T(2,128)(2,1)} %reshape.459), calls=%async_computation.3 | async-start | bytes 98304 | tf_op jit(solution)/shard_map/all_to_all | solution.py:249
  220.9 12.9 %all-reduce.2 = (f32[4,32]{1,0:T(4,128)S(1)}, f32[4,32]{1,0:T(4,128)S(1)}) all-reduce(f32[4,32]{1,0:T(4,128)S(1)} %reduce_sum.131, f32[4,32]{1,0:T(4,128)S(1)} %reduce_sum.129), channel_id=1, replica_groups=mesh['frame'=32,'space'=8] {'space'}, use_global_device_ids=true, to_apply=%region_16.17 | all-reduce | flops 256 | bytes 2048 | tf_op jit(solution)/shard_map/psum | solution.py:195
  237.5 5.7 %collective-permute-start.4 = (bf16[1,2,64,320]{3,2,1,0:T(8,128)(2,1)}, bf16[1,2,64,320]{3,2,1,0:T(8,128)(2,1)}, u32[]{:S(2)}, u32[]{:S(2)}) collective-permute-start(bf16[1,2,64,320]{3,2,1,0:T(8,128)(2,1)} %get-tuple-element.29), channel_id=1, source_target_pairs={{8,0},{16,8},{24,16},{32,24},{40,32},{48,40},{56,48},{64,56},{72,6... | collective-permute-start | bytes 245768 | tf_op jit(solution)/shard_map/ppermute | solution.py:22
  243.2 2.9 collective-permute-start.5
  249.9 3.6 %fusion.35 = f32[512,320]{0,1:T(8,128)} fusion(f32[512,320]{0,1:T(8,128)} %copy.223, f32[512,320]{0,1:T(8,128)} %copy.222, f32[512,320]{0,1:T(8,128)} %copy.221, f32[512,320]{0,1:T(8,128)} %copy.220, f32[512,320]{0,1:T(8,128)S(1)} %fusion.11, f32[512,320]{0,1:T(8,128)} %copy.218, f32[320]{0:T(512)} %param.14, bf16[3,320,320]{2,1,0:T(8,128)(2,1)} %param.13), kind=kOutput, calls=%fused_computation.89 | convolution fusion | flops 107642880 | bytes 4835328 | tf_op jit(solution)/shard_map/dot_general | solution.py:30
  255.5 76.7 %psum.39 = f32[320]{0:T(512)} all-reduce(f32[320]{0:T(512)S(1)} %multiply_reduce_fusion.1), channel_id=1, replica_groups=mesh['frame'=32,'space'=8] {'frame','space'}, use_global_device_ids=true, to_apply=%region_18.19 | all-reduce | flops 320 | bytes 2560 | tf_op jit(solution)/shard_map/psum | solution.py:271
  340.1 3.0 collective-permute-start.6
  346.7 6.4 %collective-permute-done.7 = bf16[4,1,64,320]{3,2,1,0:T(8,128)(2,1)S(1)} collective-permute-done((bf16[4,1,64,320]{3,2,1,0:T(8,128)(2,1)S(1)}, bf16[4,1,64,320]{3,2,1,0:T(8,128)(2,1)S(1)}, u32[]{:S(2)}, u32[]{:S(2)}) %collective-permute-start.7) | collective-permute-done | bytes 163872 | tf_op jit(solution)/shard_map/ppermute | solution.py:22
  (205 shorter events, 121.1 us)
Async XLA Ops:
  0.6 69.0 %copy-start = (bf16[1280,640]{1,0:T(8,128)(2,1)S(1)}, bf16[1280,640]{1,0:T(8,128)(2,1)}, u32[]{:S(2)}) copy-start(bf16[1280,640]{1,0:T(8,128)(2,1)} %param.16) | copy-start | bytes 4915204
  0.6 17.0 %copy-start.1 = (bf16[4,2,64,320]{3,2,1,0:T(8,128)(2,1)S(1)}, bf16[4,2,64,320]{3,2,1,0:T(8,128)(2,1)}, u32[]{:S(2)}) copy-start(bf16[4,2,64,320]{3,2,1,0:T(8,128)(2,1)} %param.11) | copy-start | bytes 983044
  0.7 20.6 %copy-start.18 = (f32[10,32,32]{2,1,0:T(8,128)S(1)}, f32[10,32,32]{2,1,0:T(8,128)}, u32[]{:S(2)}) copy-start(f32[10,32,32]{2,1,0:T(8,128)} %param.20) | copy-start | bytes 122884
  5.1 22.0 %all-to-all-start.4 = ((bf16[32,2,320]{2,1,0:T(2,128)(2,1)}), bf16[32,2,320]{2,1,0:T(2,128)(2,1)S(1)}, u32[]{:S(2)}, u32[]{:S(2)}) async-start(bf16[32,2,320]{2,1,0:T(2,128)(2,1)} %reshape.461), calls=%async_computation.4 | async-start | bytes 98304 | tf_op jit(solution)/shard_map/all_to_all | solution.py:254
  17.7 10.5 %collective-permute-start = (bf16[4,1,64,320]{3,2,1,0:T(8,128)(2,1)S(1)}, bf16[4,1,64,320]{3,2,1,0:T(8,128)(2,1)S(1)}, u32[]{:S(2)}, u32[]{:S(2)}) collective-permute-start(bf16[4,1,64,320]{3,2,1,0:T(8,128)(2,1)S(1)} %get-tuple-element.35), channel_id=1, source_target_pairs={{0,1},{1,2},{2,3},{3,4},{4,5},{5,6},{6,7},{8,9},{9,10},{10,11},{11... | collective-permute-start | bytes 491528 | tf_op jit(solution)/shard_map/ppermute | solution.py:20
  20.0 11.3 %collective-permute-start.1 = (bf16[4,1,64,320]{3,2,1,0:T(8,128)(2,1)S(1)}, bf16[4,1,64,320]{3,2,1,0:T(8,128)(2,1)S(1)}, u32[]{:S(2)}, u32[]{:S(2)}) collective-permute-start(bf16[4,1,64,320]{3,2,1,0:T(8,128)(2,1)S(1)} %get-tuple-element.36), channel_id=1, source_target_pairs={{1,0},{2,1},{3,2},{4,3},{5,4},{6,5},{7,6},{9,8},{10,9},{11,10},{12... | collective-permute-start | bytes 491528 | tf_op jit(solution)/shard_map/ppermute | solution.py:22
  36.5 8.0 %copy-start.12 = (bf16[3,320,320]{2,1,0:T(8,128)(2,1)S(1)}, bf16[3,320,320]{2,1,0:T(8,128)(2,1)}, u32[]{:S(2)}) copy-start(bf16[3,320,320]{2,1,0:T(8,128)(2,1)} %param.13) | copy-start | bytes 1843204
  38.4 7.5 %collective-permute-start.3 = (bf16[1,2,64,320]{3,2,1,0:T(8,128)(2,1)}, bf16[1,2,64,320]{3,2,1,0:T(8,128)(2,1)}, u32[]{:S(2)}, u32[]{:S(2)}) collective-permute-start(bf16[1,2,64,320]{3,2,1,0:T(8,128)(2,1)} %bitcast.23), channel_id=1, source_target_pairs={{8,0},{16,8},{24,16},{32,24},{40,32},{48,40},{56,48},{64,56},{72,6... | collective-permute-start | bytes 245768 | tf_op jit(solution)/shard_map/ppermute | solution.py:22
  41.3 5.1 %collective-permute-start.2 = (bf16[1,2,64,320]{3,2,1,0:T(8,128)(2,1)}, bf16[1,2,64,320]{3,2,1,0:T(8,128)(2,1)}, u32[]{:S(2)}, u32[]{:S(2)}) collective-permute-start(bf16[1,2,64,320]{3,2,1,0:T(8,128)(2,1)} %bitcast.18), channel_id=1, source_target_pairs={{0,8},{8,16},{16,24},{24,32},{32,40},{40,48},{48,56},{56,64},{64,7... | collective-permute-start | bytes 245768 | tf_op jit(solution)/shard_map/ppermute | solution.py:20
  71.7 40.8 %all-to-all-start.1 = ((bf16[32,2,320]{2,1,0:T(2,128)(2,1)}), bf16[32,2,320]{2,1,0:T(2,128)(2,1)S(1)}, u32[]{:S(2)}, u32[]{:S(2)}) async-start(bf16[32,2,320]{2,1,0:T(2,128)(2,1)} %reshape.457), calls=%async_computation.1 | async-start | bytes 98304 | tf_op jit(solution)/shard_map/all_to_all | solution.py:244
  98.0 5.4 %copy-start.15 = (f32[4,320]{1,0:T(4,128)S(1)}, f32[4,320]{1,0:T(4,128)}, u32[]{:S(2)}) copy-start(f32[4,320]{1,0:T(4,128)} %copy-done.14) | copy-start | bytes 15364
  112.5 19.3 %all-to-all-start.2 = ((bf16[32,2,320]{2,1,0:T(2,128)(2,1)}), bf16[32,2,320]{2,1,0:T(2,128)(2,1)S(1)}, u32[]{:S(2)}, u32[]{:S(2)}) async-start(bf16[32,2,320]{2,1,0:T(2,128)(2,1)} %reshape.455), calls=%async_computation.2 | async-start | bytes 98304 | tf_op jit(solution)/shard_map/all_to_all | solution.py:245
  131.8 14.1 %all-to-all-start = ((bf16[32,2,320]{2,1,0:T(2,128)(2,1)}), bf16[32,2,320]{2,1,0:T(2,128)(2,1)S(1)}, u32[]{:S(2)}, u32[]{:S(2)}) async-start(bf16[32,2,320]{2,1,0:T(2,128)(2,1)} %reshape.453), calls=%async_computation | async-start | bytes 98304 | tf_op jit(solution)/shard_map/all_to_all | solution.py:246
  156.7 14.1 %all-to-all-start.5 = ((bf16[32,2,320]{2,1,0:T(2,128)(2,1)}), bf16[32,2,320]{2,1,0:T(2,128)(2,1)S(1)}, u32[]{:S(2)}, u32[]{:S(2)}) async-start(bf16[32,2,320]{2,1,0:T(2,128)(2,1)} %reshape.463), calls=%async_computation.5 | async-start | bytes 98304 | tf_op jit(solution)/shard_map/all_to_all | solution.py:259
  170.8 18.0 %all-to-all-start.6 = ((bf16[32,2,320]{2,1,0:T(2,128)(2,1)}), bf16[32,2,320]{2,1,0:T(2,128)(2,1)S(1)}, u32[]{:S(2)}, u32[]{:S(2)}) async-start(bf16[32,2,320]{2,1,0:T(2,128)(2,1)} %reshape.465), calls=%async_computation.6 | async-start | bytes 98304 | tf_op jit(solution)/shard_map/all_to_all | solution.py:260
  188.8 14.9 %all-to-all-start.7 = ((bf16[32,2,320]{2,1,0:T(2,128)(2,1)}), bf16[32,2,320]{2,1,0:T(2,128)(2,1)}, u32[]{:S(2)}, u32[]{:S(2)}) async-start(bf16[32,2,320]{2,1,0:T(2,128)(2,1)} %reshape.467), calls=%async_computation.7 | async-start | bytes 98304 | tf_op jit(solution)/shard_map/all_to_all | solution.py:261
  203.7 50.3 %all-to-all-start.3 = ((bf16[32,2,320]{2,1,0:T(2,128)(2,1)}), bf16[32,2,320]{2,1,0:T(2,128)(2,1)}, u32[]{:S(2)}, u32[]{:S(2)}) async-start(bf16[32,2,320]{2,1,0:T(2,128)(2,1)} %reshape.459), calls=%async_computation.3 | async-start | bytes 98304 | tf_op jit(solution)/shard_map/all_to_all | solution.py:249
  213.0 5.9 %copy-start.19 = (f32[320]{0:T(512)S(1)}, f32[320]{0:T(512)}, u32[]{:S(2)}) copy-start(f32[320]{0:T(512)} %param.14) | copy-start | bytes 3844
  237.5 94.8 %collective-permute-start.4 = (bf16[1,2,64,320]{3,2,1,0:T(8,128)(2,1)}, bf16[1,2,64,320]{3,2,1,0:T(8,128)(2,1)}, u32[]{:S(2)}, u32[]{:S(2)}) collective-permute-start(bf16[1,2,64,320]{3,2,1,0:T(8,128)(2,1)} %get-tuple-element.29), channel_id=1, source_target_pairs={{8,0},{16,8},{24,16},{32,24},{40,32},{48,40},{56,48},{64,56},{72,6... | collective-permute-start | bytes 245768 | tf_op jit(solution)/shard_map/ppermute | solution.py:22
  243.2 89.0 %collective-permute-start.5 = (bf16[1,2,64,320]{3,2,1,0:T(8,128)(2,1)}, bf16[1,2,64,320]{3,2,1,0:T(8,128)(2,1)}, u32[]{:S(2)}, u32[]{:S(2)}) collective-permute-start(bf16[1,2,64,320]{3,2,1,0:T(8,128)(2,1)} %get-tuple-element.30), channel_id=1, source_target_pairs={{0,8},{8,16},{16,24},{24,32},{32,40},{40,48},{48,56},{56,64},{64,7... | collective-permute-start | bytes 245768 | tf_op jit(solution)/shard_map/ppermute | solution.py:20
  334.7 9.8 %copy-start.5 = (bf16[640,1280]{1,0:T(8,128)(2,1)S(1)}, bf16[640,1280]{1,0:T(8,128)(2,1)}, u32[]{:S(2)}) copy-start(bf16[640,1280]{1,0:T(8,128)(2,1)} %param.19) | copy-start | bytes 4915204
  339.0 14.0 %copy-start.6 = (bf16[512,320]{1,0:T(8,128)(2,1)S(1)}, bf16[512,320]{1,0:T(8,128)(2,1)}, u32[]{:S(2)}) copy-start(bf16[512,320]{1,0:T(8,128)(2,1)} %copy.224) | copy-start | bytes 983044
  340.1 6.6 %collective-permute-start.6 = (bf16[4,1,64,320]{3,2,1,0:T(8,128)(2,1)S(1)}, bf16[4,1,64,320]{3,2,1,0:T(8,128)(2,1)S(1)}, u32[]{:S(2)}, u32[]{:S(2)}) collective-permute-start(bf16[4,1,64,320]{3,2,1,0:T(8,128)(2,1)S(1)} %get-tuple-element.25), channel_id=1, source_target_pairs={{0,1},{1,2},{2,3},{3,4},{4,5},{5,6},{6,7},{8,9},{9,10},{10,11},{11... | collective-permute-start | bytes 491528 | tf_op jit(solution)/shard_map/ppermute | solution.py:20
  343.1 9.9 %collective-permute-start.7 = (bf16[4,1,64,320]{3,2,1,0:T(8,128)(2,1)S(1)}, bf16[4,1,64,320]{3,2,1,0:T(8,128)(2,1)S(1)}, u32[]{:S(2)}, u32[]{:S(2)}) collective-permute-start(bf16[4,1,64,320]{3,2,1,0:T(8,128)(2,1)S(1)} %get-tuple-element.26), channel_id=1, source_target_pairs={{1,0},{2,1},{3,2},{4,3},{5,4},{6,5},{7,6},{9,8},{10,9},{11,10},{12... | collective-permute-start | bytes 491528 | tf_op jit(solution)/shard_map/ppermute | solution.py:22
  (13 other events, 34.0 us)
where the time goes:
time: 362 us; the launch traced here: 360 us
  blocking collectives  103 us (28%)
  starting transfers between devices  88.5 us (24%)
  local copies, waits for them, and re-layouts  61.3 us (17%)
  waiting for transfers between devices  49.2 us (14%)
  matrix products  38 us (10%)
  other arithmetic  18.4 us (5%)
    psum x1, blocking collectives, local(): lax.psum(jnp.sum(grad_gated * normed, axis=(0, 1, 2)), ('frame', 'space'))  76.7 us
    psum x2, blocking collectives, group_totals(): lax.psum((group_reduce(first_term), group_reduce(second_term)), 'space')  26.4 us
    dot_general x16, matrix products, dot_transposed(): lax.dot_general(matrix, weight, (((1,), (1,)), ((), ())), preferred_eleme...  18.7 us
    all_to_all x1, starting transfers between devices, local(): lax.all_to_all(queries, 'frame', split_axis=1, concat_axis=0, tiled=True)  15.6 us
    unnamed x60, local copies, waits for them, and re-layouts  13.7 us
    all_to_all x1, starting transfers between devices, local(): lax.all_to_all(grad_heads, 'frame', split_axis=1, concat_axis=0, tiled=True)  12.6 us
    ppermute x4, starting transfers between devices, with_halo(): lax.ppermute(tail, axis, [(i, (i + 1) % count) for i in range(ends)])  11.3 us
    ppermute x4, starting transfers between devices, with_halo(): lax.ppermute(head, axis, [((i + 1) % count, i) for i in range(ends)])  11.2 us
  transfers between devices with their start and end apart: 16, of which 10 were waited for; matrix products, arithmetic and copies ran while one was open for 19% of the time, Pallas kernels for 0%

commit v1 on v0

v1 whole, which is shorter than its diff:
```python
import math

import jax
import jax.numpy as jnp
from jax import lax
from jax.experimental import pallas as pl
from jax.experimental.pallas import tpu as pltpu
from jax.sharding import PartitionSpec as P

GROUPS = 32
LANES = 128
SLOT = 384
PAYLOAD = 16
bf16 = jnp.bfloat16
f32 = jnp.float32


def dot(a, b):
    return jnp.dot(a, b, preferred_element_type=f32)


def dot_nt(a, b):
    return lax.dot_general(a, b, (((1,), (1,)), ((), ())), preferred_element_type=f32)


def dot_tn(a, b):
    return lax.dot_general(a, b, (((0,), (0,)), ((), ())), preferred_element_type=f32)


def dot_exact(a, b):
    return jnp.dot(a, b, preferred_element_type=f32, precision=lax.Precision.HIGHEST)


def call(kernel, out_shape, *operands, scratch=()):
    return pl.pallas_call(
        kernel,
        out_shape=out_shape,
        in_specs=[pl.BlockSpec(memory_space=pltpu.VMEM)] * len(operands),
        out_specs=jax.tree.map(lambda _: pl.BlockSpec(memory_space=pltpu.VMEM), out_shape),
        scratch_shapes=list(scratch),
        compiler_params=pltpu.CompilerParams(vmem_limit_bytes=50 * 1024 * 1024),
    )(*operands)


def shape(dims, dtype):
    return jax.ShapeDtypeStruct(dims, dtype)


def taps(cells):
    wide = cells.astype(f32)
    columns = cells.shape[1]
    col = lax.broadcasted_iota(jnp.int32, cells.shape, 1)
    left = jnp.where(col == 0, 0.0, pltpu.roll(wide, 1, 1)).astype(bf16)
    right = jnp.where(col == columns - 1, 0.0, pltpu.roll(wide, columns - 1, 1)).astype(bf16)
    merged = jnp.concatenate([left, cells, right], axis=2)
    return merged.reshape(-1, merged.shape[2])


def space_own(cells, weight, part):
    first = taps(cells[:, 0])
    second = taps(cells[:, 1])
    part[0] = dot(first, weight[1]) + dot(second, weight[2])
    part[1] = dot(second, weight[1]) + dot(first, weight[0])


def space_edges(part, above, below, weight):
    at = lax.axis_index("space")
    count = lax.axis_size("space")
    upper = jnp.where(at > 0, above[:, 0], jnp.zeros_like(above[:, 0]))
    lower = jnp.where(at < count - 1, below[:, 0], jnp.zeros_like(below[:, 0]))
    return part[0] + dot(taps(upper), weight[0]), part[1] + dot(taps(lower), weight[2])


def spatial_finish(part, above, below, weight, spatial, first, last):
    rows = space_edges(part, above, below, weight)
    for at, row in enumerate(rows):
        row = row.astype(bf16).reshape(spatial.shape[0], *spatial.shape[2:])
        spatial[:, at] = row
        first[0, at] = row[0]
        last[0, at] = row[-1]


def time_own(cells, weight, part):
    frames, _, _, channels = cells.shape
    flat = cells[...].reshape(-1, channels)
    step = flat.shape[0] // frames
    part[...] = dot(flat, weight[1])
    part[step:] += dot(flat[:-step], weight[0])
    part[:-step] += dot(flat[step:], weight[2])


def time_edges(part, before, after, weight):
    at = lax.axis_index("frame")
    count = lax.axis_size("frame")
    channels = before.shape[-1]
    earlier = jnp.where(at > 0, before[...], jnp.zeros_like(before[...])).reshape(-1, channels)
    later = jnp.where(at < count - 1, after[...], jnp.zeros_like(after[...])).reshape(-1, channels)
    step = earlier.shape[0]
    head = part[:step] + dot(earlier, weight[0])
    tail = part[-step:] + dot(later, weight[2])
    return jnp.concatenate([head, part[step:-step], tail], axis=0)


def members(channels):
    channel = lax.broadcasted_iota(jnp.int32, (channels, LANES), 0)
    group = lax.broadcasted_iota(jnp.int32, (channels, LANES), 1)
    width = channels // GROUPS
    return jnp.where((channel >= group * width) & (channel < (group + 1) * width), 1.0, 0.0)


def spread(statistic, channels):
    return lax.dot_general(
        statistic,
        members(channels),
        (((1,), (1,)), ((), ())),
        preferred_element_type=f32,
        precision=lax.Precision.HIGHEST,
    )


def temporal_finish(part, before, after, weight, temporal, stats, *, frames):
    cells = time_edges(part, before, after, weight)
    temporal[...] = cells
    step = cells.shape[0] // frames
    split = cells.reshape(frames, step, cells.shape[1])
    sums = jnp.concatenate([jnp.sum(split, axis=1), jnp.sum(split * split, axis=1)], axis=0)
    stats[...] = jnp.broadcast_to(dot_exact(sums, members(cells.shape[1]))[None], stats.shape)


def moments(stats, frames, cell_count, channels):
    total = jnp.sum(stats[...], axis=0)
    mean = total[:frames] / cell_count
    inv = lax.rsqrt(total[frames:] / cell_count - mean * mean + 1e-05)
    return spread(mean, channels), spread(inv, channels)


def pairs(half, value):
    row = lax.broadcasted_iota(jnp.int32, (half, 2 * half), 0)
    col = lax.broadcasted_iota(jnp.int32, (half, 2 * half), 1)
    return jnp.where((col == 2 * row) | (col == 2 * row + 1), value, 0.0)


def pack(parts, wide, chunks, payload):
    wide[...] = jnp.zeros_like(wide)
    chunks[...] = jnp.zeros_like(chunks)
    for at, part in parts:
        wide[:, at : at + part.shape[1]] = part.astype(f32)
    pixels = wide.shape[0]
    for k in range(wide.shape[1] // LANES):
        chunks[pl.ds(k, pixels, stride=PAYLOAD), :] = wide[:, k * LANES : (k + 1) * LANES]
    payload[...] = chunks[...].reshape(payload.shape).astype(bf16)


def unpack(payload, wide, chunks):
    chunks[...] = payload[...].astype(f32).reshape(chunks.shape)
    pixels = wide.shape[0]
    for k in range(wide.shape[1] // LANES):
        wide[:, k * LANES : (k + 1) * LANES] = chunks[pl.ds(k, pixels, stride=PAYLOAD), :]


def activation(normed, gain):
    gated = normed * gain
    sig = jax.nn.sigmoid(gated)
    return gated * sig, sig * (1.0 + gated * (1.0 - sig))


def pool_out(
    temporal, stats, cells, gain, grad_heads, cot_in, payload, pooled, wide, chunks, *, cell_count
):
    frames, rows, columns, channels = cells.shape
    mean, inv = moments(stats, frames, cell_count, channels)
    half = columns // 2
    fine = jnp.zeros((columns, channels), f32)
    sway = jnp.zeros((columns, channels), f32)
    for f in range(frames):
        for r in range(rows):
            at = (f * rows + r) * columns
            normed = (temporal[at : at + columns] - mean[f : f + 1]) * inv[f : f + 1]
            silu, slope = activation(normed, gain[...])
            fine += cells[f, r].astype(f32) + silu
            sway += slope * normed
    select = pairs(half, 1.0 / 16.0)
    low = dot_exact(select, fine).astype(bf16)
    pooled[...] = low
    pack(
        [
            (0, low),
            (SLOT, dot_exact(select, sway)),
            (2 * SLOT, cot_in[...]),
            (3 * SLOT, grad_heads[...]),
        ],
        wide,
        chunks,
        payload,
    )


def slopes(temporal, stats, gain, normed_out, slope_out, first, second, inv_out, *, dims, cell_count):
    frames, rows, columns = dims
    channels = temporal.shape[1]
    mean, inv = moments(stats, frames, cell_count, channels)
    inv_out[...] = inv
    select = pairs(columns // 2, 1.0)
    for f in range(frames):
        lead = jnp.zeros((columns, channels), f32)
        sway = jnp.zeros((columns, channels), f32)
        for r in range(rows):
            at = (f * rows + r) * columns
            normed = (temporal[at : at + columns] - mean[f : f + 1]) * inv[f : f + 1]
            slope = activation(normed, gain[...])[1] * gain[...] * (1.0 / 16.0)
            normed_out[at : at + columns] = normed
            slope_out[at : at + columns] = slope
            lead += slope
            sway += slope * normed
        first[f] = dot_exact(select, lead)
        second[f] = dot_exact(select, sway)


def coarse(payload, merged, bias, out, wide, chunks, *, heads, channels):
    unpack(payload, wide, chunks)
    frames = payload.shape[0]
    pooled = wide[:, :channels].astype(bf16)
    sway = wide[:, SLOT : SLOT + channels]
    cot_in = wide[:, 2 * SLOT : 2 * SLOT + channels]
    width = merged.shape[1] // 3
    grad_heads = wide[:, 3 * SLOT : 3 * SLOT + width].astype(bf16)
    depth = width // heads
    factor = 1.0 / math.sqrt(depth)
    qkv = dot(pooled, merged[...]).astype(bf16)
    queries, keys, values = (qkv[:, i * width : (i + 1) * width] for i in range(3))
    row = lax.broadcasted_iota(jnp.int32, (heads, frames, width), 0)
    lane = lax.broadcasted_iota(jnp.int32, (heads, frames, width), 2)
    own = (lane >= row * depth) & (lane < (row + 1) * depth)

    def by_head(matrix):
        tiled = jnp.broadcast_to(matrix.astype(f32)[None], (heads, frames, width))
        return jnp.where(own, tiled, 0.0).astype(bf16).reshape(heads * frames, width)

    def gather(product):
        return jnp.sum(jnp.where(own, product.reshape(heads, frames, width), 0.0), axis=0)

    query_rows = by_head(queries)
    grad_rows = by_head(grad_heads)
    scores = dot_nt(query_rows, keys) * factor + bias[...]
    expd = jnp.exp(scores - jnp.max(scores, axis=1, keepdims=True))
    weights = expd / jnp.sum(expd, axis=1, keepdims=True)
    rounded = weights.astype(bf16)
    blended = gather(dot(rounded, values))
    grad_weights = dot_nt(grad_rows, values)
    grad_values = dot_tn(rounded, grad_rows)
    centre = jnp.sum(weights * grad_weights, axis=1, keepdims=True)
    grad_scores = (weights * (grad_weights - centre)).astype(bf16)
    grad_queries = gather(dot(grad_scores, keys)) * factor
    grad_keys = dot_tn(grad_scores, query_rows) * factor
    grads = jnp.concatenate([grad_queries, grad_keys, grad_values], axis=1).astype(bf16)
    grad_pooled = (cot_in + dot_nt(grads, merged[...])).astype(bf16)
    gain = jnp.sum(grad_pooled.astype(f32) * sway, axis=0, keepdims=True)
    high = gain.astype(bf16).astype(f32)
    pack(
        [
            (0, grad_pooled),
            (SLOT, jnp.broadcast_to(high, (frames, channels))),
            (2 * SLOT, jnp.broadcast_to(gain - high, (frames, channels))),
            (3 * SLOT, blended),
        ],
        wide,
        chunks,
        out,
    )


def totals(payload, first, second, stats, grad_pooled, blended, wide, chunks):
    unpack(payload, wide, chunks)
    frames, _, channels = first.shape
    low = wide[:, :channels]
    grad_pooled[...] = low.astype(bf16)
    blended[...] = wide[:, 3 * SLOT : 3 * SLOT + blended.shape[1]].astype(bf16)
    gain = jnp.sum(wide[:, SLOT : 2 * SLOT] + wide[:, 2 * SLOT : 3 * SLOT], axis=0, keepdims=True)
    sums = jnp.concatenate(
        [jnp.sum(first[...] * low[None], axis=1), jnp.sum(second[...] * low[None], axis=1)], axis=0
    )
    block = jnp.concatenate(
        [
            dot_exact(sums, members(channels)),
            *[gain[:, k * LANES : (k + 1) * LANES] for k in range(SLOT // LANES)],
            jnp.zeros((stats.shape[1] - 2 * frames - SLOT // LANES, LANES), f32),
        ],
        axis=0,
    )
    stats[...] = jnp.broadcast_to(block[None], stats.shape)


def unpooled(grad_pooled):
    half = grad_pooled.shape[0]
    row = lax.broadcasted_iota(jnp.int32, (2 * half, half), 0)
    col = lax.broadcasted_iota(jnp.int32, (2 * half, half), 1)
    grow = jnp.where((row == 2 * col) | (row == 2 * col + 1), 1.0, 0.0).astype(bf16)
    return dot(grow, grad_pooled[...])


def norm_back(
    stats, grad_pooled, normed, slope, inv, grad, first, last, gain, *, cell_count
):
    frames, rows, columns, channels = grad.shape
    total = jnp.sum(stats[...], axis=0)
    for k in range(gain.shape[1] // LANES):
        gain[:, k * LANES : (k + 1) * LANES] = total[2 * frames + k : 2 * frames + k + 1]
    means = spread(total[: 2 * frames] / cell_count, channels)
    grown = unpooled(grad_pooled)
    for f in range(frames):
        for r in range(rows):
            at = (f * rows + r) * columns
            here = slice(at, at + columns)
            value = inv[f : f + 1] * (
                grown * slope[here]
                - means[f : f + 1]
                - normed[here] * means[frames + f : frames + f + 1]
            )
            value = value.astype(bf16)
            grad[f, r] = value
            if f == 0:
                first[0, r] = value
            if f == frames - 1:
                last[0, r] = value


def time_back_finish(part, before, after, weight, grad, top, bottom):
    cells = time_edges(part, before, after, weight).astype(bf16).reshape(grad.shape)
    grad[...] = cells
    top[...] = cells[:, :1]
    bottom[...] = cells[:, -1:]


def space_back_finish(part, above, below, weight, grad_pooled, out):
    grown = unpooled(grad_pooled) * (1.0 / 16.0)
    for at, row in enumerate(space_edges(part, above, below, weight)):
        row = row.reshape(out.shape[0], *out.shape[2:]) + grown[None]
        out[:, at] = row.astype(bf16)


def prepare(cot, proj_in, proj_query, proj_key, proj_value, proj_out, merged, grad_heads, cot_in):
    width = proj_query.shape[1]
    for at, weight in enumerate((proj_query, proj_key, proj_value)):
        merged[:, at * width : (at + 1) * width] = dot(proj_in[...], weight[...]).astype(bf16)
    grad_heads[...] = dot_nt(cot[...], proj_out[...]).astype(bf16)
    cot_in[...] = dot_nt(cot[...], proj_in[...])


def coarse_finish(pooled, proj_in, blended, proj_out, out):
    low = dot(pooled[...], proj_in[...]).astype(bf16).astype(f32)
    out[...] = (low + dot(blended[...], proj_out[...])).astype(bf16)


def neighbours(tail, head, axis):
    count = lax.axis_size(axis)
    return (
        lax.ppermute(tail, axis, [(i, (i + 1) % count) for i in range(count)]),
        lax.ppermute(head, axis, [((i + 1) % count, i) for i in range(count)]),
    )


def exchange(payload, axis):
    return lax.all_to_all(payload, axis, split_axis=0, concat_axis=0, tiled=True)


def local(
    frames_in,
    kernel_space,
    kernel_time,
    norm_gain,
    proj_in,
    proj_query,
    proj_key,
    proj_value,
    proj_out,
    frame_bias,
    cotangent,
):
    frames, rows, columns, channels = frames_in.shape
    bands = lax.axis_size("space")
    cell_count = rows * bands * columns * (channels // GROUPS)
    cells = frames * rows * columns
    half = columns // 2
    heads = frame_bias.shape[0]
    width = proj_query.shape[1]
    depth = cotangent.shape[-1]
    flat = shape((cells, channels), f32)
    edge = shape((1, rows, columns, channels), bf16)
    band = shape(frames_in.shape, bf16)
    gain = norm_gain.reshape(1, channels)
    packing = (
        pltpu.VMEM((half, 3 * SLOT + width), f32),
        pltpu.VMEM((half * PAYLOAD, LANES), f32),
    )
    payload = shape((half, PAYLOAD, LANES), bf16)
    partial = shape((rows, frames * columns, channels), f32)

    weight_space = kernel_space.reshape(3, 3 * channels, channels)
    back_space = jnp.flip(kernel_space, (0, 1)).swapaxes(2, 3).reshape(3, 3 * channels, channels)
    back_time = jnp.flip(kernel_time, 0).swapaxes(1, 2)

    above, below = neighbours(frames_in[:, -1:], frames_in[:, :1], "space")
    part = call(space_own, partial, frames_in, weight_space)
    cot = cotangent.reshape(half, depth)
    merged, grad_heads, cot_in = call(
        prepare,
        (
            shape((channels, 3 * width), bf16),
            shape((half, width), bf16),
            shape((half, channels), f32),
        ),
        cot,
        proj_in,
        proj_query,
        proj_key,
        proj_value,
        proj_out,
    )
    spatial, first, last = call(
        spatial_finish, (band, edge, edge), part, above, below, weight_space
    )
    before, after = neighbours(last, first, "frame")
    part = call(time_own, flat, spatial, kernel_time)
    temporal, stats = call(
        lambda *refs: temporal_finish(*refs, frames=frames),
        (flat, shape((bands, 2 * frames, LANES), f32)),
        part,
        before,
        after,
        kernel_time,
    )
    stats = exchange(stats, "space")
    sent, pooled = call(
        lambda *refs: pool_out(*refs, cell_count=cell_count),
        (payload, shape((half, channels), bf16)),
        temporal,
        stats,
        frames_in,
        gain,
        grad_heads,
        cot_in,
        scratch=packing,
    )
    received = exchange(sent, "frame")
    normed, slope, slope_sum, sway_sum, inv = call(
        lambda *refs: slopes(*refs, dims=(frames, rows, columns), cell_count=cell_count),
        (
            flat,
            flat,
            shape((frames, half, channels), f32),
            shape((frames, half, channels), f32),
            shape((frames, channels), f32),
        ),
        temporal,
        stats,
        gain,
    )
    sent = call(
        lambda *refs: coarse(*refs, heads=heads, channels=channels),
        payload,
        received,
        merged,
        frame_bias.reshape(-1, frame_bias.shape[-1]),
        scratch=packing,
    )
    received = exchange(sent, "frame")
    stats, grad_pooled, blended = call(
        totals,
        (
            shape((bands, 16, LANES), f32),
            shape((half, channels), bf16),
            shape((half, width), bf16),
        ),
        received,
        slope_sum,
        sway_sum,
        scratch=packing,
    )
    stats = exchange(stats, "space")
    coarse_out = call(
        coarse_finish, shape((half, depth), bf16), pooled, proj_in, blended, proj_out
    )
    grad_temporal, first, last, grad_gain = call(
        lambda *refs: norm_back(*refs, cell_count=cell_count),
        (band, edge, edge, shape((1, SLOT), f32)),
        stats,
        grad_pooled,
        normed,
        slope,
        inv,
    )
    before, after = neighbours(last, first, "frame")
    part = call(time_own, flat, grad_temporal, back_time)
    row_edge = shape((frames, 1, columns, channels), bf16)
    grad_spatial, top, bottom = call(
        time_back_finish, (band, row_edge, row_edge), part, before, after, back_time
    )
    above, below = neighbours(bottom, top, "space")
    part = call(space_own, partial, grad_spatial, back_space)
    grad_frames = call(
        space_back_finish, band, part, above, below, back_space, grad_pooled
    )
    return coarse_out.reshape(cotangent.shape), grad_frames, grad_gain[0, :channels]


def solution(mesh):
    in_specs = (
        P("frame", "space", None, None),
        P(),
        P(),
        P(),
        P(),
        P(),
        P(),
        P(),
        P(),
        P(),
        P("frame", "space", None, None),
    )
    out_specs = (P("frame", "space", None, None), P("frame", "space", None, None), P())
    return jax.shard_map(local, mesh=mesh, in_specs=in_specs, out_specs=out_specs, check_vma=False)
```

time: 362 us -> 123 us (0.34)
  the two profiles are of different devices: /device:TPU:1 before, /device:TPU:0 now
where the time goes in v1:
time: 123 us; the launch traced here: 122 us
  starting transfers between devices  34.1 us (28%)
  local copies, waits for them, and re-layouts  29 us (24%)
  Pallas kernels  22.1 us (18%)
  blocking collectives  19.7 us (16%)
  waiting for transfers between devices  16 us (13%)
    pallas_call x15, Pallas kernels, call(): pl.pallas_call(kernel, out_shape=out_shape, in_specs=[pl.BlockSpec(memory...  22.1 us
    unnamed x59, local copies, waits for them, and re-layouts  21.5 us
    ppermute x4, starting transfers between devices, neighbours(): lax.ppermute(head, axis, [((i + 1) % count, i) for i in range(count)])  19.8 us
    all_to_all x1, blocking collectives, exchange(): lax.all_to_all(payload, axis, split_axis=0, concat_axis=0, tiled=True)  19.7 us
    all_to_all x3, starting transfers between devices, exchange(): lax.all_to_all(payload, axis, split_axis=0, concat_axis=0, tiled=True)  13.3 us
    all_to_all x3, waiting for transfers between devices, exchange(): lax.all_to_all(payload, axis, split_axis=0, concat_axis=0, tiled=True)  12.1 us
    transpose x2, local copies, waits for them, and re-layouts, local(): jnp.flip(kernel_space, (0, 1)).swapaxes(2, 3)  4.7 us
    ppermute x4, waiting for transfers between devices, neighbours(): lax.ppermute(tail, axis, [(i, (i + 1) % count) for i in range(count)])  2.95 us
  transfers between devices with their start and end apart: 11, of which 6 were waited for; matrix products, arithmetic and copies ran while one was open for 6% of the time, Pallas kernels for 9%

profile of v1, /device:TPU:0, one launch (start us, length us, event | category | flops | bytes accessed | tf_op | source)
XLA Modules:
  0.0 121.9 jit_solution(10956670356411773013)
XLA Ops:
  1.8 4.1 %collective-permute-start.1 = (bf16[4,1,64,320]{3,2,1,0:T(8,128)(2,1)S(1)}, bf16[4,1,64,320]{3,2,1,0:T(8,128)(2,1)S(1)}, u32[]{:S(2)}, u32[]{:S(2)}) collective-permute-start(bf16[4,1,64,320]{3,2,1,0:T(8,128)(2,1)S(1)} %get-tuple-element.53), channel_id=1, source_target_pairs={{1,0},{2,1},{3,2},{4,3},{5,4},{6,5},{7,6},{0,7},{9,8},{10,9},{11,1... | collective-permute-start | bytes 491528 | tf_op jit(solution)/shard_map/ppermute | solution.py:358
  5.9 1.6 %copy-done = bf16[3,3,320,320]{3,2,1,0:T(8,128)(2,1)S(1)} copy-done((bf16[3,3,320,320]{3,2,1,0:T(8,128)(2,1)S(1)}, bf16[3,3,320,320]{3,2,1,0:T(8,128)(2,1)}, u32[]{:S(2)}) %copy-start) | copy-done | bytes 1843224
  8.5 1.2 %shard_map.130.part = f32[2,256,320]{2,1,0:T(8,128)S(1)} custom-call(bf16[4,2,64,320]{3,2,1,0:T(8,128)(2,1)S(1)} %copy-done.4, bf16[3,960,320]{2,1,0:T(8,128)(2,1)S(1)} %bitcast.9), custom_call_target="tpu_custom_call" | custom-call | tf_op jit(solution)/shard_map/pallas_call | solution.py:35
  9.8 1.2 collective-permute-done.above
  12.7 7.0 %collective-permute-start.3 = (bf16[1,2,64,320]{3,2,1,0:T(8,128)(2,1)S(1)}, bf16[1,2,64,320]{3,2,1,0:T(8,128)(2,1)S(1)}, u32[]{:S(2)}, u32[]{:S(2)}) collective-permute-start(bf16[1,2,64,320]{3,2,1,0:T(8,128)(2,1)S(1)} %get-tuple-element.30), channel_id=1, source_target_pairs={{8,0},{16,8},{24,16},{32,24},{40,32},{48,40},{56,48},{64,56},{72,6... | collective-permute-start | bytes 245768 | tf_op jit(solution)/shard_map/ppermute | solution.py:358
  20.5 1.4 %collective-permute-done.2.refs_1_ = bf16[1,2,64,320]{3,2,1,0:T(8,128)(2,1)S(1)} collective-permute-done((bf16[1,2,64,320]{3,2,1,0:T(8,128)(2,1)S(1)}, bf16[1,2,64,320]{3,2,1,0:T(8,128)(2,1)S(1)}, u32[]{:S(2)}, u32[]{:S(2)}) %collective-permute-start.2) | collective-permute-done | bytes 81952 | tf_op jit(solution)/shard_map/ppermute | solution.py:357
  24.0 4.2 %all-to-all-start = ((f32[8,8,128]{2,1,0:T(8,128)}), f32[8,8,128]{2,1,0:T(8,128)S(1)}, u32[]{:S(2)}, u32[]{:S(2)}) async-start(f32[8,8,128]{2,1,0:T(8,128)} %get-tuple-element.32), calls=%async_computation | async-start | bytes 65536 | tf_op jit(solution)/shard_map/all_to_all | solution.py:363
  29.3 1.4 %copy-done.11 = bf16[1280,640]{1,0:T(8,128)(2,1)S(1)} copy-done((bf16[1280,640]{1,0:T(8,128)(2,1)S(1)}, bf16[1280,640]{1,0:T(8,128)(2,1)}, u32[]{:S(2)}) %copy-start.11) | copy-done | bytes 1638424
  31.7 5.1 %shard_map.134 = (bf16[320,1920]{1,0:T(8,128)(2,1)S(1)}, bf16[32,640]{1,0:T(8,128)(2,1)S(1)}, f32[32,320]{1,0:T(8,128)S(1)}) custom-call(bf16[32,1280]{1,0:T(8,128)(2,1)S(1)} %bitcast.14, bf16[320,1280]{1,0:T(8,128)(2,1)S(1)} %copy-done.6, bf16[1280,640]{1,0:T(8,128)(2,1)S(1)} %copy-done.11, bf16[1280,640]{1,0:T(8,128)(2,1)} %proj_key.1, ...), custom_call_target="tpu_custom_call" | custom-call | tf_op jit(solution)/shard_map/pallas_call | solution.py:35
  43.0 19.7 %all_to_all.20.refs_0_ = bf16[32,16,128]{2,1,0:T(8,128)(2,1)S(1)} all-to-all(bf16[32,16,128]{2,1,0:T(8,128)(2,1)S(1)} %get-tuple-element.36), channel_id=1, replica_groups=mesh['frame'=32,'space'=8] {'frame'}, dimensions={0} | all-to-all | bytes 262144 | tf_op jit(solution)/shard_map/all_to_all | solution.py:363
  62.8 2.7 %shard_map.136 = bf16[32,16,128]{2,1,0:T(8,128)(2,1)} custom-call(bf16[32,16,128]{2,1,0:T(8,128)(2,1)S(1)} %all_to_all.20.refs_0_, bf16[320,1920]{1,0:T(8,128)(2,1)S(1)} %copy-done.13, f32[320,32]{1,0:T(8,128)S(1)} %bitcast.13), custom_call_target="tpu_custom_call" | custom-call | tf_op jit(solution)/shard_map/pallas_call | solution.py:35
  65.4 4.0 %all-to-all-start.2 = ((bf16[32,16,128]{2,1,0:T(8,128)(2,1)}), bf16[32,16,128]{2,1,0:T(8,128)(2,1)S(1)}, u32[]{:S(2)}, u32[]{:S(2)}) async-start(bf16[32,16,128]{2,1,0:T(8,128)(2,1)} %shard_map.136), calls=%async_computation.2 | async-start | bytes 262144 | tf_op jit(solution)/shard_map/all_to_all | solution.py:363
  70.6 1.2 %shard_map.137 = (f32[512,320]{1,0:T(8,128)S(1)}, f32[512,320]{1,0:T(8,128)S(1)}, f32[4,32,320]{2,1,0:T(8,128)S(1)}, f32[4,32,320]{2,1,0:T(8,128)S(1)}, f32[4,320]{1,0:T(4,128)S(1)}) custom-call(f32[512,320]{1,0:T(8,128)S(1)} %copy-done.10, f32[8,8,128]{2,1,0:T(8,128)S(1)} %all-to-all-done.refs_1_, f32[1,320]{1,0:T(1,128)S(1)} %reshape.25.refs_3_.refs_2_), custom_call_target="tpu_custom_call" | custom-call | tf_op jit(solution)/shard_map/pallas_call | solution.py:35
  74.3 6.9 %all-to-all-done.2.payload = bf16[32,16,128]{2,1,0:T(8,128)(2,1)S(1)} async-done(((bf16[32,16,128]{2,1,0:T(8,128)(2,1)}), bf16[32,16,128]{2,1,0:T(8,128)(2,1)S(1)}, u32[]{:S(2)}, u32[]{:S(2)}) %all-to-all-start.2) | async-done | bytes 131104 | tf_op jit(solution)/shard_map/all_to_all | solution.py:363
  83.1 5.1 %all-to-all-start.3 = ((f32[8,16,128]{2,1,0:T(8,128)}), f32[8,16,128]{2,1,0:T(8,128)S(1)}, u32[]{:S(2)}, u32[]{:S(2)}) async-start(f32[8,16,128]{2,1,0:T(8,128)} %get-tuple-element.41), calls=%async_computation.3 | async-start | bytes 131072 | tf_op jit(solution)/shard_map/all_to_all | solution.py:363
  89.4 5.2 %all-to-all-done.3.refs_0_ = f32[8,16,128]{2,1,0:T(8,128)S(1)} async-done(((f32[8,16,128]{2,1,0:T(8,128)}), f32[8,16,128]{2,1,0:T(8,128)S(1)}, u32[]{:S(2)}, u32[]{:S(2)}) %all-to-all-start.3) | async-done | bytes 65568 | tf_op jit(solution)/shard_map/all_to_all | solution.py:363
  97.4 5.3 %collective-permute-start.5 = (bf16[1,2,64,320]{3,2,1,0:T(8,128)(2,1)S(1)}, bf16[1,2,64,320]{3,2,1,0:T(8,128)(2,1)S(1)}, u32[]{:S(2)}, u32[]{:S(2)}) collective-permute-start(bf16[1,2,64,320]{3,2,1,0:T(8,128)(2,1)S(1)} %get-tuple-element.48), channel_id=1, source_target_pairs={{8,0},{16,8},{24,16},{32,24},{40,32},{48,40},{56,48},{64,56},{72,6... | collective-permute-start | bytes 245768 | tf_op jit(solution)/shard_map/ppermute | solution.py:358
  102.7 1.2 reverse_bitcast_fusion.1.weight
  106.8 3.4 %collective-permute-start.7 = (bf16[4,1,64,320]{3,2,1,0:T(8,128)(2,1)}, bf16[4,1,64,320]{3,2,1,0:T(8,128)(2,1)}, u32[]{:S(2)}, u32[]{:S(2)}) collective-permute-start(bf16[4,1,64,320]{3,2,1,0:T(8,128)(2,1)} %get-tuple-element.51), channel_id=1, source_target_pairs={{1,0},{2,1},{3,2},{4,3},{5,4},{6,5},{7,6},{0,7},{9,8},{10,9},{11,1... | collective-permute-start | bytes 491528 | tf_op jit(solution)/shard_map/ppermute | solution.py:358
  110.2 1.6 %reverse_bitcast_fusion = bf16[3,3,320,320]{2,3,1,0:T(8,128)(2,1)} fusion(bf16[3,3,320,320]{3,2,1,0:T(8,128)(2,1)S(1)} %copy-done.1), kind=kLoop, calls=%fused_computation | loop fusion | bytes 3686400 | tf_op jit(solution)/shard_map/transpose | solution.py:399
  111.8 3.1 %copy.15 = bf16[3,3,320,320]{3,2,1,0:T(8,128)(2,1)S(1)} copy(bf16[3,3,320,320]{2,3,1,0:T(8,128)(2,1)} %reverse_bitcast_fusion) | data formatting | bytes 3686400 | tf_op jit(solution)/shard_map/transpose | solution.py:399
  114.9 1.4 %copy-done.3 = bf16[640,1280]{1,0:T(8,128)(2,1)S(1)} copy-done((bf16[640,1280]{1,0:T(8,128)(2,1)S(1)}, bf16[640,1280]{1,0:T(8,128)(2,1)}, u32[]{:S(2)}) %copy-start.3) | copy-done | bytes 1638424
  118.1 1.2 %shard_map.143.part = f32[2,256,320]{2,1,0:T(8,128)S(1)} custom-call(bf16[4,2,64,320]{3,2,1,0:T(8,128)(2,1)S(1)} %get-tuple-element.49.cells, bf16[3,960,320]{2,1,0:T(8,128)(2,1)S(1)} %bitcast.11), custom_call_target="tpu_custom_call" | custom-call | tf_op jit(solution)/shard_map/pallas_call | solution.py:35
  119.4 2.5 %shard_map.144 = bf16[4,2,64,320]{3,2,1,0:T(8,128)(2,1)} custom-call(f32[2,256,320]{2,1,0:T(8,128)S(1)} %shard_map.143.part, bf16[4,1,64,320]{3,2,1,0:T(8,128)(2,1)} %collective-permute-done.6.above, bf16[4,1,64,320]{3,2,1,0:T(8,128)(2,1)} %collective-permute-done.7.below, bf16[3,960,320]{2,1,0:T(8,128)(2,1)S(1)} %bitcast.12, ...), custom_call_target="tpu_custom_call" | custom-call | tf_op jit(solution)/shard_map/pallas_call | solution.py:35
  (79 shorter events, 29.0 us)
Async XLA Ops:
  1.7 9.3 %collective-permute-start = (bf16[4,1,64,320]{3,2,1,0:T(8,128)(2,1)S(1)}, bf16[4,1,64,320]{3,2,1,0:T(8,128)(2,1)S(1)}, u32[]{:S(2)}, u32[]{:S(2)}) collective-permute-start(bf16[4,1,64,320]{3,2,1,0:T(8,128)(2,1)S(1)} %get-tuple-element.54), channel_id=1, source_target_pairs={{0,1},{1,2},{2,3},{3,4},{4,5},{5,6},{6,7},{7,0},{8,9},{9,10},{10,1... | collective-permute-start | bytes 491528 | tf_op jit(solution)/shard_map/ppermute | solution.py:357
  1.8 10.1 %collective-permute-start.1 = (bf16[4,1,64,320]{3,2,1,0:T(8,128)(2,1)S(1)}, bf16[4,1,64,320]{3,2,1,0:T(8,128)(2,1)S(1)}, u32[]{:S(2)}, u32[]{:S(2)}) collective-permute-start(bf16[4,1,64,320]{3,2,1,0:T(8,128)(2,1)S(1)} %get-tuple-element.53), channel_id=1, source_target_pairs={{1,0},{2,1},{3,2},{4,3},{5,4},{6,5},{7,6},{0,7},{9,8},{10,9},{11,1... | collective-permute-start | bytes 491528 | tf_op jit(solution)/shard_map/ppermute | solution.py:358
  5.9 1.6 %copy-start = (bf16[3,3,320,320]{3,2,1,0:T(8,128)(2,1)S(1)}, bf16[3,3,320,320]{3,2,1,0:T(8,128)(2,1)}, u32[]{:S(2)}) copy-start(bf16[3,3,320,320]{3,2,1,0:T(8,128)(2,1)} %param.12) | copy-start | bytes 5529604
  8.5 3.4 %copy-start.1 = (bf16[3,3,320,320]{3,2,1,0:T(8,128)(2,1)S(1)}, bf16[3,3,320,320]{3,2,1,0:T(8,128)(2,1)}, u32[]{:S(2)}) copy-start(bf16[3,3,320,320]{3,2,1,0:T(8,128)(2,1)} %param.12) | copy-start | bytes 5529604
  9.8 9.9 %copy-start.2 = (bf16[3,320,320]{2,1,0:T(8,128)(2,1)S(1)}, bf16[3,320,320]{2,1,0:T(8,128)(2,1)}, u32[]{:S(2)}) copy-start(bf16[3,320,320]{2,1,0:T(8,128)(2,1)} %refs_3_.1) | copy-start | bytes 1843204
  12.6 15.5 %copy-start.28 = (f32[320]{0:T(512)S(1)}, f32[320]{0:T(512)}, u32[]{:S(2)}) copy-start(f32[320]{0:T(512)} %param.14) | copy-start | bytes 3844
  12.6 9.3 %collective-permute-start.2 = (bf16[1,2,64,320]{3,2,1,0:T(8,128)(2,1)S(1)}, bf16[1,2,64,320]{3,2,1,0:T(8,128)(2,1)S(1)}, u32[]{:S(2)}, u32[]{:S(2)}) collective-permute-start(bf16[1,2,64,320]{3,2,1,0:T(8,128)(2,1)S(1)} %get-tuple-element.29), channel_id=1, source_target_pairs={{0,8},{8,16},{16,24},{24,32},{32,40},{40,48},{48,56},{56,64},{64,7... | collective-permute-start | bytes 245768 | tf_op jit(solution)/shard_map/ppermute | solution.py:357
  12.7 9.2 %collective-permute-start.3 = (bf16[1,2,64,320]{3,2,1,0:T(8,128)(2,1)S(1)}, bf16[1,2,64,320]{3,2,1,0:T(8,128)(2,1)S(1)}, u32[]{:S(2)}, u32[]{:S(2)}) collective-permute-start(bf16[1,2,64,320]{3,2,1,0:T(8,128)(2,1)S(1)} %get-tuple-element.30), channel_id=1, source_target_pairs={{8,0},{16,8},{24,16},{32,24},{40,32},{48,40},{56,48},{64,56},{72,6... | collective-permute-start | bytes 245768 | tf_op jit(solution)/shard_map/ppermute | solution.py:358
  24.0 15.2 %all-to-all-start = ((f32[8,8,128]{2,1,0:T(8,128)}), f32[8,8,128]{2,1,0:T(8,128)S(1)}, u32[]{:S(2)}, u32[]{:S(2)}) async-start(f32[8,8,128]{2,1,0:T(8,128)} %get-tuple-element.32), calls=%async_computation | async-start | bytes 65536 | tf_op jit(solution)/shard_map/all_to_all | solution.py:363
  28.2 1.1 copy-start.6
  29.3 1.4 %copy-start.11 = (bf16[1280,640]{1,0:T(8,128)(2,1)S(1)}, bf16[1280,640]{1,0:T(8,128)(2,1)}, u32[]{:S(2)}) copy-start(bf16[1280,640]{1,0:T(8,128)(2,1)} %proj_query.1) | copy-start | bytes 4915204
  31.6 7.5 %copy-start.5 = (bf16[4,2,64,320]{3,2,1,0:T(8,128)(2,1)S(1)}, bf16[4,2,64,320]{3,2,1,0:T(8,128)(2,1)}, u32[]{:S(2)}) copy-start(bf16[4,2,64,320]{3,2,1,0:T(8,128)(2,1)} %refs_2_.1) | copy-start | bytes 983044
  31.7 31.1 %copy-start.20 = (f32[10,32,32]{2,1,0:T(8,128)S(1)}, f32[10,32,32]{2,1,0:T(8,128)}, u32[]{:S(2)}) copy-start(f32[10,32,32]{2,1,0:T(8,128)} %param.20) | copy-start | bytes 122884
  41.8 20.9 %copy-start.13 = (bf16[320,1920]{1,0:T(8,128)(2,1)S(1)}, bf16[320,1920]{1,0:T(8,128)(2,1)}, u32[]{:S(2)}) copy-start(bf16[320,1920]{1,0:T(8,128)(2,1)} %copy-done.12) | copy-start | bytes 3686404
  43.0 19.8 %copy-start.26 = (bf16[32,320]{1,0:T(8,128)(2,1)}, bf16[32,320]{1,0:T(8,128)(2,1)S(1)}, u32[]{:S(2)}) copy-start(bf16[32,320]{1,0:T(8,128)(2,1)S(1)} %get-tuple-element.35.pooled) | copy-start | bytes 61444
  65.4 15.8 %all-to-all-start.2 = ((bf16[32,16,128]{2,1,0:T(8,128)(2,1)}), bf16[32,16,128]{2,1,0:T(8,128)(2,1)S(1)}, u32[]{:S(2)}, u32[]{:S(2)}) async-start(bf16[32,16,128]{2,1,0:T(8,128)(2,1)} %shard_map.136), calls=%async_computation.2 | async-start | bytes 262144 | tf_op jit(solution)/shard_map/all_to_all | solution.py:363
  83.1 11.4 %all-to-all-start.3 = ((f32[8,16,128]{2,1,0:T(8,128)}), f32[8,16,128]{2,1,0:T(8,128)S(1)}, u32[]{:S(2)}, u32[]{:S(2)}) async-start(f32[8,16,128]{2,1,0:T(8,128)} %get-tuple-element.41), calls=%async_computation.3 | async-start | bytes 131072 | tf_op jit(solution)/shard_map/all_to_all | solution.py:363
  97.3 7.7 %collective-permute-start.4 = (bf16[1,2,64,320]{3,2,1,0:T(8,128)(2,1)S(1)}, bf16[1,2,64,320]{3,2,1,0:T(8,128)(2,1)S(1)}, u32[]{:S(2)}, u32[]{:S(2)}) collective-permute-start(bf16[1,2,64,320]{3,2,1,0:T(8,128)(2,1)S(1)} %get-tuple-element.47), channel_id=1, source_target_pairs={{0,8},{8,16},{16,24},{24,32},{32,40},{40,48},{48,56},{56,64},{64,7... | collective-permute-start | bytes 245768 | tf_op jit(solution)/shard_map/ppermute | solution.py:357
  97.4 7.6 %collective-permute-start.5 = (bf16[1,2,64,320]{3,2,1,0:T(8,128)(2,1)S(1)}, bf16[1,2,64,320]{3,2,1,0:T(8,128)(2,1)S(1)}, u32[]{:S(2)}, u32[]{:S(2)}) collective-permute-start(bf16[1,2,64,320]{3,2,1,0:T(8,128)(2,1)S(1)} %get-tuple-element.48), channel_id=1, source_target_pairs={{8,0},{16,8},{24,16},{32,24},{40,32},{48,40},{56,48},{64,56},{72,6... | collective-permute-start | bytes 245768 | tf_op jit(solution)/shard_map/ppermute | solution.py:358
  106.1 13.3 %collective-permute-start.6 = (bf16[4,1,64,320]{3,2,1,0:T(8,128)(2,1)}, bf16[4,1,64,320]{3,2,1,0:T(8,128)(2,1)}, u32[]{:S(2)}, u32[]{:S(2)}) collective-permute-start(bf16[4,1,64,320]{3,2,1,0:T(8,128)(2,1)} %get-tuple-element.50), channel_id=1, source_target_pairs={{0,1},{1,2},{2,3},{3,4},{4,5},{5,6},{6,7},{7,0},{8,9},{9,10},{10,1... | collective-permute-start | bytes 491528 | tf_op jit(solution)/shard_map/ppermute | solution.py:357
  106.8 12.5 %collective-permute-start.7 = (bf16[4,1,64,320]{3,2,1,0:T(8,128)(2,1)}, bf16[4,1,64,320]{3,2,1,0:T(8,128)(2,1)}, u32[]{:S(2)}, u32[]{:S(2)}) collective-permute-start(bf16[4,1,64,320]{3,2,1,0:T(8,128)(2,1)} %get-tuple-element.51), channel_id=1, source_target_pairs={{1,0},{2,1},{3,2},{4,3},{5,4},{6,5},{7,6},{0,7},{9,8},{10,9},{11,1... | collective-permute-start | bytes 491528 | tf_op jit(solution)/shard_map/ppermute | solution.py:358
  111.8 3.1 %copy-start.7 = (bf16[320,1280]{1,0:T(8,128)(2,1)S(1)}, bf16[320,1280]{1,0:T(8,128)(2,1)}, u32[]{:S(2)}) copy-start(bf16[320,1280]{1,0:T(8,128)(2,1)} %proj_in.3) | copy-start | bytes 2457604
  111.8 3.1 %copy-start.27 = (bf16[32,320]{1,0:T(8,128)(2,1)S(1)}, bf16[32,320]{1,0:T(8,128)(2,1)}, u32[]{:S(2)}) copy-start(bf16[32,320]{1,0:T(8,128)(2,1)} %copy-done.26) | copy-start | bytes 61444
  114.9 1.4 %copy-start.3 = (bf16[640,1280]{1,0:T(8,128)(2,1)S(1)}, bf16[640,1280]{1,0:T(8,128)(2,1)}, u32[]{:S(2)}) copy-start(bf16[640,1280]{1,0:T(8,128)(2,1)} %proj_out.3) | copy-start | bytes 4915204
  (16 other events, 14.6 us)

commit v2 on v1

--- a/solution.py
+++ b/solution.py
@@ -31,15 +31,43 @@
     return jnp.dot(a, b, preferred_element_type=f32, precision=lax.Precision.HIGHEST)
 
 
-def call(kernel, out_shape, *operands, scratch=()):
+def call(kernel, out_shape, *operands, scratch=(), limit=12, far=(), far_out=(), pin=(), after=()):
+    count = len(operands)
+    near = pl.BlockSpec(memory_space=pltpu.VMEM)
+    away = pl.BlockSpec(memory_space=pltpu.HBM)
+    single = not isinstance(out_shape, tuple)
+    shapes = (out_shape,) if single else out_shape
+    out_specs = tuple(away if i in far_out else near for i in range(len(shapes)))
+    places = {**{i: pltpu.HBM for i in far_out}, **{i: pltpu.VMEM for i in pin}}
+    shapes = tuple(
+        places[i](each.shape, each.dtype) if i in places else each for i, each in enumerate(shapes)
+    )
+    operands = [
+        pltpu.with_memory_space_constraint(each, pltpu.HBM) if i in far else each
+        for i, each in enumerate(operands)
+    ]
+
+    def body(*refs):
+        kernel(*refs[:count], *refs[count + len(after) :])
+
     return pl.pallas_call(
-        kernel,
-        out_shape=out_shape,
-        in_specs=[pl.BlockSpec(memory_space=pltpu.VMEM)] * len(operands),
-        out_specs=jax.tree.map(lambda _: pl.BlockSpec(memory_space=pltpu.VMEM), out_shape),
+        body,
+        out_shape=shapes[0] if single else shapes,
+        in_specs=[away if i in far else near for i in range(count)] + [near] * len(after),
+        out_specs=out_specs[0] if single else out_specs,
         scratch_shapes=list(scratch),
-        compiler_params=pltpu.CompilerParams(vmem_limit_bytes=50 * 1024 * 1024),
-    )(*operands)
+        compiler_params=pltpu.CompilerParams(vmem_limit_bytes=limit * 1024 * 1024),
+    )(*operands, *after)
+
+
+def start(*copies):
+    for source, target, semaphore in copies:
+        pltpu.make_async_copy(source, target, semaphore).start()
+
+
+def wait(*copies):
+    for source, target, semaphore in copies:
+        pltpu.make_async_copy(source, target, semaphore).wait()
 
 
 def shape(dims, dtype):
@@ -216,7 +244,9 @@
         second[f] = dot_exact(select, sway)
 
 
-def coarse(payload, merged, bias, out, wide, chunks, *, heads, channels):
+def coarse(payload, merged, bias, out, wide, chunks, bias_here, sems, *, heads, channels):
+    bias_copy = (bias, bias_here, sems.at[0])
+    start(bias_copy)
     unpack(payload, wide, chunks)
     frames = payload.shape[0]
     pooled = wide[:, :channels].astype(bf16)
@@ -241,7 +271,8 @@
 
     query_rows = by_head(queries)
     grad_rows = by_head(grad_heads)
-    scores = dot_nt(query_rows, keys) * factor + bias[...]
+    wait(bias_copy)
+    scores = dot_nt(query_rows, keys) * factor + bias_here[...].reshape(heads * frames, frames)
     expd = jnp.exp(scores - jnp.max(scores, axis=1, keepdims=True))
     weights = expd / jnp.sum(expd, axis=1, keepdims=True)
     rounded = weights.astype(bf16)
@@ -338,17 +369,55 @@
         out[:, at] = row.astype(bf16)
 
 
-def prepare(cot, proj_in, proj_query, proj_key, proj_value, proj_out, merged, grad_heads, cot_in):
+def project_cot(cot, proj_in, proj_out, grad_heads, cot_in, low, high, sems):
+    copies = ((proj_in, low, sems.at[0]), (proj_out, high, sems.at[1]))
+    start(*copies)
+    wait(copies[0])
+    cot_in[...] = dot_nt(cot[...], low[...])
+    wait(copies[1])
+    grad_heads[...] = dot_nt(cot[...], high[...]).astype(bf16)
+
+
+def merge(proj_in, proj_query, proj_key, proj_value, merged, token, low, weights, sems):
     width = proj_query.shape[1]
-    for at, weight in enumerate((proj_query, proj_key, proj_value)):
-        merged[:, at * width : (at + 1) * width] = dot(proj_in[...], weight[...]).astype(bf16)
-    grad_heads[...] = dot_nt(cot[...], proj_out[...]).astype(bf16)
-    cot_in[...] = dot_nt(cot[...], proj_in[...])
-
-
-def coarse_finish(pooled, proj_in, blended, proj_out, out):
-    low = dot(pooled[...], proj_in[...]).astype(bf16).astype(f32)
-    out[...] = (low + dot(blended[...], proj_out[...])).astype(bf16)
+    first = (proj_in, low, sems.at[3])
+    copies = [
+        (weight, weights.at[at], sems.at[at])
+        for at, weight in enumerate((proj_query, proj_key, proj_value))
+    ]
+    start(first, *copies)
+    wait(first)
+    for at in range(3):
+        wait(copies[at])
+        merged[:, at * width : (at + 1) * width] = dot(low[...], weights[at]).astype(bf16)
+    token[...] = jnp.zeros_like(token)
+
+
+def turn(kernel_space, kernel_time, back_space, back_time, token, space, turned, time, sems):
+    channels = kernel_time.shape[-1]
+    inward = ((kernel_time, time, sems.at[0]), (kernel_space, space, sems.at[1]))
+    outward = [(turned.at[i], back_space.at[i], sems.at[2 + i]) for i in range(3)]
+    start(*inward)
+    wait(inward[0])
+    for i in range(3):
+        back_time[i] = time[2 - i].T
+    wait(inward[1])
+    for i in range(3):
+        for j in range(3):
+            turned[i, j * channels : (j + 1) * channels] = space[2 - i, 2 - j].T
+        start(outward[i])
+    token[...] = jnp.zeros_like(token)
+    wait(*outward)
+
+
+def coarse_finish(pooled, proj_in, blended, proj_out, out, token, low, high, sems):
+    copies = ((proj_in, low, sems.at[0]), (proj_out, high, sems.at[1]))
+    start(*copies)
+    wait(copies[0])
+    base = dot(pooled[...], low[...]).astype(bf16).astype(f32)
+    wait(copies[1])
+    out[...] = (base + dot(blended[...], high[...])).astype(bf16)
+    token[...] = jnp.zeros_like(token)
 
 
 def neighbours(tail, head, axis):
@@ -396,28 +465,30 @@
     partial = shape((rows, frames * columns, channels), f32)
 
     weight_space = kernel_space.reshape(3, 3 * channels, channels)
-    back_space = jnp.flip(kernel_space, (0, 1)).swapaxes(2, 3).reshape(3, 3 * channels, channels)
-    back_time = jnp.flip(kernel_time, 0).swapaxes(1, 2)
 
     above, below = neighbours(frames_in[:, -1:], frames_in[:, :1], "space")
     part = call(space_own, partial, frames_in, weight_space)
     cot = cotangent.reshape(half, depth)
-    merged, grad_heads, cot_in = call(
-        prepare,
-        (
-            shape((channels, 3 * width), bf16),
-            shape((half, width), bf16),
-            shape((half, channels), f32),
-        ),
+    token = shape((8, LANES), f32)
+    low = pltpu.VMEM(proj_in.shape, bf16)
+    high = pltpu.VMEM(proj_out.shape, bf16)
+    grad_heads, cot_in = call(
+        project_cot,
+        (shape((half, width), bf16), shape((half, channels), f32)),
         cot,
         proj_in,
-        proj_query,
-        proj_key,
-        proj_value,
         proj_out,
+        scratch=(low, high, pltpu.SemaphoreType.DMA((2,))),
+        far=(1, 2),
     )
     spatial, first, last = call(
-        spatial_finish, (band, edge, edge), part, above, below, weight_space
+        spatial_finish,
+        (band, edge, edge),
+        part,
+        above,
+        below,
+        weight_space,
+        after=(cot_in,),
     )
     before, after = neighbours(last, first, "frame")
     part = call(time_own, flat, spatial, kernel_time)
@@ -428,6 +499,23 @@
         before,
         after,
         kernel_time,
+        pin=(0,),
+    )
+    merged, merged_token = call(
+        merge,
+        (shape((channels, 3 * width), bf16), token),
+        proj_in,
+        proj_query,
+        proj_key,
+        proj_value,
+        scratch=(
+            low,
+            pltpu.VMEM((3, *proj_query.shape), bf16),
+            pltpu.SemaphoreType.DMA((4,)),
+        ),
+        far=(0, 1, 2, 3),
+        pin=(0,),
+        after=(stats,),
     )
     stats = exchange(stats, "space")
     sent, pooled = call(
@@ -440,6 +528,22 @@
         grad_heads,
         cot_in,
         scratch=packing,
+        after=(merged_token,),
+    )
+    back_space, back_time, turn_token = call(
+        turn,
+        (shape(weight_space.shape, bf16), shape(kernel_time.shape, bf16), token),
+        kernel_space,
+        kernel_time,
+        scratch=(
+            pltpu.VMEM(kernel_space.shape, bf16),
+            pltpu.VMEM(weight_space.shape, bf16),
+            pltpu.VMEM(kernel_time.shape, bf16),
+            pltpu.SemaphoreType.DMA((5,)),
+        ),
+        far=(0, 1),
+        far_out=(0,),
+        after=(pooled,),
     )
     received = exchange(sent, "frame")
     normed, slope, slope_sum, sway_sum, inv = call(
@@ -454,14 +558,21 @@
         temporal,
         stats,
         gain,
+        pin=(0, 1, 2, 3, 4),
     )
     sent = call(
         lambda *refs: coarse(*refs, heads=heads, channels=channels),
         payload,
         received,
         merged,
-        frame_bias.reshape(-1, frame_bias.shape[-1]),
-        scratch=packing,
+        frame_bias,
+        scratch=(
+            *packing,
+            pltpu.VMEM(frame_bias.shape, f32),
+            pltpu.SemaphoreType.DMA((1,)),
+        ),
+        far=(2,),
+        after=(turn_token,),
     )
     received = exchange(sent, "frame")
     stats, grad_pooled, blended = call(
@@ -476,10 +587,18 @@
         sway_sum,
         scratch=packing,
     )
+    coarse_out, coarse_token = call(
+        coarse_finish,
+        (shape((half, depth), bf16), token),
+        pooled,
+        proj_in,
+        blended,
+        proj_out,
+        scratch=(low, high, pltpu.SemaphoreType.DMA((2,))),
+        far=(1, 3),
+        after=(stats,),
+    )
     stats = exchange(stats, "space")
-    coarse_out = call(
-        coarse_finish, shape((half, depth), bf16), pooled, proj_in, blended, proj_out
-    )
     grad_temporal, first, last, grad_gain = call(
         lambda *refs: norm_back(*refs, cell_count=cell_count),
         (band, edge, edge, shape((1, SLOT), f32)),
@@ -488,6 +607,7 @@
         normed,
         slope,
         inv,
+        after=(coarse_token,),
     )
     before, after = neighbours(last, first, "frame")
     part = call(time_own, flat, grad_temporal, back_time)

time: 123 us -> 108 us (0.88)
  the two profiles are of different devices: /device:TPU:0 before, /device:TPU:26 now
where the time goes in v2:
time: 108 us; the launch traced here: 107 us
  starting transfers between devices  40.3 us (37%)
  Pallas kernels  30.7 us (28%)
  waiting for transfers between devices  29.3 us (27%)
  local copies, waits for them, and re-layouts  5.92 us (5%)
    pallas_call x17, Pallas kernels, call(): pl.pallas_call(body, out_shape=shapes[0] if single else shapes, in_specs=...  30.7 us
    all_to_all x4, starting transfers between devices, exchange(): lax.all_to_all(payload, axis, split_axis=0, concat_axis=0, tiled=True)  23.8 us
    all_to_all x4, waiting for transfers between devices, exchange(): lax.all_to_all(payload, axis, split_axis=0, concat_axis=0, tiled=True)  18.2 us
    ppermute x4, starting transfers between devices, neighbours(): lax.ppermute(head, axis, [((i + 1) % count, i) for i in range(count)])  11.5 us
    ppermute x4, waiting for transfers between devices, neighbours(): lax.ppermute(head, axis, [((i + 1) % count, i) for i in range(count)])  6.37 us
    ppermute x4, starting transfers between devices, neighbours(): lax.ppermute(tail, axis, [(i, (i + 1) % count) for i in range(count)])  5 us
    ppermute x4, waiting for transfers between devices, neighbours(): lax.ppermute(tail, axis, [(i, (i + 1) % count) for i in range(count)])  4.67 us
    unnamed x20, local copies, waits for them, and re-layouts  4.25 us
  transfers between devices with their start and end apart: 12, of which 7 were waited for; matrix products, arithmetic and copies ran while one was open for 1% of the time, Pallas kernels for 19%

profile of v2, /device:TPU:26, one launch (start us, length us, event | category | flops | bytes accessed | tf_op | source)
XLA Modules:
  0.0 107.0 jit_solution(18064821604421585993)
XLA Ops:
  1.7 2.0 %collective-permute-start = (bf16[4,1,64,320]{3,2,1,0:T(8,128)(2,1)S(1)}, bf16[4,1,64,320]{3,2,1,0:T(8,128)(2,1)S(1)}, u32[]{:S(2)}, u32[]{:S(2)}) collective-permute-start(bf16[4,1,64,320]{3,2,1,0:T(8,128)(2,1)S(1)} %get-tuple-element.66), channel_id=1, source_target_pairs={{0,1},{1,2},{2,3},{3,4},{4,5},{5,6},{6,7},{7,0},{8,9},{9,10},{10,1... | collective-permute-start | bytes 491528 | tf_op jit(solution)/shard_map/ppermute | solution.py:426
  3.8 1.6 %copy-done = bf16[3,3,320,320]{3,2,1,0:T(8,128)(2,1)S(1)} copy-done((bf16[3,3,320,320]{3,2,1,0:T(8,128)(2,1)S(1)}, bf16[3,3,320,320]{3,2,1,0:T(8,128)(2,1)}, u32[]{:S(2)}) %copy-start) | copy-done | bytes 1843224
  7.7 2.5 %shard_map.131 = (bf16[32,640]{1,0:T(8,128)(2,1)S(1)}, f32[32,320]{1,0:T(8,128)S(1)}) custom-call(bf16[32,1280]{1,0:T(8,128)(2,1)S(1)} %bitcast.5, bf16[320,1280]{1,0:T(8,128)(2,1)} %refs_1_.9, bf16[640,1280]{1,0:T(8,128)(2,1)} %refs_3_.5), custom_call_target="tpu_custom_call" | custom-call | tf_op jit(solution)/shard_map/pallas_call | solution.py:53
  10.2 2.1 %collective-permute-done.1.refs_2_ = bf16[4,1,64,320]{3,2,1,0:T(8,128)(2,1)S(1)} collective-permute-done((bf16[4,1,64,320]{3,2,1,0:T(8,128)(2,1)S(1)}, bf16[4,1,64,320]{3,2,1,0:T(8,128)(2,1)S(1)}, u32[]{:S(2)}, u32[]{:S(2)}) %collective-permute-start.1) | collective-permute-done | bytes 163872 | tf_op jit(solution)/shard_map/ppermute | solution.py:427
  13.1 6.1 %collective-permute-start.3 = (bf16[1,2,64,320]{3,2,1,0:T(8,128)(2,1)S(1)}, bf16[1,2,64,320]{3,2,1,0:T(8,128)(2,1)S(1)}, u32[]{:S(2)}, u32[]{:S(2)}) collective-permute-start(bf16[1,2,64,320]{3,2,1,0:T(8,128)(2,1)S(1)} %get-tuple-element.37), channel_id=1, source_target_pairs={{8,0},{16,8},{24,16},{32,24},{40,32},{48,40},{56,48},{64,56},{72,6... | collective-permute-start | bytes 245768 | tf_op jit(solution)/shard_map/ppermute | solution.py:427
  19.9 1.4 %collective-permute-done.2.refs_1_ = bf16[1,2,64,320]{3,2,1,0:T(8,128)(2,1)S(1)} collective-permute-done((bf16[1,2,64,320]{3,2,1,0:T(8,128)(2,1)S(1)}, bf16[1,2,64,320]{3,2,1,0:T(8,128)(2,1)S(1)}, u32[]{:S(2)}, u32[]{:S(2)}) %collective-permute-start.2) | collective-permute-done | bytes 81952 | tf_op jit(solution)/shard_map/ppermute | solution.py:426
  22.5 6.7 %all-to-all-start = ((f32[8,8,128]{2,1,0:T(8,128)}), f32[8,8,128]{2,1,0:T(8,128)S(1)}, u32[]{:S(2)}, u32[]{:S(2)}) async-start(f32[8,8,128]{2,1,0:T(8,128)} %get-tuple-element.39.refs_4_), calls=%async_computation | async-start | bytes 65536 | tf_op jit(solution)/shard_map/all_to_all | solution.py:432
  29.2 5.4 %shard_map.135 = (bf16[320,1920]{1,0:T(8,128)(2,1)S(1)}, f32[8,128]{1,0:T(8,128)S(1)}) custom-call(bf16[320,1280]{1,0:T(8,128)(2,1)} %refs_1_.9, bf16[1280,640]{1,0:T(8,128)(2,1)} %refs_1_.7, bf16[1280,640]{1,0:T(8,128)(2,1)} %refs_2_.5, bf16[1280,640]{1,0:T(8,128)(2,1)} %refs_3_.4, f32[8,8,128]{2,1,0:T(8,128)} %get-tuple-element.39.refs_4_), custom_call_target="tpu_custom_call" | custom-call | tf_op jit(solution)/shard_map/pallas_call | solution.py:53
  34.6 1.8 %shard_map.136 = (bf16[32,16,128]{2,1,0:T(8,128)(2,1)}, bf16[32,320]{1,0:T(8,128)(2,1)S(1)}) custom-call(f32[512,320]{1,0:T(8,128)S(1)} %get-tuple-element.38.refs_0_, f32[8,8,128]{2,1,0:T(8,128)S(1)} %all-to-all-done.refs_1_, bf16[4,2,64,320]{3,2,1,0:T(8,128)(2,1)S(1)} %copy-done.5, f32[1,320]{1,0:T(1,128)S(1)} %reshape.20.refs_3_.refs_2_, ...), custom_call_target="tpu_custom_call" | custom-call | tf_op jit(solution)/shard_map/pallas_call | solution.py:53
  36.4 7.6 %all-to-all-start.1 = ((bf16[32,16,128]{2,1,0:T(8,128)(2,1)}), bf16[32,16,128]{2,1,0:T(8,128)(2,1)S(1)}, u32[]{:S(2)}, u32[]{:S(2)}) async-start(bf16[32,16,128]{2,1,0:T(8,128)(2,1)} %get-tuple-element.43), calls=%async_computation.1 | async-start | bytes 262144 | tf_op jit(solution)/shard_map/all_to_all | solution.py:432
  44.0 3.6 %shard_map.137 = (bf16[3,960,320]{2,1,0:T(8,128)(2,1)}, bf16[3,320,320]{2,1,0:T(8,128)(2,1)S(1)}, f32[8,128]{1,0:T(8,128)S(1)}) custom-call(bf16[3,3,320,320]{3,2,1,0:T(8,128)(2,1)} %refs_0_.5, bf16[3,320,320]{2,1,0:T(8,128)(2,1)} %refs_1_.8, bf16[32,320]{1,0:T(8,128)(2,1)S(1)} %get-tuple-element.42.refs_2_.refs_0_), custom_call_target="tpu_custom_call" | custom-call | tf_op jit(solution)/shard_map/pallas_call | solution.py:53
  47.6 8.2 %all-to-all-done.1.refs_0_ = bf16[32,16,128]{2,1,0:T(8,128)(2,1)S(1)} async-done(((bf16[32,16,128]{2,1,0:T(8,128)(2,1)}), bf16[32,16,128]{2,1,0:T(8,128)(2,1)S(1)}, u32[]{:S(2)}, u32[]{:S(2)}) %all-to-all-start.1) | async-done | bytes 131104 | tf_op jit(solution)/shard_map/all_to_all | solution.py:432
  55.7 3.5 %shard_map.138 = bf16[32,16,128]{2,1,0:T(8,128)(2,1)} custom-call(bf16[32,16,128]{2,1,0:T(8,128)(2,1)S(1)} %all-to-all-done.1.refs_0_, bf16[320,1920]{1,0:T(8,128)(2,1)S(1)} %get-tuple-element.44.refs_1_, f32[10,32,32]{2,1,0:T(8,128)} %refs_2_.7, f32[8,128]{1,0:T(8,128)S(1)} %get-tuple-element.45.refs_3_), custom_call_target="tpu_custom_call" | custom-call | tf_op jit(solution)/shard_map/pallas_call | solution.py:53
  59.3 3.9 %all-to-all-start.2 = ((bf16[32,16,128]{2,1,0:T(8,128)(2,1)}), bf16[32,16,128]{2,1,0:T(8,128)(2,1)S(1)}, u32[]{:S(2)}, u32[]{:S(2)}) async-start(bf16[32,16,128]{2,1,0:T(8,128)(2,1)} %shard_map.138), calls=%async_computation.2 | async-start | bytes 262144 | tf_op jit(solution)/shard_map/all_to_all | solution.py:432
  65.1 10.0 %all-to-all-done.2.refs_0_ = bf16[32,16,128]{2,1,0:T(8,128)(2,1)S(1)} async-done(((bf16[32,16,128]{2,1,0:T(8,128)(2,1)}), bf16[32,16,128]{2,1,0:T(8,128)(2,1)S(1)}, u32[]{:S(2)}, u32[]{:S(2)}) %all-to-all-start.2) | async-done | bytes 131104 | tf_op jit(solution)/shard_map/all_to_all | solution.py:432
  77.0 5.7 %all-to-all-start.3 = ((f32[8,16,128]{2,1,0:T(8,128)}), f32[8,16,128]{2,1,0:T(8,128)S(1)}, u32[]{:S(2)}, u32[]{:S(2)}) async-start(f32[8,16,128]{2,1,0:T(8,128)} %get-tuple-element.49.refs_4_), calls=%async_computation.3 | async-start | bytes 131072 | tf_op jit(solution)/shard_map/all_to_all | solution.py:432
  82.7 3.6 %shard_map.141 = (bf16[32,1280]{1,0:T(8,128)(2,1)}, f32[8,128]{1,0:T(8,128)S(1)}) custom-call(bf16[32,320]{1,0:T(8,128)(2,1)S(1)} %get-tuple-element.42.refs_2_.refs_0_, bf16[320,1280]{1,0:T(8,128)(2,1)} %refs_1_.9, bf16[32,640]{1,0:T(8,128)(2,1)S(1)} %get-tuple-element.48.refs_2_, bf16[640,1280]{1,0:T(8,128)(2,1)} %refs_3_.5, ...), custom_call_target="tpu_custom_call" | custom-call | tf_op jit(solution)/shard_map/pallas_call | solution.py:53
  86.8 5.3 %collective-permute-start.5 = (bf16[1,2,64,320]{3,2,1,0:T(8,128)(2,1)S(1)}, bf16[1,2,64,320]{3,2,1,0:T(8,128)(2,1)S(1)}, u32[]{:S(2)}, u32[]{:S(2)}) collective-permute-start(bf16[1,2,64,320]{3,2,1,0:T(8,128)(2,1)S(1)} %get-tuple-element.59), channel_id=1, source_target_pairs={{8,0},{16,8},{24,16},{32,24},{40,32},{48,40},{56,48},{64,56},{72,6... | collective-permute-start | bytes 245768 | tf_op jit(solution)/shard_map/ppermute | solution.py:427
  93.0 1.5 %collective-permute-done.4.refs_1_ = bf16[1,2,64,320]{3,2,1,0:T(8,128)(2,1)S(1)} collective-permute-done((bf16[1,2,64,320]{3,2,1,0:T(8,128)(2,1)S(1)}, bf16[1,2,64,320]{3,2,1,0:T(8,128)(2,1)S(1)}, u32[]{:S(2)}, u32[]{:S(2)}) %collective-permute-start.4) | collective-permute-done | bytes 81952 | tf_op jit(solution)/shard_map/ppermute | solution.py:426
  94.8 2.8 %collective-permute-start.6 = (bf16[4,1,64,320]{3,2,1,0:T(8,128)(2,1)S(1)}, bf16[4,1,64,320]{3,2,1,0:T(8,128)(2,1)S(1)}, u32[]{:S(2)}, u32[]{:S(2)}) collective-permute-start(bf16[4,1,64,320]{3,2,1,0:T(8,128)(2,1)S(1)} %get-tuple-element.62), channel_id=1, source_target_pairs={{0,1},{1,2},{2,3},{3,4},{4,5},{5,6},{6,7},{7,0},{8,9},{9,10},{10,1... | collective-permute-start | bytes 491528 | tf_op jit(solution)/shard_map/ppermute | solution.py:426
  98.2 1.3 %shard_map.145.refs_0_ = f32[2,256,320]{2,1,0:T(8,128)S(1)} custom-call(bf16[4,2,64,320]{3,2,1,0:T(8,128)(2,1)S(1)} %get-tuple-element.60.refs_0_, bf16[3,960,320]{2,1,0:T(8,128)(2,1)S(1)} %copy-done.2), custom_call_target="tpu_custom_call" | custom-call | tf_op jit(solution)/shard_map/pallas_call | solution.py:53
  99.5 1.7 %collective-permute-done.6.refs_1_ = bf16[4,1,64,320]{3,2,1,0:T(8,128)(2,1)S(1)} collective-permute-done((bf16[4,1,64,320]{3,2,1,0:T(8,128)(2,1)S(1)}, bf16[4,1,64,320]{3,2,1,0:T(8,128)(2,1)S(1)}, u32[]{:S(2)}, u32[]{:S(2)}) %collective-permute-start.6) | collective-permute-done | bytes 163872 | tf_op jit(solution)/shard_map/ppermute | solution.py:426
  101.2 4.3 %collective-permute-done.7.refs_2_ = bf16[4,1,64,320]{3,2,1,0:T(8,128)(2,1)S(1)} collective-permute-done((bf16[4,1,64,320]{3,2,1,0:T(8,128)(2,1)S(1)}, bf16[4,1,64,320]{3,2,1,0:T(8,128)(2,1)S(1)}, u32[]{:S(2)}, u32[]{:S(2)}) %collective-permute-start.7) | collective-permute-done | bytes 163872 | tf_op jit(solution)/shard_map/ppermute | solution.py:427
  105.5 1.5 %shard_map.146 = bf16[4,2,64,320]{3,2,1,0:T(8,128)(2,1)} custom-call(f32[2,256,320]{2,1,0:T(8,128)S(1)} %shard_map.145.refs_0_, bf16[4,1,64,320]{3,2,1,0:T(8,128)(2,1)S(1)} %collective-permute-done.6.refs_1_, bf16[4,1,64,320]{3,2,1,0:T(8,128)(2,1)S(1)} %collective-permute-done.7.refs_2_, bf16[3,960,320]{2,1,0:T(8,128)(2,1)S(1)} %copy-done.2, ...), custom_call_target="tpu_custom_call" | custom-call | tf_op jit(solution)/shard_map/pallas_call | solution.py:53
  (40 shorter events, 12.1 us)
Async XLA Ops:
  1.7 8.5 %collective-permute-start = (bf16[4,1,64,320]{3,2,1,0:T(8,128)(2,1)S(1)}, bf16[4,1,64,320]{3,2,1,0:T(8,128)(2,1)S(1)}, u32[]{:S(2)}, u32[]{:S(2)}) collective-permute-start(bf16[4,1,64,320]{3,2,1,0:T(8,128)(2,1)S(1)} %get-tuple-element.66), channel_id=1, source_target_pairs={{0,1},{1,2},{2,3},{3,4},{4,5},{5,6},{6,7},{7,0},{8,9},{9,10},{10,1... | collective-permute-start | bytes 491528 | tf_op jit(solution)/shard_map/ppermute | solution.py:426
  3.7 8.6 %collective-permute-start.1 = (bf16[4,1,64,320]{3,2,1,0:T(8,128)(2,1)S(1)}, bf16[4,1,64,320]{3,2,1,0:T(8,128)(2,1)S(1)}, u32[]{:S(2)}, u32[]{:S(2)}) collective-permute-start(bf16[4,1,64,320]{3,2,1,0:T(8,128)(2,1)S(1)} %get-tuple-element.65), channel_id=1, source_target_pairs={{1,0},{2,1},{3,2},{4,3},{5,4},{6,5},{7,6},{0,7},{9,8},{10,9},{11,1... | collective-permute-start | bytes 491528 | tf_op jit(solution)/shard_map/ppermute | solution.py:427
  3.8 1.6 %copy-start = (bf16[3,3,320,320]{3,2,1,0:T(8,128)(2,1)S(1)}, bf16[3,3,320,320]{3,2,1,0:T(8,128)(2,1)}, u32[]{:S(2)}) copy-start(bf16[3,3,320,320]{3,2,1,0:T(8,128)(2,1)} %refs_0_.5) | copy-start | bytes 5529604
  5.4 1.0 copy-start.4
  6.4 1.3 %copy-start.8 = (bf16[1,1,32,1280]{3,2,1,0:T(8,128)(2,1)S(1)}, bf16[1,1,32,1280]{3,2,1,0:T(8,128)(2,1)}, u32[]{:S(2)}) copy-start(bf16[1,1,32,1280]{3,2,1,0:T(8,128)(2,1)} %param.21) | copy-start | bytes 245764
  7.7 4.6 %copy-start.1 = (bf16[3,3,320,320]{3,2,1,0:T(8,128)(2,1)S(1)}, bf16[3,3,320,320]{3,2,1,0:T(8,128)(2,1)}, u32[]{:S(2)}) copy-start(bf16[3,3,320,320]{3,2,1,0:T(8,128)(2,1)} %refs_0_.5) | copy-start | bytes 5529604
  12.3 6.9 %copy-start.3 = (bf16[3,320,320]{2,1,0:T(8,128)(2,1)S(1)}, bf16[3,320,320]{2,1,0:T(8,128)(2,1)}, u32[]{:S(2)}) copy-start(bf16[3,320,320]{2,1,0:T(8,128)(2,1)} %refs_1_.8) | copy-start | bytes 1843204
  13.0 8.4 %collective-permute-start.2 = (bf16[1,2,64,320]{3,2,1,0:T(8,128)(2,1)S(1)}, bf16[1,2,64,320]{3,2,1,0:T(8,128)(2,1)S(1)}, u32[]{:S(2)}, u32[]{:S(2)}) collective-permute-start(bf16[1,2,64,320]{3,2,1,0:T(8,128)(2,1)S(1)} %get-tuple-element.36), channel_id=1, source_target_pairs={{0,8},{8,16},{16,24},{24,32},{32,40},{40,48},{48,56},{56,64},{64,7... | collective-permute-start | bytes 245768 | tf_op jit(solution)/shard_map/ppermute | solution.py:426
  13.1 8.3 %collective-permute-start.3 = (bf16[1,2,64,320]{3,2,1,0:T(8,128)(2,1)S(1)}, bf16[1,2,64,320]{3,2,1,0:T(8,128)(2,1)S(1)}, u32[]{:S(2)}, u32[]{:S(2)}) collective-permute-start(bf16[1,2,64,320]{3,2,1,0:T(8,128)(2,1)S(1)} %get-tuple-element.37), channel_id=1, source_target_pairs={{8,0},{16,8},{24,16},{32,24},{40,32},{48,40},{56,48},{64,56},{72,6... | collective-permute-start | bytes 245768 | tf_op jit(solution)/shard_map/ppermute | solution.py:427
  19.2 10.0 %copy-start.9 = (f32[320]{0:T(512)S(1)}, f32[320]{0:T(512)}, u32[]{:S(2)}) copy-start(f32[320]{0:T(512)} %param.14) | copy-start | bytes 3844
  22.5 12.0 %all-to-all-start = ((f32[8,8,128]{2,1,0:T(8,128)}), f32[8,8,128]{2,1,0:T(8,128)S(1)}, u32[]{:S(2)}, u32[]{:S(2)}) async-start(f32[8,8,128]{2,1,0:T(8,128)} %get-tuple-element.39.refs_4_), calls=%async_computation | async-start | bytes 65536 | tf_op jit(solution)/shard_map/all_to_all | solution.py:432
  29.2 5.4 %copy-start.5 = (bf16[4,2,64,320]{3,2,1,0:T(8,128)(2,1)S(1)}, bf16[4,2,64,320]{3,2,1,0:T(8,128)(2,1)}, u32[]{:S(2)}) copy-start(bf16[4,2,64,320]{3,2,1,0:T(8,128)(2,1)} %refs_2_.6) | copy-start | bytes 983044
  36.4 19.4 %all-to-all-start.1 = ((bf16[32,16,128]{2,1,0:T(8,128)(2,1)}), bf16[32,16,128]{2,1,0:T(8,128)(2,1)S(1)}, u32[]{:S(2)}, u32[]{:S(2)}) async-start(bf16[32,16,128]{2,1,0:T(8,128)(2,1)} %get-tuple-element.43), calls=%async_computation.1 | async-start | bytes 262144 | tf_op jit(solution)/shard_map/all_to_all | solution.py:432
  59.3 15.8 %all-to-all-start.2 = ((bf16[32,16,128]{2,1,0:T(8,128)(2,1)}), bf16[32,16,128]{2,1,0:T(8,128)(2,1)S(1)}, u32[]{:S(2)}, u32[]{:S(2)}) async-start(bf16[32,16,128]{2,1,0:T(8,128)(2,1)} %shard_map.138), calls=%async_computation.2 | async-start | bytes 262144 | tf_op jit(solution)/shard_map/all_to_all | solution.py:432
  64.4 0.7 copy-start.6
  75.1 0.9 copy-start.7
  77.0 9.3 %all-to-all-start.3 = ((f32[8,16,128]{2,1,0:T(8,128)}), f32[8,16,128]{2,1,0:T(8,128)S(1)}, u32[]{:S(2)}, u32[]{:S(2)}) async-start(f32[8,16,128]{2,1,0:T(8,128)} %get-tuple-element.49.refs_4_), calls=%async_computation.3 | async-start | bytes 131072 | tf_op jit(solution)/shard_map/all_to_all | solution.py:432
  86.7 7.7 %collective-permute-start.4 = (bf16[1,2,64,320]{3,2,1,0:T(8,128)(2,1)S(1)}, bf16[1,2,64,320]{3,2,1,0:T(8,128)(2,1)S(1)}, u32[]{:S(2)}, u32[]{:S(2)}) collective-permute-start(bf16[1,2,64,320]{3,2,1,0:T(8,128)(2,1)S(1)} %get-tuple-element.58), channel_id=1, source_target_pairs={{0,8},{8,16},{16,24},{24,32},{32,40},{40,48},{48,56},{56,64},{64,7... | collective-permute-start | bytes 245768 | tf_op jit(solution)/shard_map/ppermute | solution.py:426
  86.8 7.6 %collective-permute-start.5 = (bf16[1,2,64,320]{3,2,1,0:T(8,128)(2,1)S(1)}, bf16[1,2,64,320]{3,2,1,0:T(8,128)(2,1)S(1)}, u32[]{:S(2)}, u32[]{:S(2)}) collective-permute-start(bf16[1,2,64,320]{3,2,1,0:T(8,128)(2,1)S(1)} %get-tuple-element.59), channel_id=1, source_target_pairs={{8,0},{16,8},{24,16},{32,24},{40,32},{48,40},{56,48},{64,56},{72,6... | collective-permute-start | bytes 245768 | tf_op jit(solution)/shard_map/ppermute | solution.py:427
  92.2 6.0 %copy-start.2 = (bf16[3,960,320]{2,1,0:T(8,128)(2,1)S(1)}, bf16[3,960,320]{2,1,0:T(8,128)(2,1)}, u32[]{:S(2)}) copy-start(bf16[3,960,320]{2,1,0:T(8,128)(2,1)} %get-tuple-element.61.refs_1_.refs_3_) | copy-start | bytes 5529604
  94.8 6.4 %collective-permute-start.6 = (bf16[4,1,64,320]{3,2,1,0:T(8,128)(2,1)S(1)}, bf16[4,1,64,320]{3,2,1,0:T(8,128)(2,1)S(1)}, u32[]{:S(2)}, u32[]{:S(2)}) collective-permute-start(bf16[4,1,64,320]{3,2,1,0:T(8,128)(2,1)S(1)} %get-tuple-element.62), channel_id=1, source_target_pairs={{0,1},{1,2},{2,3},{3,4},{4,5},{5,6},{6,7},{7,0},{8,9},{9,10},{10,1... | collective-permute-start | bytes 491528 | tf_op jit(solution)/shard_map/ppermute | solution.py:426
  97.6 7.9 %collective-permute-start.7 = (bf16[4,1,64,320]{3,2,1,0:T(8,128)(2,1)S(1)}, bf16[4,1,64,320]{3,2,1,0:T(8,128)(2,1)S(1)}, u32[]{:S(2)}, u32[]{:S(2)}) collective-permute-start(bf16[4,1,64,320]{3,2,1,0:T(8,128)(2,1)S(1)} %get-tuple-element.63), channel_id=1, source_target_pairs={{1,0},{2,1},{3,2},{4,3},{5,4},{6,5},{7,6},{0,7},{9,8},{10,9},{11,1... | collective-permute-start | bytes 491528 | tf_op jit(solution)/shard_map/ppermute | solution.py:427

commit v3 on v2

--- a/solution.py
+++ b/solution.py
@@ -80,27 +80,40 @@
     col = lax.broadcasted_iota(jnp.int32, cells.shape, 1)
     left = jnp.where(col == 0, 0.0, pltpu.roll(wide, 1, 1)).astype(bf16)
     right = jnp.where(col == columns - 1, 0.0, pltpu.roll(wide, columns - 1, 1)).astype(bf16)
-    merged = jnp.concatenate([left, cells, right], axis=2)
-    return merged.reshape(-1, merged.shape[2])
-
-
-def space_own(cells, weight, part):
+    return [each.reshape(-1, cells.shape[2]) for each in (left, cells, right)]
+
+
+def row_sum(cells, weight, i, back):
+    if back:
+        return sum(dot_nt(cells[j], weight[2 - i, 2 - j]) for j in range(3))
+    channels = cells[0].shape[1]
+    merged = jnp.concatenate(cells, axis=1)
+    return dot(merged, weight[i].reshape(3 * channels, channels))
+
+
+def space_own(cells, weight_far, part, weight, sems, *, back):
+    copies = [(weight_far.at[i], weight.at[i], sems.at[i]) for i in range(3)]
+    start(*copies)
     first = taps(cells[:, 0])
     second = taps(cells[:, 1])
-    part[0] = dot(first, weight[1]) + dot(second, weight[2])
-    part[1] = dot(second, weight[1]) + dot(first, weight[0])
-
-
-def space_edges(part, above, below, weight):
+    wait(*copies)
+    part[0] = row_sum(first, weight, 1, back) + row_sum(second, weight, 2, back)
+    part[1] = row_sum(second, weight, 1, back) + row_sum(first, weight, 0, back)
+
+
+def space_edges(part, above, below, weight, back):
     at = lax.axis_index("space")
     count = lax.axis_size("space")
     upper = jnp.where(at > 0, above[:, 0], jnp.zeros_like(above[:, 0]))
     lower = jnp.where(at < count - 1, below[:, 0], jnp.zeros_like(below[:, 0]))
-    return part[0] + dot(taps(upper), weight[0]), part[1] + dot(taps(lower), weight[2])
+    return (
+        part[0] + row_sum(taps(upper), weight, 0, back),
+        part[1] + row_sum(taps(lower), weight, 2, back),
+    )
 
 
 def spatial_finish(part, above, below, weight, spatial, first, last):
-    rows = space_edges(part, above, below, weight)
+    rows = space_edges(part, above, below, weight, False)
     for at, row in enumerate(rows):
         row = row.astype(bf16).reshape(spatial.shape[0], *spatial.shape[2:])
         spatial[:, at] = row
@@ -108,10 +121,13 @@
         last[0, at] = row[-1]
 
 
-def time_own(cells, weight, part):
+def time_own(cells, weight_far, part, weight, sems):
+    copy = (weight_far, weight, sems.at[0])
+    start(copy)
     frames, _, _, channels = cells.shape
     flat = cells[...].reshape(-1, channels)
     step = flat.shape[0] // frames
+    wait(copy)
     part[...] = dot(flat, weight[1])
     part[step:] += dot(flat[:-step], weight[0])
     part[:-step] += dot(flat[step:], weight[2])
@@ -223,28 +239,70 @@
     )
 
 
-def slopes(temporal, stats, gain, normed_out, slope_out, first, second, inv_out, *, dims, cell_count):
+def slopes(
+    temporal,
+    stats,
+    gain,
+    normed_out,
+    slope_out,
+    first,
+    second,
+    inv_out,
+    head,
+    tail,
+    token,
+    *,
+    dims,
+    cell_count,
+):
     frames, rows, columns = dims
     channels = temporal.shape[1]
+    step = rows * columns
     mean, inv = moments(stats, frames, cell_count, channels)
     inv_out[...] = inv
-    select = pairs(columns // 2, 1.0)
     for f in range(frames):
-        lead = jnp.zeros((columns, channels), f32)
-        sway = jnp.zeros((columns, channels), f32)
-        for r in range(rows):
-            at = (f * rows + r) * columns
-            normed = (temporal[at : at + columns] - mean[f : f + 1]) * inv[f : f + 1]
-            slope = activation(normed, gain[...])[1] * gain[...] * (1.0 / 16.0)
-            normed_out[at : at + columns] = normed
-            slope_out[at : at + columns] = slope
-            lead += slope
-            sway += slope * normed
-        first[f] = dot_exact(select, lead)
-        second[f] = dot_exact(select, sway)
-
-
-def coarse(payload, merged, bias, out, wide, chunks, bias_here, sems, *, heads, channels):
+        here = slice(f * step, (f + 1) * step)
+        normed = (temporal[here] - mean[f : f + 1]) * inv[f : f + 1]
+        slope = slope_of(normed, gain)
+        normed_out[here] = normed.astype(bf16)
+        slope_out[here] = slope.astype(bf16)
+        first[f] = by_pixel(slope, rows, columns)
+        second[f] = by_pixel(slope * normed, rows, columns)
+    for f, edge in ((0, head), (frames - 1, tail)):
+        high = inv[f : f + 1].astype(bf16).astype(f32)
+        edge[:step] = normed_out[f * step : (f + 1) * step]
+        edge[step:] = jnp.concatenate(
+            [high, inv[f : f + 1] - high, jnp.zeros((edge.shape[0] - step - 2, channels), f32)],
+            axis=0,
+        ).astype(bf16)
+    token[...] = jnp.zeros_like(token)
+
+
+def slope_of(normed, gain):
+    return activation(normed, gain[...])[1] * gain[...] * (1.0 / 16.0)
+
+
+def by_pixel(cells, rows, columns):
+    total = cells[:columns]
+    for r in range(1, rows):
+        total = total + cells[r * columns : (r + 1) * columns]
+    return dot_exact(pairs(columns // 2, 1.0), total)
+
+
+def slopes_beside(before, after, gain, slope_out, first, second, inv_out, *, dims):
+    _, rows, columns = dims
+    step = rows * columns
+    for at, edge in enumerate((before, after)):
+        normed = edge[:step].astype(f32)
+        extra = edge[step:].astype(f32)
+        inv_out[at : at + 1] = extra[0:1] + extra[1:2]
+        slope = slope_of(normed, gain)
+        slope_out[at] = slope.astype(bf16)
+        first[at] = by_pixel(slope, rows, columns)
+        second[at] = by_pixel(slope * normed, rows, columns)
+
+
+def coarse(payload, merged, bias, out, wide, out_wide, chunks, bias_here, sems, *, heads, channels):
     bias_copy = (bias, bias_here, sems.at[0])
     start(bias_copy)
     unpack(payload, wide, chunks)
@@ -285,36 +343,51 @@
     grad_keys = dot_tn(grad_scores, query_rows) * factor
     grads = jnp.concatenate([grad_queries, grad_keys, grad_values], axis=1).astype(bf16)
     grad_pooled = (cot_in + dot_nt(grads, merged[...])).astype(bf16)
-    gain = jnp.sum(grad_pooled.astype(f32) * sway, axis=0, keepdims=True)
-    high = gain.astype(bf16).astype(f32)
+    low = grad_pooled.astype(f32)
+    gain = jnp.sum(low * sway, axis=0, keepdims=True)
+    outside = jnp.zeros((1, channels), f32)
     pack(
         [
-            (0, grad_pooled),
-            (SLOT, jnp.broadcast_to(high, (frames, channels))),
-            (2 * SLOT, jnp.broadcast_to(gain - high, (frames, channels))),
-            (3 * SLOT, blended),
+            (0, jnp.concatenate([outside, low[:-1]], axis=0)),
+            (channels, low),
+            (2 * channels, jnp.concatenate([low[1:], outside], axis=0)),
+            (3 * channels, jnp.broadcast_to(gain, (frames, channels))),
+            (4 * channels, blended),
         ],
-        wide,
+        out_wide,
         chunks,
         out,
     )
 
 
-def totals(payload, first, second, stats, grad_pooled, blended, wide, chunks):
+def totals(
+    payload, first, second, beside_first, beside_second, stats, grad_pooled, blended, wide, chunks
+):
     unpack(payload, wide, chunks)
     frames, _, channels = first.shape
-    low = wide[:, :channels]
-    grad_pooled[...] = low.astype(bf16)
-    blended[...] = wide[:, 3 * SLOT : 3 * SLOT + blended.shape[1]].astype(bf16)
-    gain = jnp.sum(wide[:, SLOT : 2 * SLOT] + wide[:, 2 * SLOT : 3 * SLOT], axis=0, keepdims=True)
+    lows = [wide[:, i * channels : (i + 1) * channels] for i in range(3)]
+    for i, low in enumerate(lows):
+        grad_pooled[i] = low.astype(bf16)
+    blended[...] = wide[:, 4 * channels : 4 * channels + blended.shape[1]].astype(bf16)
+    gain = jnp.sum(wide[:, 3 * channels : 4 * channels], axis=0, keepdims=True)
+
+    def over(own, beside):
+        return [
+            jnp.sum(beside[0] * lows[0], axis=0, keepdims=True),
+            jnp.sum(own[...] * lows[1][None], axis=1),
+            jnp.sum(beside[1] * lows[2], axis=0, keepdims=True),
+        ]
+
     sums = jnp.concatenate(
-        [jnp.sum(first[...] * low[None], axis=1), jnp.sum(second[...] * low[None], axis=1)], axis=0
-    )
+        [*over(first, beside_first), *over(second, beside_second)], axis=0
+    )
+    gain = jnp.concatenate([gain, jnp.zeros((1, SLOT - channels), f32)], axis=1)
+    count = 2 * (frames + 2)
     block = jnp.concatenate(
         [
             dot_exact(sums, members(channels)),
             *[gain[:, k * LANES : (k + 1) * LANES] for k in range(SLOT // LANES)],
-            jnp.zeros((stats.shape[1] - 2 * frames - SLOT // LANES, LANES), f32),
+            jnp.zeros((stats.shape[1] - count - SLOT // LANES, LANES), f32),
         ],
         axis=0,
     )
@@ -326,45 +399,75 @@
     row = lax.broadcasted_iota(jnp.int32, (2 * half, half), 0)
     col = lax.broadcasted_iota(jnp.int32, (2 * half, half), 1)
     grow = jnp.where((row == 2 * col) | (row == 2 * col + 1), 1.0, 0.0).astype(bf16)
-    return dot(grow, grad_pooled[...])
+    return dot(grow, grad_pooled)
 
 
 def norm_back(
-    stats, grad_pooled, normed, slope, inv, grad, first, last, gain, *, cell_count
+    stats,
+    grad_pooled,
+    normed,
+    slope,
+    inv,
+    before,
+    after,
+    beside_slope,
+    beside_inv,
+    weight,
+    grad,
+    top,
+    bottom,
+    gain,
+    cells,
+    time,
+    sems,
+    *,
+    cell_count,
 ):
+    copy = (weight, time, sems.at[0])
+    start(copy)
     frames, rows, columns, channels = grad.shape
+    step = rows * columns
+    count = frames + 2
     total = jnp.sum(stats[...], axis=0)
     for k in range(gain.shape[1] // LANES):
-        gain[:, k * LANES : (k + 1) * LANES] = total[2 * frames + k : 2 * frames + k + 1]
-    means = spread(total[: 2 * frames] / cell_count, channels)
-    grown = unpooled(grad_pooled)
+        gain[:, k * LANES : (k + 1) * LANES] = total[2 * count + k : 2 * count + k + 1]
+    means = spread(total[: 2 * count] / cell_count, channels)
+    at = lax.axis_index("frame")
+    last = lax.axis_size("frame") - 1
+
+    def back(f, low, cells_normed, cells_slope, scale):
+        grown = unpooled(low)
+        grown = jnp.concatenate([grown] * rows, axis=0)
+        return scale * (
+            grown * cells_slope.astype(f32)
+            - means[f : f + 1]
+            - cells_normed.astype(f32) * means[count + f : count + f + 1]
+        )
+
+    early = back(0, grad_pooled[0], before[:step], beside_slope[0], beside_inv[0:1])
+    cells[:step] = jnp.where(at > 0, early, 0.0).astype(bf16)
     for f in range(frames):
-        for r in range(rows):
-            at = (f * rows + r) * columns
-            here = slice(at, at + columns)
-            value = inv[f : f + 1] * (
-                grown * slope[here]
-                - means[f : f + 1]
-                - normed[here] * means[frames + f : frames + f + 1]
-            )
-            value = value.astype(bf16)
-            grad[f, r] = value
-            if f == 0:
-                first[0, r] = value
-            if f == frames - 1:
-                last[0, r] = value
-
-
-def time_back_finish(part, before, after, weight, grad, top, bottom):
-    cells = time_edges(part, before, after, weight).astype(bf16).reshape(grad.shape)
-    grad[...] = cells
-    top[...] = cells[:, :1]
-    bottom[...] = cells[:, -1:]
+        here = slice(f * step, (f + 1) * step)
+        value = back(f + 1, grad_pooled[1], normed[here], slope[here], inv[f : f + 1])
+        cells[(f + 1) * step : (f + 2) * step] = value.astype(bf16)
+    late = back(
+        count - 1, grad_pooled[2], after[:step], beside_slope[1], beside_inv[1:2]
+    )
+    cells[(count - 1) * step :] = jnp.where(at < last, late, 0.0).astype(bf16)
+    size = frames * step
+    wait(copy)
+    sums = dot_nt(cells[:size], time[2])
+    sums += dot_nt(cells[step : step + size], time[1])
+    sums += dot_nt(cells[2 * step :], time[0])
+    spatial = sums.astype(bf16).reshape(grad.shape)
+    grad[...] = spatial
+    top[...] = spatial[:, :1]
+    bottom[...] = spatial[:, -1:]
 
 
 def space_back_finish(part, above, below, weight, grad_pooled, out):
-    grown = unpooled(grad_pooled) * (1.0 / 16.0)
-    for at, row in enumerate(space_edges(part, above, below, weight)):
+    grown = unpooled(grad_pooled[1]) * (1.0 / 16.0)
+    for at, row in enumerate(space_edges(part, above, below, weight, True)):
         row = row.reshape(out.shape[0], *out.shape[2:]) + grown[None]
         out[:, at] = row.astype(bf16)
 
@@ -391,23 +494,6 @@
         wait(copies[at])
         merged[:, at * width : (at + 1) * width] = dot(low[...], weights[at]).astype(bf16)
     token[...] = jnp.zeros_like(token)
-
-
-def turn(kernel_space, kernel_time, back_space, back_time, token, space, turned, time, sems):
-    channels = kernel_time.shape[-1]
-    inward = ((kernel_time, time, sems.at[0]), (kernel_space, space, sems.at[1]))
-    outward = [(turned.at[i], back_space.at[i], sems.at[2 + i]) for i in range(3)]
-    start(*inward)
-    wait(inward[0])
-    for i in range(3):
-        back_time[i] = time[2 - i].T
-    wait(inward[1])
-    for i in range(3):
-        for j in range(3):
-            turned[i, j * channels : (j + 1) * channels] = space[2 - i, 2 - j].T
-        start(outward[i])
-    token[...] = jnp.zeros_like(token)
-    wait(*outward)
 
 
 def coarse_finish(pooled, proj_in, blended, proj_out, out, token, low, high, sems):
@@ -454,6 +540,7 @@
     width = proj_query.shape[1]
     depth = cotangent.shape[-1]
     flat = shape((cells, channels), f32)
+    low_flat = shape((cells, channels), bf16)
     edge = shape((1, rows, columns, channels), bf16)
     band = shape(frames_in.shape, bf16)
     gain = norm_gain.reshape(1, channels)
@@ -464,10 +551,17 @@
     payload = shape((half, PAYLOAD, LANES), bf16)
     partial = shape((rows, frames * columns, channels), f32)
 
-    weight_space = kernel_space.reshape(3, 3 * channels, channels)
-
     above, below = neighbours(frames_in[:, -1:], frames_in[:, :1], "space")
-    part = call(space_own, partial, frames_in, weight_space)
+    space_here = shape(kernel_space.shape, bf16)
+    part, weight = call(
+        lambda *refs: space_own(*refs, back=False),
+        (partial, space_here),
+        frames_in,
+        kernel_space,
+        scratch=(pltpu.SemaphoreType.DMA((3,)),),
+        far=(1,),
+        pin=(0, 1),
+    )
     cot = cotangent.reshape(half, depth)
     token = shape((8, LANES), f32)
     low = pltpu.VMEM(proj_in.shape, bf16)
@@ -487,18 +581,26 @@
         part,
         above,
         below,
-        weight_space,
+        weight,
         after=(cot_in,),
     )
     before, after = neighbours(last, first, "frame")
-    part = call(time_own, flat, spatial, kernel_time)
+    part, weight = call(
+        time_own,
+        (flat, shape(kernel_time.shape, bf16)),
+        spatial,
+        kernel_time,
+        scratch=(pltpu.SemaphoreType.DMA((1,)),),
+        far=(1,),
+        pin=(0, 1),
+    )
     temporal, stats = call(
         lambda *refs: temporal_finish(*refs, frames=frames),
         (flat, shape((bands, 2 * frames, LANES), f32)),
         part,
         before,
         after,
-        kernel_time,
+        weight,
         pin=(0,),
     )
     merged, merged_token = call(
@@ -530,36 +632,21 @@
         scratch=packing,
         after=(merged_token,),
     )
-    back_space, back_time, turn_token = call(
-        turn,
-        (shape(weight_space.shape, bf16), shape(kernel_time.shape, bf16), token),
-        kernel_space,
-        kernel_time,
-        scratch=(
-            pltpu.VMEM(kernel_space.shape, bf16),
-            pltpu.VMEM(weight_space.shape, bf16),
-            pltpu.VMEM(kernel_time.shape, bf16),
-            pltpu.SemaphoreType.DMA((5,)),
-        ),
-        far=(0, 1),
-        far_out=(0,),
-        after=(pooled,),
-    )
     received = exchange(sent, "frame")
-    normed, slope, slope_sum, sway_sum, inv = call(
-        lambda *refs: slopes(*refs, dims=(frames, rows, columns), cell_count=cell_count),
-        (
-            flat,
-            flat,
-            shape((frames, half, channels), f32),
-            shape((frames, half, channels), f32),
-            shape((frames, channels), f32),
-        ),
+    dims = (frames, rows, columns)
+    pixels = shape((frames, half, channels), f32)
+    beside_pixels = shape((2, half, channels), f32)
+    edge_frame = shape((rows * columns + 16, channels), bf16)
+    normed, slope, slope_sum, sway_sum, inv, head, tail, slopes_token = call(
+        lambda *refs: slopes(*refs, dims=dims, cell_count=cell_count),
+        (low_flat, low_flat, pixels, pixels, shape((frames, channels), f32), edge_frame, edge_frame, token),
         temporal,
         stats,
         gain,
         pin=(0, 1, 2, 3, 4),
-    )
+        after=(pooled,),
+    )
+    before, after = neighbours(tail, head, "frame")
     sent = call(
         lambda *refs: coarse(*refs, heads=heads, channels=channels),
         payload,
@@ -567,25 +654,42 @@
         merged,
         frame_bias,
         scratch=(
-            *packing,
+            packing[0],
+            pltpu.VMEM((half, 4 * channels + width), f32),
+            packing[1],
             pltpu.VMEM(frame_bias.shape, f32),
             pltpu.SemaphoreType.DMA((1,)),
         ),
         far=(2,),
-        after=(turn_token,),
+        after=(slopes_token,),
+    )
+    beside_slope, beside_first, beside_second, beside_inv = call(
+        lambda *refs: slopes_beside(*refs, dims=dims),
+        (
+            shape((2, rows * columns, channels), bf16),
+            beside_pixels,
+            beside_pixels,
+            shape((2, channels), f32),
+        ),
+        before,
+        after,
+        gain,
+        pin=(0, 1, 2, 3),
     )
     received = exchange(sent, "frame")
     stats, grad_pooled, blended = call(
         totals,
         (
             shape((bands, 16, LANES), f32),
-            shape((half, channels), bf16),
+            shape((3, half, channels), bf16),
             shape((half, width), bf16),
         ),
         received,
         slope_sum,
         sway_sum,
-        scratch=packing,
+        beside_first,
+        beside_second,
+        scratch=(pltpu.VMEM((half, 4 * channels + width), f32), packing[1]),
     )
     coarse_out, coarse_token = call(
         coarse_finish,
@@ -599,27 +703,39 @@
         after=(stats,),
     )
     stats = exchange(stats, "space")
-    grad_temporal, first, last, grad_gain = call(
+    row_edge = shape((frames, 1, columns, channels), bf16)
+    grad_spatial, top, bottom, grad_gain = call(
         lambda *refs: norm_back(*refs, cell_count=cell_count),
-        (band, edge, edge, shape((1, SLOT), f32)),
+        (band, row_edge, row_edge, shape((1, SLOT), f32)),
         stats,
         grad_pooled,
         normed,
         slope,
         inv,
+        before,
+        after,
+        beside_slope,
+        beside_inv,
+        kernel_time,
+        scratch=(
+            pltpu.VMEM(((frames + 2) * rows * columns, channels), bf16),
+            pltpu.VMEM(kernel_time.shape, bf16),
+            pltpu.SemaphoreType.DMA((1,)),
+        ),
+        far=(9,),
         after=(coarse_token,),
     )
-    before, after = neighbours(last, first, "frame")
-    part = call(time_own, flat, grad_temporal, back_time)
-    row_edge = shape((frames, 1, columns, channels), bf16)
-    grad_spatial, top, bottom = call(
-        time_back_finish, (band, row_edge, row_edge), part, before, after, back_time
-    )
     above, below = neighbours(bottom, top, "space")
-    part = call(space_own, partial, grad_spatial, back_space)
-    grad_frames = call(
-        space_back_finish, band, part, above, below, back_space, grad_pooled
-    )
+    part, weight = call(
+        lambda *refs: space_own(*refs, back=True),
+        (partial, space_here),
+        grad_spatial,
+        kernel_space,
+        scratch=(pltpu.SemaphoreType.DMA((3,)),),
+        far=(1,),
+        pin=(0, 1),
+    )
+    grad_frames = call(space_back_finish, band, part, above, below, weight, grad_pooled)
     return coarse_out.reshape(cotangent.shape), grad_frames, grad_gain[0, :channels]
 
 

time: 108 us -> 102 us (0.944)
  waiting for transfers between devices: 29.3 us -> 22.1 us
  Pallas kernels: 30.7 us -> 33.3 us
    all_to_all x4, waiting for transfers between devices: 18.2 us -> 10.4 us  [exchange(): lax.all_to_all(payload, axis, split_axis=0, concat_axis=0, tiled=True)]
    pallas_call x17 -> x15, Pallas kernels: 30.7 us -> 33.3 us  [call(): pl.pallas_call(body, out_shape=shapes[0] if single else shapes, in_specs=...]
  transfers between devices with their start and end apart: 12 -> 12, of which waited for: 7 -> 7; matrix products, arithmetic and copies ran while one was open for 1% -> 1% of each run, Pallas kernels for 19% -> 21%
where the time goes in v3:
time: 102 us; the launch traced here: 101 us
  starting transfers between devices  40.3 us (40%)
  Pallas kernels  33.3 us (33%)
  waiting for transfers between devices  22.1 us (22%)
  local copies, waits for them, and re-layouts  4.93 us (5%)
    pallas_call x15, Pallas kernels, call(): pl.pallas_call(body, out_shape=shapes[0] if single else shapes, in_specs=...  33.3 us
    all_to_all x4, starting transfers between devices, exchange(): lax.all_to_all(payload, axis, split_axis=0, concat_axis=0, tiled=True)  23.8 us
    ppermute x4, starting transfers between devices, neighbours(): lax.ppermute(head, axis, [((i + 1) % count, i) for i in range(count)])  11.4 us
    all_to_all x4, waiting for transfers between devices, exchange(): lax.all_to_all(payload, axis, split_axis=0, concat_axis=0, tiled=True)  10.4 us
    ppermute x4, waiting for transfers between devices, neighbours(): lax.ppermute(head, axis, [((i + 1) % count, i) for i in range(count)])  5.96 us
    ppermute x4, waiting for transfers between devices, neighbours(): lax.ppermute(tail, axis, [(i, (i + 1) % count) for i in range(count)])  5.74 us
    ppermute x4, starting transfers between devices, neighbours(): lax.ppermute(tail, axis, [(i, (i + 1) % count) for i in range(count)])  5.15 us
    unnamed x20, local copies, waits for them, and re-layouts  3.23 us
  transfers between devices with their start and end apart: 12, of which 7 were waited for; matrix products, arithmetic and copies ran while one was open for 1% of the time, Pallas kernels for 21%

profile of v3, /device:TPU:26, one launch (start us, length us, event | category | flops | bytes accessed | tf_op | source)
XLA Modules:
  0.0 101.4 jit_solution(18328070188565202617)
XLA Ops:
  1.7 2.0 %collective-permute-start = (bf16[4,1,64,320]{3,2,1,0:T(8,128)(2,1)S(1)}, bf16[4,1,64,320]{3,2,1,0:T(8,128)(2,1)S(1)}, u32[]{:S(2)}, u32[]{:S(2)}) collective-permute-start(bf16[4,1,64,320]{3,2,1,0:T(8,128)(2,1)S(1)} %get-tuple-element.80), channel_id=1, source_target_pairs={{0,1},{1,2},{2,3},{3,4},{4,5},{5,6},{6,7},{7,0},{8,9},{9,10},{10,1... | collective-permute-start | bytes 491528 | tf_op jit(solution)/shard_map/ppermute | solution.py:512
  4.8 2.8 %shard_map.130 = (f32[2,256,320]{2,1,0:T(8,128)S(1)}, bf16[3,3,320,320]{3,2,1,0:T(8,128)(2,1)S(1)}) custom-call(bf16[4,2,64,320]{3,2,1,0:T(8,128)(2,1)S(1)} %copy-done, bf16[3,3,320,320]{3,2,1,0:T(8,128)(2,1)} %refs_1_.11), custom_call_target="tpu_custom_call" | custom-call | tf_op jit(solution)/shard_map/pallas_call | solution.py:53
  7.7 2.4 %shard_map.131 = (bf16[32,640]{1,0:T(8,128)(2,1)S(1)}, f32[32,320]{1,0:T(8,128)S(1)}) custom-call(bf16[32,1280]{1,0:T(8,128)(2,1)S(1)} %bitcast.2, bf16[320,1280]{1,0:T(8,128)(2,1)} %refs_1_.10, bf16[640,1280]{1,0:T(8,128)(2,1)} %refs_3_.3), custom_call_target="tpu_custom_call" | custom-call | tf_op jit(solution)/shard_map/pallas_call | solution.py:53
  10.1 2.2 %collective-permute-done.1.refs_2_ = bf16[4,1,64,320]{3,2,1,0:T(8,128)(2,1)S(1)} collective-permute-done((bf16[4,1,64,320]{3,2,1,0:T(8,128)(2,1)S(1)}, bf16[4,1,64,320]{3,2,1,0:T(8,128)(2,1)S(1)}, u32[]{:S(2)}, u32[]{:S(2)}) %collective-permute-start.1) | collective-permute-done | bytes 163872 | tf_op jit(solution)/shard_map/ppermute | solution.py:513
  13.1 6.1 %collective-permute-start.3 = (bf16[1,2,64,320]{3,2,1,0:T(8,128)(2,1)S(1)}, bf16[1,2,64,320]{3,2,1,0:T(8,128)(2,1)S(1)}, u32[]{:S(2)}, u32[]{:S(2)}) collective-permute-start(bf16[1,2,64,320]{3,2,1,0:T(8,128)(2,1)S(1)} %get-tuple-element.47), channel_id=1, source_target_pairs={{8,0},{16,8},{24,16},{32,24},{40,32},{48,40},{56,48},{64,56},{72,6... | collective-permute-start | bytes 245768 | tf_op jit(solution)/shard_map/ppermute | solution.py:513
  19.2 1.9 %shard_map.133 = (f32[512,320]{1,0:T(8,128)S(1)}, bf16[3,320,320]{2,1,0:T(8,128)(2,1)S(1)}) custom-call(bf16[4,2,64,320]{3,2,1,0:T(8,128)(2,1)S(1)} %get-tuple-element.44.refs_0_, bf16[3,320,320]{2,1,0:T(8,128)(2,1)} %refs_9_.1), custom_call_target="tpu_custom_call" | custom-call | tf_op jit(solution)/shard_map/pallas_call | solution.py:53
  22.6 6.7 %all-to-all-start = ((f32[8,8,128]{2,1,0:T(8,128)}), f32[8,8,128]{2,1,0:T(8,128)S(1)}, u32[]{:S(2)}, u32[]{:S(2)}) async-start(f32[8,8,128]{2,1,0:T(8,128)} %get-tuple-element.50.refs_4_), calls=%async_computation | async-start | bytes 65536 | tf_op jit(solution)/shard_map/all_to_all | solution.py:518
  29.2 5.4 %shard_map.135 = (bf16[320,1920]{1,0:T(8,128)(2,1)S(1)}, f32[8,128]{1,0:T(8,128)S(1)}) custom-call(bf16[320,1280]{1,0:T(8,128)(2,1)} %refs_1_.10, bf16[1280,640]{1,0:T(8,128)(2,1)} %refs_1_.9, bf16[1280,640]{1,0:T(8,128)(2,1)} %refs_2_.5, bf16[1280,640]{1,0:T(8,128)(2,1)} %refs_3_.2, f32[8,8,128]{2,1,0:T(8,128)} %get-tuple-element.50.refs_4_), custom_call_target="tpu_custom_call" | custom-call | tf_op jit(solution)/shard_map/pallas_call | solution.py:53
  34.6 1.8 %shard_map.136 = (bf16[32,16,128]{2,1,0:T(8,128)(2,1)}, bf16[32,320]{1,0:T(8,128)(2,1)S(1)}) custom-call(f32[512,320]{1,0:T(8,128)S(1)} %get-tuple-element.49.refs_0_, f32[8,8,128]{2,1,0:T(8,128)S(1)} %all-to-all-done.refs_1_, bf16[4,2,64,320]{3,2,1,0:T(8,128)(2,1)S(1)} %copy-done.1, f32[1,320]{1,0:T(1,128)S(1)} %reshape.16.refs_3_.refs_2_, ...), custom_call_target="tpu_custom_call" | custom-call | tf_op jit(solution)/shard_map/pallas_call | solution.py:53
  36.4 7.6 %all-to-all-start.1 = ((bf16[32,16,128]{2,1,0:T(8,128)(2,1)}), bf16[32,16,128]{2,1,0:T(8,128)(2,1)S(1)}, u32[]{:S(2)}, u32[]{:S(2)}) async-start(bf16[32,16,128]{2,1,0:T(8,128)(2,1)} %get-tuple-element.54), calls=%async_computation.1 | async-start | bytes 262144 | tf_op jit(solution)/shard_map/all_to_all | solution.py:518
  44.0 1.3 %shard_map.137 = (bf16[512,320]{1,0:T(8,128)(2,1)S(1)}, bf16[512,320]{1,0:T(8,128)(2,1)S(1)}, f32[4,32,320]{2,1,0:T(8,128)S(1)}, f32[4,32,320]{2,1,0:T(8,128)S(1...) custom-call(f32[512,320]{1,0:T(8,128)S(1)} %get-tuple-element.49.ref, ...), custom_call_target="tpu_custom_call" | custom-call | tf_op jit(solution)/shard_map/pallas_call | solution.py:53
  46.6 9.2 %all-to-all-done.1.refs_0_ = bf16[32,16,128]{2,1,0:T(8,128)(2,1)S(1)} async-done(((bf16[32,16,128]{2,1,0:T(8,128)(2,1)}), bf16[32,16,128]{2,1,0:T(8,128)(2,1)S(1)}, u32[]{:S(2)}, u32[]{:S(2)}) %all-to-all-start.1) | async-done | bytes 131104 | tf_op jit(solution)/shard_map/all_to_all | solution.py:518
  55.8 3.6 %shard_map.138 = bf16[32,16,128]{2,1,0:T(8,128)(2,1)} custom-call(bf16[32,16,128]{2,1,0:T(8,128)(2,1)S(1)} %all-to-all-done.1.refs_0_, bf16[320,1920]{1,0:T(8,128)(2,1)S(1)} %get-tuple-element.55.refs_1_, f32[10,32,32]{2,1,0:T(8,128)} %refs_2_.7, f32[8,128]{1,0:T(8,128)S(1)} %get-tuple-element.56.refs_3_), custom_call_target="tpu_custom_call" | custom-call | tf_op jit(solution)/shard_map/pallas_call | solution.py:53
  59.4 3.9 %all-to-all-start.2 = ((bf16[32,16,128]{2,1,0:T(8,128)(2,1)}), bf16[32,16,128]{2,1,0:T(8,128)(2,1)S(1)}, u32[]{:S(2)}, u32[]{:S(2)}) async-start(bf16[32,16,128]{2,1,0:T(8,128)(2,1)} %shard_map.138), calls=%async_computation.2 | async-start | bytes 262144 | tf_op jit(solution)/shard_map/all_to_all | solution.py:518
  63.5 5.2 %collective-permute-start.5 = (bf16[144,320]{1,0:T(8,128)(2,1)S(1)}, bf16[144,320]{1,0:T(8,128)(2,1)S(1)}, u32[]{:S(2)}, u32[]{:S(2)}) collective-permute-start(bf16[144,320]{1,0:T(8,128)(2,1)S(1)} %copy-done.6), channel_id=1, source_target_pairs={{8,0},{16,8},{24,16},{32,24},{40,32},{48,40},{56,48},{64,56},{72,6... | collective-permute-start | bytes 276488 | tf_op jit(solution)/shard_map/ppermute | solution.py:513
  68.7 5.0 %collective-permute-done.4.refs_0_.refs_5_ = bf16[144,320]{1,0:T(8,128)(2,1)S(1)} collective-permute-done((bf16[144,320]{1,0:T(8,128)(2,1)S(1)}, bf16[144,320]{1,0:T(8,128)(2,1)S(1)}, u32[]{:S(2)}, u32[]{:S(2)}) %collective-permute-start.4) | collective-permute-done | bytes 92192 | tf_op jit(solution)/shard_map/ppermute | solution.py:512
  74.2 1.2 %all-to-all-done.2.refs_0_ = bf16[32,16,128]{2,1,0:T(8,128)(2,1)S(1)} async-done(((bf16[32,16,128]{2,1,0:T(8,128)(2,1)}), bf16[32,16,128]{2,1,0:T(8,128)(2,1)S(1)}, u32[]{:S(2)}, u32[]{:S(2)}) %all-to-all-start.2) | async-done | bytes 131104 | tf_op jit(solution)/shard_map/all_to_all | solution.py:518
  77.3 5.7 %all-to-all-start.3 = ((f32[8,16,128]{2,1,0:T(8,128)}), f32[8,16,128]{2,1,0:T(8,128)S(1)}, u32[]{:S(2)}, u32[]{:S(2)}) async-start(f32[8,16,128]{2,1,0:T(8,128)} %get-tuple-element.64.refs_4_), calls=%async_computation.3 | async-start | bytes 131072 | tf_op jit(solution)/shard_map/all_to_all | solution.py:518
  83.0 3.6 %shard_map.141 = (bf16[32,1280]{1,0:T(8,128)(2,1)}, f32[8,128]{1,0:T(8,128)S(1)}) custom-call(bf16[32,320]{1,0:T(8,128)(2,1)S(1)} %get-tuple-element.53.refs_3_.refs_0_, bf16[320,1280]{1,0:T(8,128)(2,1)} %refs_1_.10, bf16[32,640]{1,0:T(8,128)(2,1)S(1)} %get-tuple-element.63.refs_2_, bf16[640,1280]{1,0:T(8,128)(2,1)} %refs_3_.3, ...), custom_call_target="tpu_custom_call" | custom-call | tf_op jit(solution)/shard_map/pallas_call | solution.py:53
  86.6 2.3 %shard_map.142 = (bf16[4,2,64,320]{3,2,1,0:T(8,128)(2,1)S(1)}, bf16[4,1,64,320]{3,2,1,0:T(8,128)(2,1)S(1)}, bf16[4,1,64,320]{3,2,1,0:T(8,128)(2,1)S(1)}, f32[1,384]{1,0:T(1,128)S(1)}) custom-call(f32[8,16,128]{2,1,0:T(8,128)S(1)} %all-to-all-done.3.refs_0_, bf16[3,32,320]{2,1,0:T(8,128)(2,1)S(1)} %get-tuple-element.66.refs_1_.refs_4_, ...), custom_call_target="tpu_custom_call" | custom-call | tf_op jit(solution)/shard_map/pallas_call | solution.py:53
  88.9 2.8 %collective-permute-start.6 = (bf16[4,1,64,320]{3,2,1,0:T(8,128)(2,1)S(1)}, bf16[4,1,64,320]{3,2,1,0:T(8,128)(2,1)S(1)}, u32[]{:S(2)}, u32[]{:S(2)}) collective-permute-start(bf16[4,1,64,320]{3,2,1,0:T(8,128)(2,1)S(1)} %get-tuple-element.75), channel_id=1, source_target_pairs={{0,1},{1,2},{2,3},{3,4},{4,5},{5,6},{6,7},{7,0},{8,9},{9,10},{10,1... | collective-permute-start | bytes 491528 | tf_op jit(solution)/shard_map/ppermute | solution.py:512
  91.7 3.2 %shard_map.143 = (f32[2,256,320]{2,1,0:T(8,128)S(1)}, bf16[3,3,320,320]{3,2,1,0:T(8,128)(2,1)S(1)}) custom-call(bf16[4,2,64,320]{3,2,1,0:T(8,128)(2,1)S(1)} %get-tuple-element.73.refs_0_, bf16[3,3,320,320]{3,2,1,0:T(8,128)(2,1)} %refs_1_.11), custom_call_target="tpu_custom_call" | custom-call | tf_op jit(solution)/shard_map/pallas_call | solution.py:53
  96.0 3.7 %collective-permute-done.7.refs_2_ = bf16[4,1,64,320]{3,2,1,0:T(8,128)(2,1)S(1)} collective-permute-done((bf16[4,1,64,320]{3,2,1,0:T(8,128)(2,1)S(1)}, bf16[4,1,64,320]{3,2,1,0:T(8,128)(2,1)S(1)}, u32[]{:S(2)}, u32[]{:S(2)}) %collective-permute-start.7) | collective-permute-done | bytes 163872 | tf_op jit(solution)/shard_map/ppermute | solution.py:513
  99.7 1.7 %shard_map.144 = bf16[4,2,64,320]{3,2,1,0:T(8,128)(2,1)} custom-call(f32[2,256,320]{2,1,0:T(8,128)S(1)} %get-tuple-element.74.refs_0_, bf16[4,1,64,320]{3,2,1,0:T(8,128)(2,1)S(1)} %collective-permute-done.6.refs_1_, bf16[4,1,64,320]{3,2,1,0:T(8,128)(2,1)S(1)} %collective-permute-done.7.refs_2_, bf16[3,3,320,320]{3,2,1,0:T(8,128)(2,1)S(1)} %get-tuple-element.77.refs_3_, ...), custom_call_target="tpu_custom_call" | custom-call | tf_op jit(solution)/shard_map/pallas_call | solution.py:53
  (38 shorter events, 9.5 us)
Async XLA Ops:
  0.6 7.1 %copy-start.4 = (bf16[1,1,32,1280]{3,2,1,0:T(8,128)(2,1)S(1)}, bf16[1,1,32,1280]{3,2,1,0:T(8,128)(2,1)}, u32[]{:S(2)}) copy-start(bf16[1,1,32,1280]{3,2,1,0:T(8,128)(2,1)} %param.21) | copy-start | bytes 245764
  1.7 8.3 %collective-permute-start = (bf16[4,1,64,320]{3,2,1,0:T(8,128)(2,1)S(1)}, bf16[4,1,64,320]{3,2,1,0:T(8,128)(2,1)S(1)}, u32[]{:S(2)}, u32[]{:S(2)}) collective-permute-start(bf16[4,1,64,320]{3,2,1,0:T(8,128)(2,1)S(1)} %get-tuple-element.80), channel_id=1, source_target_pairs={{0,1},{1,2},{2,3},{3,4},{4,5},{5,6},{6,7},{7,0},{8,9},{9,10},{10,1... | collective-permute-start | bytes 491528 | tf_op jit(solution)/shard_map/ppermute | solution.py:512
  3.8 8.6 %collective-permute-start.1 = (bf16[4,1,64,320]{3,2,1,0:T(8,128)(2,1)S(1)}, bf16[4,1,64,320]{3,2,1,0:T(8,128)(2,1)S(1)}, u32[]{:S(2)}, u32[]{:S(2)}) collective-permute-start(bf16[4,1,64,320]{3,2,1,0:T(8,128)(2,1)S(1)} %get-tuple-element.79), channel_id=1, source_target_pairs={{1,0},{2,1},{3,2},{4,3},{5,4},{6,5},{7,6},{0,7},{9,8},{10,9},{11,1... | collective-permute-start | bytes 491528 | tf_op jit(solution)/shard_map/ppermute | solution.py:513
  3.8 1.0 copy-start
  13.0 16.2 %copy-start.9 = (f32[320]{0:T(512)S(1)}, f32[320]{0:T(512)}, u32[]{:S(2)}) copy-start(f32[320]{0:T(512)} %param.14) | copy-start | bytes 3844
  13.1 8.4 %collective-permute-start.2 = (bf16[1,2,64,320]{3,2,1,0:T(8,128)(2,1)S(1)}, bf16[1,2,64,320]{3,2,1,0:T(8,128)(2,1)S(1)}, u32[]{:S(2)}, u32[]{:S(2)}) collective-permute-start(bf16[1,2,64,320]{3,2,1,0:T(8,128)(2,1)S(1)} %get-tuple-element.46), channel_id=1, source_target_pairs={{0,8},{8,16},{16,24},{24,32},{32,40},{40,48},{48,56},{56,64},{64,7... | collective-permute-start | bytes 245768 | tf_op jit(solution)/shard_map/ppermute | solution.py:512
  13.1 8.3 %collective-permute-start.3 = (bf16[1,2,64,320]{3,2,1,0:T(8,128)(2,1)S(1)}, bf16[1,2,64,320]{3,2,1,0:T(8,128)(2,1)S(1)}, u32[]{:S(2)}, u32[]{:S(2)}) collective-permute-start(bf16[1,2,64,320]{3,2,1,0:T(8,128)(2,1)S(1)} %get-tuple-element.47), channel_id=1, source_target_pairs={{8,0},{16,8},{24,16},{32,24},{40,32},{48,40},{56,48},{64,56},{72,6... | collective-permute-start | bytes 245768 | tf_op jit(solution)/shard_map/ppermute | solution.py:513
  22.6 12.0 %all-to-all-start = ((f32[8,8,128]{2,1,0:T(8,128)}), f32[8,8,128]{2,1,0:T(8,128)S(1)}, u32[]{:S(2)}, u32[]{:S(2)}) async-start(f32[8,8,128]{2,1,0:T(8,128)} %get-tuple-element.50.refs_4_), calls=%async_computation | async-start | bytes 65536 | tf_op jit(solution)/shard_map/all_to_all | solution.py:518
  29.2 5.4 %copy-start.1 = (bf16[4,2,64,320]{3,2,1,0:T(8,128)(2,1)S(1)}, bf16[4,2,64,320]{3,2,1,0:T(8,128)(2,1)}, u32[]{:S(2)}) copy-start(bf16[4,2,64,320]{3,2,1,0:T(8,128)(2,1)} %refs_2_.6) | copy-start | bytes 983044
  36.4 19.4 %all-to-all-start.1 = ((bf16[32,16,128]{2,1,0:T(8,128)(2,1)}), bf16[32,16,128]{2,1,0:T(8,128)(2,1)S(1)}, u32[]{:S(2)}, u32[]{:S(2)}) async-start(bf16[32,16,128]{2,1,0:T(8,128)(2,1)} %get-tuple-element.54), calls=%async_computation.1 | async-start | bytes 262144 | tf_op jit(solution)/shard_map/all_to_all | solution.py:518
  45.3 0.7 copy-start.5
  45.9 0.6 copy-start.7
  46.6 16.7 %copy-start.2 = (f32[4,32,320]{2,1,0:T(8,128)}, f32[4,32,320]{2,1,0:T(8,128)S(1)}, u32[]{:S(2)}) copy-start(f32[4,32,320]{2,1,0:T(8,128)S(1)} %get-tuple-element.58.refs_2_) | copy-start | bytes 491524
  55.8 7.5 %copy-start.8 = (bf16[144,320]{1,0:T(8,128)(2,1)S(1)}, bf16[144,320]{1,0:T(8,128)(2,1)}, u32[]{:S(2)}) copy-start(bf16[144,320]{1,0:T(8,128)(2,1)} %copy-done.7) | copy-start | bytes 276484
  55.8 7.7 %copy-start.6 = (bf16[144,320]{1,0:T(8,128)(2,1)S(1)}, bf16[144,320]{1,0:T(8,128)(2,1)}, u32[]{:S(2)}) copy-start(bf16[144,320]{1,0:T(8,128)(2,1)} %copy-done.5) | copy-start | bytes 276484
  59.4 16.0 %all-to-all-start.2 = ((bf16[32,16,128]{2,1,0:T(8,128)(2,1)}), bf16[32,16,128]{2,1,0:T(8,128)(2,1)S(1)}, u32[]{:S(2)}, u32[]{:S(2)}) async-start(bf16[32,16,128]{2,1,0:T(8,128)(2,1)} %shard_map.138), calls=%async_computation.2 | async-start | bytes 262144 | tf_op jit(solution)/shard_map/all_to_all | solution.py:518
  63.3 10.4 %collective-permute-start.4 = (bf16[144,320]{1,0:T(8,128)(2,1)S(1)}, bf16[144,320]{1,0:T(8,128)(2,1)S(1)}, u32[]{:S(2)}, u32[]{:S(2)}) collective-permute-start(bf16[144,320]{1,0:T(8,128)(2,1)S(1)} %copy-done.8), channel_id=1, source_target_pairs={{0,8},{8,16},{16,24},{24,32},{32,40},{40,48},{48,56},{56,64},{64,7... | collective-permute-start | bytes 276488 | tf_op jit(solution)/shard_map/ppermute | solution.py:512
  63.5 10.2 %collective-permute-start.5 = (bf16[144,320]{1,0:T(8,128)(2,1)S(1)}, bf16[144,320]{1,0:T(8,128)(2,1)S(1)}, u32[]{:S(2)}, u32[]{:S(2)}) collective-permute-start(bf16[144,320]{1,0:T(8,128)(2,1)S(1)} %copy-done.6), channel_id=1, source_target_pairs={{8,0},{16,8},{24,16},{32,24},{40,32},{48,40},{56,48},{64,56},{72,6... | collective-permute-start | bytes 276488 | tf_op jit(solution)/shard_map/ppermute | solution.py:513
  75.4 0.9 copy-start.3
  77.3 9.3 %all-to-all-start.3 = ((f32[8,16,128]{2,1,0:T(8,128)}), f32[8,16,128]{2,1,0:T(8,128)S(1)}, u32[]{:S(2)}, u32[]{:S(2)}) async-start(f32[8,16,128]{2,1,0:T(8,128)} %get-tuple-element.64.refs_4_), calls=%async_computation.3 | async-start | bytes 131072 | tf_op jit(solution)/shard_map/all_to_all | solution.py:518
  88.9 7.1 %collective-permute-start.6 = (bf16[4,1,64,320]{3,2,1,0:T(8,128)(2,1)S(1)}, bf16[4,1,64,320]{3,2,1,0:T(8,128)(2,1)S(1)}, u32[]{:S(2)}, u32[]{:S(2)}) collective-permute-start(bf16[4,1,64,320]{3,2,1,0:T(8,128)(2,1)S(1)} %get-tuple-element.75), channel_id=1, source_target_pairs={{0,1},{1,2},{2,3},{3,4},{4,5},{5,6},{6,7},{7,0},{8,9},{9,10},{10,1... | collective-permute-start | bytes 491528 | tf_op jit(solution)/shard_map/ppermute | solution.py:512
  91.7 8.0 %collective-permute-start.7 = (bf16[4,1,64,320]{3,2,1,0:T(8,128)(2,1)S(1)}, bf16[4,1,64,320]{3,2,1,0:T(8,128)(2,1)S(1)}, u32[]{:S(2)}, u32[]{:S(2)}) collective-permute-start(bf16[4,1,64,320]{3,2,1,0:T(8,128)(2,1)S(1)} %get-tuple-element.76), channel_id=1, source_target_pairs={{1,0},{2,1},{3,2},{4,3},{5,4},{6,5},{7,6},{0,7},{9,8},{10,9},{11,1... | collective-permute-start | bytes 491528 | tf_op jit(solution)/shard_map/ppermute | solution.py:513

commit v4 on v3

--- a/solution.py
+++ b/solution.py
@@ -91,9 +91,30 @@
     return dot(merged, weight[i].reshape(3 * channels, channels))
 
 
-def space_own(cells, weight_far, part, weight, sems, *, back):
+def rims(cells, outer_top, outer_bottom, inner_top, inner_bottom, sems):
+    last = cells.shape[0] - 1
+    copies = []
+    for row, (outer, inner) in ((0, (outer_top, inner_top)), (1, (outer_bottom, inner_bottom))):
+        copies += [
+            (cells.at[0, row], outer.at[0], sems.at[row, 0]),
+            (cells.at[last, row], outer.at[1], sems.at[row, 1]),
+            (cells.at[pl.ds(1, last - 1), row], inner, sems.at[row, 2]),
+        ]
+    start(*copies)
+    wait(*copies)
+
+
+def space_first(cells_far, weight_far, part, weight, cells, sems, cells_sem):
+    copy = (cells_far, cells, cells_sem.at[0])
+    start(copy)
+    space_own(cells, weight_far, part, weight, sems, back=False, copy=copy)
+
+
+def space_own(cells, weight_far, part, weight, sems, *, back, copy=None):
     copies = [(weight_far.at[i], weight.at[i], sems.at[i]) for i in range(3)]
     start(*copies)
+    if copy:
+        wait(copy)
     first = taps(cells[:, 0])
     second = taps(cells[:, 1])
     wait(*copies)
@@ -101,33 +122,50 @@
     part[1] = row_sum(second, weight, 1, back) + row_sum(first, weight, 0, back)
 
 
+def inside(above, below):
+    at = lax.axis_index("space")
+    last = lax.axis_size("space") - 1
+    return (
+        jnp.where(at > 0, above, jnp.zeros_like(above)),
+        jnp.where(at < last, below, jnp.zeros_like(below)),
+    )
+
+
 def space_edges(part, above, below, weight, back):
-    at = lax.axis_index("space")
-    count = lax.axis_size("space")
-    upper = jnp.where(at > 0, above[:, 0], jnp.zeros_like(above[:, 0]))
-    lower = jnp.where(at < count - 1, below[:, 0], jnp.zeros_like(below[:, 0]))
+    upper, lower = inside(above[:, 0], below[:, 0])
     return (
         part[0] + row_sum(taps(upper), weight, 0, back),
         part[1] + row_sum(taps(lower), weight, 2, back),
     )
 
 
-def spatial_finish(part, above, below, weight, spatial, first, last):
-    rows = space_edges(part, above, below, weight, False)
-    for at, row in enumerate(rows):
-        row = row.astype(bf16).reshape(spatial.shape[0], *spatial.shape[2:])
-        spatial[:, at] = row
-        first[0, at] = row[0]
-        last[0, at] = row[-1]
-
-
-def time_own(cells, weight_far, part, weight, sems):
-    copy = (weight_far, weight, sems.at[0])
+def spatial_outer(part, above, below, weight, first, last):
+    columns = above.shape[1]
+    for r, (i, rim) in enumerate(zip((0, 2), inside(above[...], below[...]))):
+        own = jnp.concatenate([part[r, :columns], part[r, -columns:]], axis=0)
+        row = (own + row_sum(taps(rim), weight, i, False)).astype(bf16)
+        first[0, r] = row[:columns]
+        last[0, r] = row[columns:]
+
+
+def spatial_inner(part, above, below, weight, first, last, time_far, sums, time, cells, sems):
+    copy = (time_far, time, sems.at[0])
     start(copy)
+    columns = above.shape[1]
+    frames, rows = cells.shape[:2]
+    for r, (i, rim) in enumerate(zip((0, 2), inside(above[...], below[...]))):
+        row = part[r, columns:-columns] + row_sum(taps(rim), weight, i, False)
+        cells[1 : frames - 1, r] = row.astype(bf16).reshape(frames - 2, *cells.shape[2:])
+    cells[0] = first[0]
+    cells[frames - 1] = last[0]
+    wait(copy)
+    time_own(cells, time, sums)
+
+
+def time_own(cells, weight, part):
     frames, _, _, channels = cells.shape
     flat = cells[...].reshape(-1, channels)
     step = flat.shape[0] // frames
-    wait(copy)
     part[...] = dot(flat, weight[1])
     part[step:] += dot(flat[:-step], weight[0])
     part[:-step] += dot(flat[step:], weight[2])
@@ -240,34 +278,17 @@
 
 
 def slopes(
-    temporal,
-    stats,
-    gain,
-    normed_out,
-    slope_out,
-    first,
-    second,
-    inv_out,
-    head,
-    tail,
-    token,
-    *,
-    dims,
-    cell_count,
+    temporal, stats, gain, normed_out, slope_out, inv_out, head, tail, token, *, frames, cell_count
 ):
-    frames, rows, columns = dims
     channels = temporal.shape[1]
-    step = rows * columns
+    step = temporal.shape[0] // frames
     mean, inv = moments(stats, frames, cell_count, channels)
     inv_out[...] = inv
     for f in range(frames):
         here = slice(f * step, (f + 1) * step)
         normed = (temporal[here] - mean[f : f + 1]) * inv[f : f + 1]
-        slope = slope_of(normed, gain)
         normed_out[here] = normed.astype(bf16)
-        slope_out[here] = slope.astype(bf16)
-        first[f] = by_pixel(slope, rows, columns)
-        second[f] = by_pixel(slope * normed, rows, columns)
+        slope_out[here] = slope_of(normed, gain)
     for f, edge in ((0, head), (frames - 1, tail)):
         high = inv[f : f + 1].astype(bf16).astype(f32)
         edge[:step] = normed_out[f * step : (f + 1) * step]
@@ -279,27 +300,15 @@
 
 
 def slope_of(normed, gain):
-    return activation(normed, gain[...])[1] * gain[...] * (1.0 / 16.0)
-
-
-def by_pixel(cells, rows, columns):
-    total = cells[:columns]
-    for r in range(1, rows):
-        total = total + cells[r * columns : (r + 1) * columns]
-    return dot_exact(pairs(columns // 2, 1.0), total)
-
-
-def slopes_beside(before, after, gain, slope_out, first, second, inv_out, *, dims):
-    _, rows, columns = dims
-    step = rows * columns
+    return (activation(normed, gain[...])[1] * gain[...] * (1.0 / 16.0)).astype(bf16)
+
+
+def slopes_beside(before, after, gain, slope_out, inv_out):
+    step = slope_out.shape[1]
     for at, edge in enumerate((before, after)):
-        normed = edge[:step].astype(f32)
         extra = edge[step:].astype(f32)
         inv_out[at : at + 1] = extra[0:1] + extra[1:2]
-        slope = slope_of(normed, gain)
-        slope_out[at] = slope.astype(bf16)
-        first[at] = by_pixel(slope, rows, columns)
-        second[at] = by_pixel(slope * normed, rows, columns)
+        slope_out[at] = slope_of(edge[:step].astype(f32), gain)
 
 
 def coarse(payload, merged, bias, out, wide, out_wide, chunks, bias_here, sems, *, heads, channels):
@@ -361,31 +370,46 @@
 
 
 def totals(
-    payload, first, second, beside_first, beside_second, stats, grad_pooled, blended, wide, chunks
+    payload,
+    normed,
+    slope,
+    before,
+    after,
+    beside_slope,
+    stats,
+    grad_pooled,
+    blended,
+    wide,
+    chunks,
+    *,
+    frames,
 ):
     unpack(payload, wide, chunks)
-    frames, _, channels = first.shape
-    lows = [wide[:, i * channels : (i + 1) * channels] for i in range(3)]
-    for i, low in enumerate(lows):
-        grad_pooled[i] = low.astype(bf16)
+    channels = normed.shape[1]
+    step = normed.shape[0] // frames
+    for i in range(3):
+        grad_pooled[i] = wide[:, i * channels : (i + 1) * channels].astype(bf16)
     blended[...] = wide[:, 4 * channels : 4 * channels + blended.shape[1]].astype(bf16)
     gain = jnp.sum(wide[:, 3 * channels : 4 * channels], axis=0, keepdims=True)
-
-    def over(own, beside):
-        return [
-            jnp.sum(beside[0] * lows[0], axis=0, keepdims=True),
-            jnp.sum(own[...] * lows[1][None], axis=1),
-            jnp.sum(beside[1] * lows[2], axis=0, keepdims=True),
-        ]
-
-    sums = jnp.concatenate(
-        [*over(first, beside_first), *over(second, beside_second)], axis=0
-    )
+    grown = [unpooled(grad_pooled[i]) for i in range(3)]
+    firsts, seconds = [], []
+
+    def add(low, cells_slope, cells_normed):
+        repeated = jnp.concatenate([low] * (step // low.shape[0]), axis=0)
+        first = repeated * cells_slope.astype(f32)
+        firsts.append(jnp.sum(first, axis=0, keepdims=True))
+        seconds.append(jnp.sum(first * cells_normed.astype(f32), axis=0, keepdims=True))
+
+    add(grown[0], beside_slope[0], before[:step])
+    for f in range(frames):
+        here = slice(f * step, (f + 1) * step)
+        add(grown[1], slope[here], normed[here])
+    add(grown[2], beside_slope[1], after[:step])
     gain = jnp.concatenate([gain, jnp.zeros((1, SLOT - channels), f32)], axis=1)
     count = 2 * (frames + 2)
     block = jnp.concatenate(
         [
-            dot_exact(sums, members(channels)),
+            dot_exact(jnp.concatenate(firsts + seconds, axis=0), members(channels)),
             *[gain[:, k * LANES : (k + 1) * LANES] for k in range(SLOT // LANES)],
             jnp.zeros((stats.shape[1] - count - SLOT // LANES, LANES), f32),
         ],
@@ -481,19 +505,29 @@
     grad_heads[...] = dot_nt(cot[...], high[...]).astype(bf16)
 
 
-def merge(proj_in, proj_query, proj_key, proj_value, merged, token, low, weights, sems):
-    width = proj_query.shape[1]
-    first = (proj_in, low, sems.at[3])
-    copies = [
-        (weight, weights.at[at], sems.at[at])
-        for at, weight in enumerate((proj_query, proj_key, proj_value))
-    ]
-    start(first, *copies)
+def merge(proj_in, proj_query, proj_key, proj_value, merged, low, weights, sems):
+    depth, width = proj_query.shape
+    parts = weights.shape[0]
+    piece = depth // parts
+    first = (proj_in, low, sems.at[0, 3])
+    start(first)
+    copies = []
+    for k in range(parts):
+        here = pl.ds(k * piece, piece)
+        copies.append(
+            [
+                (weight.at[here], weights.at[k, :, pl.ds(at * width, width)], sems.at[k, at])
+                for at, weight in enumerate((proj_query, proj_key, proj_value))
+            ]
+        )
+        start(*copies[k])
     wait(first)
-    for at in range(3):
-        wait(copies[at])
-        merged[:, at * width : (at + 1) * width] = dot(low[...], weights[at]).astype(bf16)
-    token[...] = jnp.zeros_like(token)
+    sums = None
+    for k in range(parts):
+        wait(*copies[k])
+        product = dot(low[:, k * piece : (k + 1) * piece], weights[k])
+        sums = product if sums is None else sums + product
+    merged[...] = sums.astype(bf16)
 
 
 def coarse_finish(pooled, proj_in, blended, proj_out, out, token, low, high, sems):
@@ -551,16 +585,58 @@
     payload = shape((half, PAYLOAD, LANES), bf16)
     partial = shape((rows, frames * columns, channels), f32)
 
-    above, below = neighbours(frames_in[:, -1:], frames_in[:, :1], "space")
+    outer = shape((2, columns, channels), bf16)
+    inner = shape((frames - 2, columns, channels), bf16)
+    outer_top, outer_bottom, inner_top, inner_bottom = call(
+        rims,
+        (outer, outer, inner, inner),
+        frames_in,
+        scratch=(pltpu.SemaphoreType.DMA((2, 3)),),
+        far=(0,),
+        pin=(0, 1, 2, 3),
+    )
+    outer_above, outer_below = neighbours(outer_bottom, outer_top, "space")
+    inner_above, inner_below = neighbours(inner_bottom, inner_top, "space")
     space_here = shape(kernel_space.shape, bf16)
     part, weight = call(
-        lambda *refs: space_own(*refs, back=False),
+        space_first,
         (partial, space_here),
         frames_in,
         kernel_space,
-        scratch=(pltpu.SemaphoreType.DMA((3,)),),
-        far=(1,),
+        scratch=(
+            pltpu.VMEM(frames_in.shape, bf16),
+            pltpu.SemaphoreType.DMA((3,)),
+            pltpu.SemaphoreType.DMA((1,)),
+        ),
+        far=(0, 1),
         pin=(0, 1),
+    )
+    first, last = call(
+        spatial_outer, (edge, edge), part, outer_above, outer_below, weight, pin=(0, 1)
+    )
+    before, after = neighbours(last, first, "frame")
+    part, weight = call(
+        spatial_inner,
+        (flat, shape(kernel_time.shape, bf16)),
+        part,
+        inner_above,
+        inner_below,
+        weight,
+        first,
+        last,
+        kernel_time,
+        scratch=(pltpu.VMEM(frames_in.shape, bf16), pltpu.SemaphoreType.DMA((1,))),
+        far=(6,),
+        pin=(0, 1),
+    )
+    temporal, stats = call(
+        lambda *refs: temporal_finish(*refs, frames=frames),
+        (flat, shape((bands, 2 * frames, LANES), f32)),
+        part,
+        before,
+        after,
+        weight,
+        pin=(0,),
     )
     cot = cotangent.reshape(half, depth)
     token = shape((8, LANES), f32)
@@ -574,49 +650,6 @@
         proj_out,
         scratch=(low, high, pltpu.SemaphoreType.DMA((2,))),
         far=(1, 2),
-    )
-    spatial, first, last = call(
-        spatial_finish,
-        (band, edge, edge),
-        part,
-        above,
-        below,
-        weight,
-        after=(cot_in,),
-    )
-    before, after = neighbours(last, first, "frame")
-    part, weight = call(
-        time_own,
-        (flat, shape(kernel_time.shape, bf16)),
-        spatial,
-        kernel_time,
-        scratch=(pltpu.SemaphoreType.DMA((1,)),),
-        far=(1,),
-        pin=(0, 1),
-    )
-    temporal, stats = call(
-        lambda *refs: temporal_finish(*refs, frames=frames),
-        (flat, shape((bands, 2 * frames, LANES), f32)),
-        part,
-        before,
-        after,
-        weight,
-        pin=(0,),
-    )
-    merged, merged_token = call(
-        merge,
-        (shape((channels, 3 * width), bf16), token),
-        proj_in,
-        proj_query,
-        proj_key,
-        proj_value,
-        scratch=(
-            low,
-            pltpu.VMEM((3, *proj_query.shape), bf16),
-            pltpu.SemaphoreType.DMA((4,)),
-        ),
-        far=(0, 1, 2, 3),
-        pin=(0,),
         after=(stats,),
     )
     stats = exchange(stats, "space")
@@ -630,21 +663,33 @@
         grad_heads,
         cot_in,
         scratch=packing,
-        after=(merged_token,),
     )
     received = exchange(sent, "frame")
-    dims = (frames, rows, columns)
-    pixels = shape((frames, half, channels), f32)
-    beside_pixels = shape((2, half, channels), f32)
     edge_frame = shape((rows * columns + 16, channels), bf16)
-    normed, slope, slope_sum, sway_sum, inv, head, tail, slopes_token = call(
-        lambda *refs: slopes(*refs, dims=dims, cell_count=cell_count),
-        (low_flat, low_flat, pixels, pixels, shape((frames, channels), f32), edge_frame, edge_frame, token),
+    normed, slope, inv, head, tail, slopes_token = call(
+        lambda *refs: slopes(*refs, frames=frames, cell_count=cell_count),
+        (low_flat, low_flat, shape((frames, channels), f32), edge_frame, edge_frame, token),
         temporal,
         stats,
         gain,
-        pin=(0, 1, 2, 3, 4),
+        pin=(0, 1, 2),
         after=(pooled,),
+    )
+    merged = call(
+        merge,
+        shape((channels, 3 * width), bf16),
+        proj_in,
+        proj_query,
+        proj_key,
+        proj_value,
+        scratch=(
+            low,
+            pltpu.VMEM((5, depth // 5, 3 * width), bf16),
+            pltpu.SemaphoreType.DMA((5, 4)),
+        ),
+        far=(0, 1, 2, 3),
+        pin=(0,),
+        after=(slopes_token,),
     )
     before, after = neighbours(tail, head, "frame")
     sent = call(
@@ -661,34 +706,29 @@
             pltpu.SemaphoreType.DMA((1,)),
         ),
         far=(2,),
-        after=(slopes_token,),
-    )
-    beside_slope, beside_first, beside_second, beside_inv = call(
-        lambda *refs: slopes_beside(*refs, dims=dims),
-        (
-            shape((2, rows * columns, channels), bf16),
-            beside_pixels,
-            beside_pixels,
-            shape((2, channels), f32),
-        ),
+    )
+    beside_slope, beside_inv = call(
+        slopes_beside,
+        (shape((2, rows * columns, channels), bf16), shape((2, channels), f32)),
         before,
         after,
         gain,
-        pin=(0, 1, 2, 3),
+        pin=(0, 1),
     )
     received = exchange(sent, "frame")
     stats, grad_pooled, blended = call(
-        totals,
+        lambda *refs: totals(*refs, frames=frames),
         (
             shape((bands, 16, LANES), f32),
             shape((3, half, channels), bf16),
             shape((half, width), bf16),
         ),
         received,
-        slope_sum,
-        sway_sum,
-        beside_first,
-        beside_second,
+        normed,
+        slope,
+        before,
+        after,
+        beside_slope,
         scratch=(pltpu.VMEM((half, 4 * channels + width), f32), packing[1]),
     )
     coarse_out, coarse_token = call(

time: 102 us -> 98.7 us (0.968)
  starting transfers between devices: 40.3 us -> 44.7 us
  local copies, waits for them, and re-layouts: 4.93 us -> 0.61 us
  waiting for transfers between devices: 22.1 us -> 18.5 us
    ppermute x4 -> x5, starting transfers between devices: 5.15 us -> 9.18 us  [neighbours(): lax.ppermute(tail, axis, [(i, (i + 1) % count) for i in range(count)])]
    unnamed x20 -> x6, local copies, waits for them, and re-layouts: 3.23 us -> 0.02 us
    ppermute x4 -> x5, waiting for transfers between devices: 5.96 us -> 3.82 us  [neighbours(): lax.ppermute(head, axis, [((i + 1) % count, i) for i in range(count)])]
    all_to_all x4, waiting for transfers between devices: 10.4 us -> 8.58 us  [exchange(): lax.all_to_all(payload, axis, split_axis=0, concat_axis=0, tiled=True)]
    slice x1 -> x0, local copies, waits for them, and re-layouts: 1.1 us -> none  [local(): above, below = neighbours(frames_in[:, -1:], frames_in[:, :1], 'space')]
    all_to_all x4, starting transfers between devices: 23.8 us -> 24.9 us  [exchange(): lax.all_to_all(payload, axis, split_axis=0, concat_axis=0, tiled=True)]
    ppermute x4 -> x5, starting transfers between devices: 11.4 us -> 10.6 us  [neighbours(): lax.ppermute(head, axis, [((i + 1) % count, i) for i in range(count)])]
    ppermute x4 -> x5, waiting for transfers between devices: 5.74 us -> 6.1 us  [neighbours(): lax.ppermute(tail, axis, [(i, (i + 1) % count) for i in range(count)])]
  transfers between devices with their start and end apart: 12 -> 14, of which waited for: 7 -> 8; matrix products, arithmetic and copies ran while one was open for 1% -> 1% of each run, Pallas kernels for 21% -> 21%
where the time goes in v4:
time: 98.7 us; the launch traced here: 98 us
  starting transfers between devices  44.7 us (45%)
  Pallas kernels  33.4 us (34%)
  waiting for transfers between devices  18.5 us (19%)
    pallas_call x16, Pallas kernels, call(): pl.pallas_call(body, out_shape=shapes[0] if single else shapes, in_specs=...  33.4 us
    all_to_all x4, starting transfers between devices, exchange(): lax.all_to_all(payload, axis, split_axis=0, concat_axis=0, tiled=True)  24.9 us
    ppermute x5, starting transfers between devices, neighbours(): lax.ppermute(head, axis, [((i + 1) % count, i) for i in range(count)])  10.6 us
    ppermute x5, starting transfers between devices, neighbours(): lax.ppermute(tail, axis, [(i, (i + 1) % count) for i in range(count)])  9.18 us
    all_to_all x4, waiting for transfers between devices, exchange(): lax.all_to_all(payload, axis, split_axis=0, concat_axis=0, tiled=True)  8.58 us
    ppermute x5, waiting for transfers between devices, neighbours(): lax.ppermute(tail, axis, [(i, (i + 1) % count) for i in range(count)])  6.1 us
    ppermute x5, waiting for transfers between devices, neighbours(): lax.ppermute(head, axis, [((i + 1) % count, i) for i in range(count)])  3.82 us
  transfers between devices with their start and end apart: 14, of which 8 were waited for; matrix products, arithmetic and copies ran while one was open for 1% of the time, Pallas kernels for 21%

profile of v4, /device:TPU:26, one launch (start us, length us, event | category | flops | bytes accessed | tf_op | source)
XLA Modules:
  0.0 98.0 jit_solution(12198308425831605591)
XLA Ops:
  1.7 2.0 %collective-permute-start.2 = (bf16[2,64,320]{2,1,0:T(8,128)(2,1)S(1)}, bf16[2,64,320]{2,1,0:T(8,128)(2,1)S(1)}, u32[]{:S(2)}, u32[]{:S(2)}) collective-permute-start(bf16[2,64,320]{2,1,0:T(8,128)(2,1)S(1)} %get-tuple-element.42), channel_id=1, source_target_pairs={{0,1},{1,2},{2,3},{3,4},{4,5},{5,6},{6,7},{7,0},{8,9},{9,10},{10,1... | collective-permute-start | bytes 245768 | tf_op jit(solution)/shard_map/ppermute | solution.py:546
  3.8 4.0 %collective-permute-start = (bf16[2,64,320]{2,1,0:T(8,128)(2,1)S(1)}, bf16[2,64,320]{2,1,0:T(8,128)(2,1)S(1)}, u32[]{:S(2)}, u32[]{:S(2)}) collective-permute-start(bf16[2,64,320]{2,1,0:T(8,128)(2,1)S(1)} %get-tuple-element.39), channel_id=1, source_target_pairs={{0,1},{1,2},{2,3},{3,4},{4,5},{5,6},{6,7},{7,0},{8,9},{9,10},{10,1... | collective-permute-start | bytes 245768 | tf_op jit(solution)/shard_map/ppermute | solution.py:546
  7.9 3.0 %shard_map.130 = (f32[2,256,320]{2,1,0:T(8,128)S(1)}, bf16[3,3,320,320]{3,2,1,0:T(8,128)(2,1)S(1)}) custom-call(bf16[4,2,64,320]{3,2,1,0:T(8,128)(2,1)} %refs_2_.5, bf16[3,3,320,320]{3,2,1,0:T(8,128)(2,1)} %refs_1_.9), custom_call_target="tpu_custom_call" | custom-call | tf_op jit(solution)/shard_map/pallas_call | solution.py:53
  11.6 5.3 %collective-permute-start.5 = (bf16[1,2,64,320]{3,2,1,0:T(8,128)(2,1)S(1)}, bf16[1,2,64,320]{3,2,1,0:T(8,128)(2,1)S(1)}, u32[]{:S(2)}, u32[]{:S(2)}) collective-permute-start(bf16[1,2,64,320]{3,2,1,0:T(8,128)(2,1)S(1)} %get-tuple-element.44.refs_4_), channel_id=1, source_target_pairs={{8,0},{16,8},{24,16},{32,24},{40,32},{48,40},{56,48},{64,56},{72,6... | collective-permute-start | bytes 245768 | tf_op jit(solution)/shard_map/ppermute | solution.py:547
  16.9 1.9 %shard_map.133 = (f32[512,320]{1,0:T(8,128)S(1)}, bf16[3,320,320]{2,1,0:T(8,128)(2,1)S(1)}) custom-call(f32[2,256,320]{2,1,0:T(8,128)S(1)} %get-tuple-element.38.refs_0_, bf16[2,64,320]{2,1,0:T(8,128)(2,1)S(1)} %collective-permute-done.refs_1_, bf16[2,64,320]{2,1,0:T(8,128)(2,1)S(1)} %collective-permute-done.1.refs_2_, ...), custom_call_target="tpu_custom_call" | custom-call | tf_op jit(solution)/shard_map/pallas_call | solution.py:53
  20.4 7.5 %all-to-all-start = ((f32[8,8,128]{2,1,0:T(8,128)}), f32[8,8,128]{2,1,0:T(8,128)S(1)}, u32[]{:S(2)}, u32[]{:S(2)}) async-start(f32[8,8,128]{2,1,0:T(8,128)} %get-tuple-element.49.refs_3_), calls=%async_computation | async-start | bytes 65536 | tf_op jit(solution)/shard_map/all_to_all | solution.py:552
  27.8 3.1 %shard_map.135 = (bf16[32,640]{1,0:T(8,128)(2,1)S(1)}, f32[32,320]{1,0:T(8,128)S(1)}) custom-call(bf16[32,1280]{1,0:T(8,128)(2,1)S(1)} %bitcast.2, bf16[320,1280]{1,0:T(8,128)(2,1)} %refs_1_.8, bf16[640,1280]{1,0:T(8,128)(2,1)} %refs_3_.3, f32[8,8,128]{2,1,0:T(8,128)} %get-tuple-element.49.refs_3_), custom_call_target="tpu_custom_call" | custom-call | tf_op jit(solution)/shard_map/pallas_call | solution.py:53
  31.2 1.8 %shard_map.136 = (bf16[32,16,128]{2,1,0:T(8,128)(2,1)}, bf16[32,320]{1,0:T(8,128)(2,1)S(1)}) custom-call(f32[512,320]{1,0:T(8,128)S(1)} %get-tuple-element.48.refs_0_, f32[8,8,128]{2,1,0:T(8,128)S(1)} %all-to-all-done.refs_1_, bf16[4,2,64,320]{3,2,1,0:T(8,128)(2,1)S(1)} %copy-done, f32[1,320]{1,0:T(1,128)S(1)} %reshape.15.refs_3_.refs_2_, ...), custom_call_target="tpu_custom_call" | custom-call | tf_op jit(solution)/shard_map/pallas_call | solution.py:53
  33.0 6.7 %all-to-all-start.1 = ((bf16[32,16,128]{2,1,0:T(8,128)(2,1)}), bf16[32,16,128]{2,1,0:T(8,128)(2,1)S(1)}, u32[]{:S(2)}, u32[]{:S(2)}) async-start(bf16[32,16,128]{2,1,0:T(8,128)(2,1)} %get-tuple-element.53), calls=%async_computation.1 | async-start | bytes 262144 | tf_op jit(solution)/shard_map/all_to_all | solution.py:552
  40.5 4.1 %shard_map.138.refs_1_ = bf16[320,1920]{1,0:T(8,128)(2,1)S(1)} custom-call(bf16[320,1280]{1,0:T(8,128)(2,1)} %refs_1_.8, bf16[1280,640]{1,0:T(8,128)(2,1)} %refs_1_.7, bf16[1280,640]{1,0:T(8,128)(2,1)} %refs_2_.6, bf16[1280,640]{1,0:T(8,128)(2,1)} %refs_3_.2, f32[8,128]{1,0:T(8,128)S(1)} %get-tuple-element.54.refs_4_), custom_call_target="tpu_custom_call" | custom-call | tf_op jit(solution)/shard_map/pallas_call | solution.py:53
  44.7 6.8 %all-to-all-done.1.refs_0_ = bf16[32,16,128]{2,1,0:T(8,128)(2,1)S(1)} async-done(((bf16[32,16,128]{2,1,0:T(8,128)(2,1)}), bf16[32,16,128]{2,1,0:T(8,128)(2,1)S(1)}, u32[]{:S(2)}, u32[]{:S(2)}) %all-to-all-start.1) | async-done | bytes 131104 | tf_op jit(solution)/shard_map/all_to_all | solution.py:552
  51.5 3.6 %shard_map.139 = bf16[32,16,128]{2,1,0:T(8,128)(2,1)} custom-call(bf16[32,16,128]{2,1,0:T(8,128)(2,1)S(1)} %all-to-all-done.1.refs_0_, bf16[320,1920]{1,0:T(8,128)(2,1)S(1)} %shard_map.138.refs_1_, f32[10,32,32]{2,1,0:T(8,128)} %refs_2_.7), custom_call_target="tpu_custom_call" | custom-call | tf_op jit(solution)/shard_map/pallas_call | solution.py:53
  55.1 3.9 %all-to-all-start.2 = ((bf16[32,16,128]{2,1,0:T(8,128)(2,1)}), bf16[32,16,128]{2,1,0:T(8,128)(2,1)S(1)}, u32[]{:S(2)}, u32[]{:S(2)}) async-start(bf16[32,16,128]{2,1,0:T(8,128)(2,1)} %shard_map.139), calls=%async_computation.2 | async-start | bytes 262144 | tf_op jit(solution)/shard_map/all_to_all | solution.py:552
  59.2 5.2 %collective-permute-start.7 = (bf16[144,320]{1,0:T(8,128)(2,1)S(1)}, bf16[144,320]{1,0:T(8,128)(2,1)S(1)}, u32[]{:S(2)}, u32[]{:S(2)}) collective-permute-start(bf16[144,320]{1,0:T(8,128)(2,1)S(1)} %get-tuple-element.58), channel_id=1, source_target_pairs={{8,0},{16,8},{24,16},{32,24},{40,32},{48,40},{56,48},{64,56},{72,6... | collective-permute-start | bytes 276488 | tf_op jit(solution)/shard_map/ppermute | solution.py:547
  64.4 5.0 %collective-permute-done.6.refs_0_.refs_3_.refs_5_ = bf16[144,320]{1,0:T(8,128)(2,1)S(1)} collective-permute-done((bf16[144,320]{1,0:T(8,128)(2,1)S(1)}, bf16[144,320]{1,0:T(8,128)(2,1)S(1)}, u32[]{:S(2)}, u32[]{:S(2)}) %collective-permute-start.6) | collective-permute-done | bytes 92192 | tf_op jit(solution)/shard_map/ppermute | solution.py:546
  69.6 1.6 %all-to-all-done.2.refs_0_ = bf16[32,16,128]{2,1,0:T(8,128)(2,1)S(1)} async-done(((bf16[32,16,128]{2,1,0:T(8,128)(2,1)}), bf16[32,16,128]{2,1,0:T(8,128)(2,1)S(1)}, u32[]{:S(2)}, u32[]{:S(2)}) %all-to-all-start.2) | async-done | bytes 131104 | tf_op jit(solution)/shard_map/all_to_all | solution.py:552
  71.1 1.4 %shard_map.141 = (f32[8,16,128]{2,1,0:T(8,128)}, bf16[3,32,320]{2,1,0:T(8,128)(2,1)S(1)}, bf16[32,640]{1,0:T(8,128)(2,1)S(1)}) custom-call(bf16[32,16,128]{2,1,0:T(8,128)(2,1)S(1)} %all-to-all-done.2.refs_0_, bf16[512,320]{1,0:T(8,128)(2,1)S(1)} %get-tuple-element.55.refs_1_.refs_2_, bf16[512,320]{1,0:T(8,128)(2,1)S(1)} %get-tuple-element.56.refs_2_.refs_3_, ...), custom_call_target="tpu_custom_call" | custom-call | tf_op jit(solution)/shard_map/pallas_call | solution.py:53
  72.5 6.8 %all-to-all-start.3 = ((f32[8,16,128]{2,1,0:T(8,128)}), f32[8,16,128]{2,1,0:T(8,128)S(1)}, u32[]{:S(2)}, u32[]{:S(2)}) async-start(f32[8,16,128]{2,1,0:T(8,128)} %get-tuple-element.61.refs_4_), calls=%async_computation.3 | async-start | bytes 131072 | tf_op jit(solution)/shard_map/all_to_all | solution.py:552
  79.3 3.6 %shard_map.142 = (bf16[32,1280]{1,0:T(8,128)(2,1)}, f32[8,128]{1,0:T(8,128)S(1)}) custom-call(bf16[32,320]{1,0:T(8,128)(2,1)S(1)} %get-tuple-element.52.refs_3_.refs_0_, bf16[320,1280]{1,0:T(8,128)(2,1)} %refs_1_.8, bf16[32,640]{1,0:T(8,128)(2,1)S(1)} %get-tuple-element.60.refs_2_, bf16[640,1280]{1,0:T(8,128)(2,1)} %refs_3_.3, ...), custom_call_target="tpu_custom_call" | custom-call | tf_op jit(solution)/shard_map/pallas_call | solution.py:53
  82.9 2.3 %shard_map.143 = (bf16[4,2,64,320]{3,2,1,0:T(8,128)(2,1)S(1)}, bf16[4,1,64,320]{3,2,1,0:T(8,128)(2,1)S(1)}, bf16[4,1,64,320]{3,2,1,0:T(8,128)(2,1)S(1)}, f32[1,384]{1,0:T(1,128)S(1)}) custom-call(f32[8,16,128]{2,1,0:T(8,128)S(1)} %all-to-all-done.3.refs_0_, bf16[3,32,320]{2,1,0:T(8,128)(2,1)S(1)} %get-tuple-element.63.refs_1_.refs_4_, ...), custom_call_target="tpu_custom_call" | custom-call | tf_op jit(solution)/shard_map/pallas_call | solution.py:53
  85.2 2.8 %collective-permute-start.8 = (bf16[4,1,64,320]{3,2,1,0:T(8,128)(2,1)S(1)}, bf16[4,1,64,320]{3,2,1,0:T(8,128)(2,1)S(1)}, u32[]{:S(2)}, u32[]{:S(2)}) collective-permute-start(bf16[4,1,64,320]{3,2,1,0:T(8,128)(2,1)S(1)} %get-tuple-element.69), channel_id=1, source_target_pairs={{0,1},{1,2},{2,3},{3,4},{4,5},{5,6},{6,7},{7,0},{8,9},{9,10},{10,1... | collective-permute-start | bytes 491528 | tf_op jit(solution)/shard_map/ppermute | solution.py:546
  88.0 3.2 %shard_map.144 = (f32[2,256,320]{2,1,0:T(8,128)S(1)}, bf16[3,3,320,320]{3,2,1,0:T(8,128)(2,1)S(1)}) custom-call(bf16[4,2,64,320]{3,2,1,0:T(8,128)(2,1)S(1)} %get-tuple-element.67.refs_0_, bf16[3,3,320,320]{3,2,1,0:T(8,128)(2,1)} %refs_1_.9), custom_call_target="tpu_custom_call" | custom-call | tf_op jit(solution)/shard_map/pallas_call | solution.py:53
  92.6 3.7 %collective-permute-done.9.refs_2_ = bf16[4,1,64,320]{3,2,1,0:T(8,128)(2,1)S(1)} collective-permute-done((bf16[4,1,64,320]{3,2,1,0:T(8,128)(2,1)S(1)}, bf16[4,1,64,320]{3,2,1,0:T(8,128)(2,1)S(1)}, u32[]{:S(2)}, u32[]{:S(2)}) %collective-permute-start.9) | collective-permute-done | bytes 163872 | tf_op jit(solution)/shard_map/ppermute | solution.py:547
  96.3 1.7 %shard_map.145 = bf16[4,2,64,320]{3,2,1,0:T(8,128)(2,1)} custom-call(f32[2,256,320]{2,1,0:T(8,128)S(1)} %get-tuple-element.68.refs_0_, bf16[4,1,64,320]{3,2,1,0:T(8,128)(2,1)S(1)} %collective-permute-done.8.refs_1_, bf16[4,1,64,320]{3,2,1,0:T(8,128)(2,1)S(1)} %collective-permute-done.9.refs_2_, bf16[3,3,320,320]{3,2,1,0:T(8,128)(2,1)S(1)} %get-tuple-element.71.refs_3_, ...), custom_call_target="tpu_custom_call" | custom-call | tf_op jit(solution)/shard_map/pallas_call | solution.py:53
  (28 shorter events, 6.1 us)
Async XLA Ops:
  1.7 9.1 %collective-permute-start.2 = (bf16[2,64,320]{2,1,0:T(8,128)(2,1)S(1)}, bf16[2,64,320]{2,1,0:T(8,128)(2,1)S(1)}, u32[]{:S(2)}, u32[]{:S(2)}) collective-permute-start(bf16[2,64,320]{2,1,0:T(8,128)(2,1)S(1)} %get-tuple-element.42), channel_id=1, source_target_pairs={{0,1},{1,2},{2,3},{3,4},{4,5},{5,6},{6,7},{7,0},{8,9},{9,10},{10,1... | collective-permute-start | bytes 245768 | tf_op jit(solution)/shard_map/ppermute | solution.py:546
  3.7 7.2 %collective-permute-start.3 = (bf16[2,64,320]{2,1,0:T(8,128)(2,1)S(1)}, bf16[2,64,320]{2,1,0:T(8,128)(2,1)S(1)}, u32[]{:S(2)}, u32[]{:S(2)}) collective-permute-start(bf16[2,64,320]{2,1,0:T(8,128)(2,1)S(1)} %get-tuple-element.43), channel_id=1, source_target_pairs={{1,0},{2,1},{3,2},{4,3},{5,4},{6,5},{7,6},{0,7},{9,8},{10,9},{11,1... | collective-permute-start | bytes 245768 | tf_op jit(solution)/shard_map/ppermute | solution.py:547
  3.8 13.1 %collective-permute-start = (bf16[2,64,320]{2,1,0:T(8,128)(2,1)S(1)}, bf16[2,64,320]{2,1,0:T(8,128)(2,1)S(1)}, u32[]{:S(2)}, u32[]{:S(2)}) collective-permute-start(bf16[2,64,320]{2,1,0:T(8,128)(2,1)S(1)} %get-tuple-element.39), channel_id=1, source_target_pairs={{0,1},{1,2},{2,3},{3,4},{4,5},{5,6},{6,7},{7,0},{8,9},{9,10},{10,1... | collective-permute-start | bytes 245768 | tf_op jit(solution)/shard_map/ppermute | solution.py:546
  7.9 9.0 %collective-permute-start.1 = (bf16[2,64,320]{2,1,0:T(8,128)(2,1)S(1)}, bf16[2,64,320]{2,1,0:T(8,128)(2,1)S(1)}, u32[]{:S(2)}, u32[]{:S(2)}) collective-permute-start(bf16[2,64,320]{2,1,0:T(8,128)(2,1)S(1)} %get-tuple-element.40), channel_id=1, source_target_pairs={{1,0},{2,1},{3,2},{4,3},{5,4},{6,5},{7,6},{0,7},{9,8},{10,9},{11,1... | collective-permute-start | bytes 245768 | tf_op jit(solution)/shard_map/ppermute | solution.py:547
  11.5 7.7 %collective-permute-start.4 = (bf16[1,2,64,320]{3,2,1,0:T(8,128)(2,1)S(1)}, bf16[1,2,64,320]{3,2,1,0:T(8,128)(2,1)S(1)}, u32[]{:S(2)}, u32[]{:S(2)}) collective-permute-start(bf16[1,2,64,320]{3,2,1,0:T(8,128)(2,1)S(1)} %get-tuple-element.45.refs_5_), channel_id=1, source_target_pairs={{0,8},{8,16},{16,24},{24,32},{32,40},{40,48},{48,56},{56,64},{64,7... | collective-permute-start | bytes 245768 | tf_op jit(solution)/shard_map/ppermute | solution.py:546
  11.6 7.6 %collective-permute-start.5 = (bf16[1,2,64,320]{3,2,1,0:T(8,128)(2,1)S(1)}, bf16[1,2,64,320]{3,2,1,0:T(8,128)(2,1)S(1)}, u32[]{:S(2)}, u32[]{:S(2)}) collective-permute-start(bf16[1,2,64,320]{3,2,1,0:T(8,128)(2,1)S(1)} %get-tuple-element.44.refs_4_), channel_id=1, source_target_pairs={{8,0},{16,8},{24,16},{32,24},{40,32},{48,40},{56,48},{64,56},{72,6... | collective-permute-start | bytes 245768 | tf_op jit(solution)/shard_map/ppermute | solution.py:547
  18.8 9.0 %copy-start.2 = (f32[320]{0:T(512)S(1)}, f32[320]{0:T(512)}, u32[]{:S(2)}) copy-start(f32[320]{0:T(512)} %param.14) | copy-start | bytes 3844
  18.8 9.0 %copy-start.1 = (bf16[1,1,32,1280]{3,2,1,0:T(8,128)(2,1)S(1)}, bf16[1,1,32,1280]{3,2,1,0:T(8,128)(2,1)}, u32[]{:S(2)}) copy-start(bf16[1,1,32,1280]{3,2,1,0:T(8,128)(2,1)} %param.21) | copy-start | bytes 245764
  20.4 10.8 %copy-start = (bf16[4,2,64,320]{3,2,1,0:T(8,128)(2,1)S(1)}, bf16[4,2,64,320]{3,2,1,0:T(8,128)(2,1)}, u32[]{:S(2)}) copy-start(bf16[4,2,64,320]{3,2,1,0:T(8,128)(2,1)} %refs_2_.5) | copy-start | bytes 983044
  20.4 10.8 %all-to-all-start = ((f32[8,8,128]{2,1,0:T(8,128)}), f32[8,8,128]{2,1,0:T(8,128)S(1)}, u32[]{:S(2)}, u32[]{:S(2)}) async-start(f32[8,8,128]{2,1,0:T(8,128)} %get-tuple-element.49.refs_3_), calls=%async_computation | async-start | bytes 65536 | tf_op jit(solution)/shard_map/all_to_all | solution.py:552
  33.0 18.5 %all-to-all-start.1 = ((bf16[32,16,128]{2,1,0:T(8,128)(2,1)}), bf16[32,16,128]{2,1,0:T(8,128)(2,1)S(1)}, u32[]{:S(2)}, u32[]{:S(2)}) async-start(bf16[32,16,128]{2,1,0:T(8,128)(2,1)} %get-tuple-element.53), calls=%async_computation.1 | async-start | bytes 262144 | tf_op jit(solution)/shard_map/all_to_all | solution.py:552
  55.1 16.0 %all-to-all-start.2 = ((bf16[32,16,128]{2,1,0:T(8,128)(2,1)}), bf16[32,16,128]{2,1,0:T(8,128)(2,1)S(1)}, u32[]{:S(2)}, u32[]{:S(2)}) async-start(bf16[32,16,128]{2,1,0:T(8,128)(2,1)} %shard_map.139), calls=%async_computation.2 | async-start | bytes 262144 | tf_op jit(solution)/shard_map/all_to_all | solution.py:552
  59.0 10.4 %collective-permute-start.6 = (bf16[144,320]{1,0:T(8,128)(2,1)S(1)}, bf16[144,320]{1,0:T(8,128)(2,1)S(1)}, u32[]{:S(2)}, u32[]{:S(2)}) collective-permute-start(bf16[144,320]{1,0:T(8,128)(2,1)S(1)} %get-tuple-element.57), channel_id=1, source_target_pairs={{0,8},{8,16},{16,24},{24,32},{32,40},{40,48},{48,56},{56,64},{64,7... | collective-permute-start | bytes 276488 | tf_op jit(solution)/shard_map/ppermute | solution.py:546
  59.2 10.2 %collective-permute-start.7 = (bf16[144,320]{1,0:T(8,128)(2,1)S(1)}, bf16[144,320]{1,0:T(8,128)(2,1)S(1)}, u32[]{:S(2)}, u32[]{:S(2)}) collective-permute-start(bf16[144,320]{1,0:T(8,128)(2,1)S(1)} %get-tuple-element.58), channel_id=1, source_target_pairs={{8,0},{16,8},{24,16},{32,24},{40,32},{48,40},{56,48},{64,56},{72,6... | collective-permute-start | bytes 276488 | tf_op jit(solution)/shard_map/ppermute | solution.py:547
  72.5 10.4 %all-to-all-start.3 = ((f32[8,16,128]{2,1,0:T(8,128)}), f32[8,16,128]{2,1,0:T(8,128)S(1)}, u32[]{:S(2)}, u32[]{:S(2)}) async-start(f32[8,16,128]{2,1,0:T(8,128)} %get-tuple-element.61.refs_4_), calls=%async_computation.3 | async-start | bytes 131072 | tf_op jit(solution)/shard_map/all_to_all | solution.py:552
  85.2 7.4 %collective-permute-start.8 = (bf16[4,1,64,320]{3,2,1,0:T(8,128)(2,1)S(1)}, bf16[4,1,64,320]{3,2,1,0:T(8,128)(2,1)S(1)}, u32[]{:S(2)}, u32[]{:S(2)}) collective-permute-start(bf16[4,1,64,320]{3,2,1,0:T(8,128)(2,1)S(1)} %get-tuple-element.69), channel_id=1, source_target_pairs={{0,1},{1,2},{2,3},{3,4},{4,5},{5,6},{6,7},{7,0},{8,9},{9,10},{10,1... | collective-permute-start | bytes 491528 | tf_op jit(solution)/shard_map/ppermute | solution.py:546
  88.0 8.3 %collective-permute-start.9 = (bf16[4,1,64,320]{3,2,1,0:T(8,128)(2,1)S(1)}, bf16[4,1,64,320]{3,2,1,0:T(8,128)(2,1)S(1)}, u32[]{:S(2)}, u32[]{:S(2)}) collective-permute-start(bf16[4,1,64,320]{3,2,1,0:T(8,128)(2,1)S(1)} %get-tuple-element.70), channel_id=1, source_target_pairs={{1,0},{2,1},{3,2},{4,3},{5,4},{6,5},{7,6},{0,7},{9,8},{10,9},{11,1... | collective-permute-start | bytes 491528 | tf_op jit(solution)/shard_map/ppermute | solution.py:547

commit v5 on v4

--- a/solution.py
+++ b/solution.py
@@ -27,11 +27,28 @@
     return lax.dot_general(a, b, (((0,), (0,)), ((), ())), preferred_element_type=f32)
 
 
-def dot_exact(a, b):
-    return jnp.dot(a, b, preferred_element_type=f32, precision=lax.Precision.HIGHEST)
-
-
-def call(kernel, out_shape, *operands, scratch=(), limit=12, far=(), far_out=(), pin=(), after=()):
+def thirds(a):
+    high = a.astype(bf16)
+    rest = a - high.astype(f32)
+    mid = rest.astype(bf16)
+    return high, mid, (rest - mid.astype(f32)).astype(bf16)
+
+
+def dot_sums(a, chosen):
+    rows = a.shape[0]
+    pad = -rows % 16
+    if pad:
+        a = jnp.concatenate([a, jnp.zeros((pad, a.shape[1]), f32)], axis=0)
+    out = dot(jnp.concatenate(thirds(a), axis=0), chosen)
+    step = rows + pad
+    return (out[:step] + out[step : 2 * step] + out[2 * step :])[:rows]
+
+
+def dot_chosen(chosen, b):
+    return dot(jnp.concatenate([chosen] * 3, axis=1), jnp.concatenate(thirds(b), axis=0))
+
+
+def call(kernel, out_shape, *operands, scratch=(), limit=12, far=(), far_out=(), pin=(), alias=None, after=()):
     count = len(operands)
     near = pl.BlockSpec(memory_space=pltpu.VMEM)
     away = pl.BlockSpec(memory_space=pltpu.HBM)
@@ -56,6 +73,7 @@
         in_specs=[away if i in far else near for i in range(count)] + [near] * len(after),
         out_specs=out_specs[0] if single else out_specs,
         scratch_shapes=list(scratch),
+        input_output_aliases=alias or {},
         compiler_params=pltpu.CompilerParams(vmem_limit_bytes=limit * 1024 * 1024),
     )(*operands, *after)
 
@@ -131,14 +149,6 @@
     )
 
 
-def space_edges(part, above, below, weight, back):
-    upper, lower = inside(above[:, 0], below[:, 0])
-    return (
-        part[0] + row_sum(taps(upper), weight, 0, back),
-        part[1] + row_sum(taps(lower), weight, 2, back),
-    )
-
-
 def spatial_outer(part, above, below, weight, first, last):
     columns = above.shape[1]
     for r, (i, rim) in enumerate(zip((0, 2), inside(above[...], below[...]))):
@@ -148,7 +158,7 @@
         last[0, r] = row[columns:]
 
 
-def spatial_inner(part, above, below, weight, first, last, time_far, sums, time, cells, sems):
+def spatial_inner(part, above, below, weight, first, last, time_far, sums, time, moments_out, cells, sems):
     copy = (time_far, time, sems.at[0])
     start(copy)
     columns = above.shape[1]
@@ -160,6 +170,15 @@
     cells[frames - 1] = last[0]
     wait(copy)
     time_own(cells, time, sums)
+    step = sums.shape[0] // frames
+    for f in range(1, frames - 1):
+        frame_sums(sums[f * step : (f + 1) * step], f, moments_out)
+
+
+def frame_sums(cells, f, out):
+    frames = out.shape[0] // 2
+    out[f : f + 1] = jnp.sum(cells, axis=0, keepdims=True)
+    out[frames + f : frames + f + 1] = jnp.sum(cells * cells, axis=0, keepdims=True)
 
 
 def time_own(cells, weight, part):
@@ -171,65 +190,68 @@
     part[:-step] += dot(flat[step:], weight[2])
 
 
-def time_edges(part, before, after, weight):
-    at = lax.axis_index("frame")
-    count = lax.axis_size("frame")
-    channels = before.shape[-1]
-    earlier = jnp.where(at > 0, before[...], jnp.zeros_like(before[...])).reshape(-1, channels)
-    later = jnp.where(at < count - 1, after[...], jnp.zeros_like(after[...])).reshape(-1, channels)
-    step = earlier.shape[0]
-    head = part[:step] + dot(earlier, weight[0])
-    tail = part[-step:] + dot(later, weight[2])
-    return jnp.concatenate([head, part[step:-step], tail], axis=0)
-
-
 def members(channels):
     channel = lax.broadcasted_iota(jnp.int32, (channels, LANES), 0)
     group = lax.broadcasted_iota(jnp.int32, (channels, LANES), 1)
+    return belong(channel, group, channels)
+
+
+def belong(channel, group, channels):
     width = channels // GROUPS
-    return jnp.where((channel >= group * width) & (channel < (group + 1) * width), 1.0, 0.0)
+    inside_group = (channel >= group * width) & (channel < (group + 1) * width)
+    return jnp.where(inside_group, 1.0, 0.0).astype(bf16)
 
 
 def spread(statistic, channels):
-    return lax.dot_general(
-        statistic,
-        members(channels),
-        (((1,), (1,)), ((), ())),
-        preferred_element_type=f32,
-        precision=lax.Precision.HIGHEST,
-    )
-
-
-def temporal_finish(part, before, after, weight, temporal, stats, *, frames):
-    cells = time_edges(part, before, after, weight)
-    temporal[...] = cells
-    step = cells.shape[0] // frames
-    split = cells.reshape(frames, step, cells.shape[1])
-    sums = jnp.concatenate([jnp.sum(split, axis=1), jnp.sum(split * split, axis=1)], axis=0)
-    stats[...] = jnp.broadcast_to(dot_exact(sums, members(cells.shape[1]))[None], stats.shape)
+    group = lax.broadcasted_iota(jnp.int32, (LANES, channels), 0)
+    channel = lax.broadcasted_iota(jnp.int32, (LANES, channels), 1)
+    return dot_sums(statistic, belong(channel, group, channels))
+
+
+def temporal_finish(part, before, after, weight, inner, temporal, stats, sums):
+    at = lax.axis_index("frame")
+    ends = lax.axis_size("frame") - 1
+    channels = before.shape[-1]
+    frames = inner.shape[0] // 2
+    step = part.shape[0] // frames
+    sums[...] = inner[...]
+    for f, edge, i, there in ((0, before, 0, at > 0), (frames - 1, after, 2, at < ends)):
+        here = slice(f * step, (f + 1) * step)
+        halo = jnp.where(there, edge[...], jnp.zeros_like(edge[...])).reshape(-1, channels)
+        cells = part[here] + dot(halo, weight[i])
+        temporal[here] = cells
+        frame_sums(cells, f, sums)
+    stats[...] = jnp.broadcast_to(dot_sums(sums[...], members(channels))[None], stats.shape)
 
 
 def moments(stats, frames, cell_count, channels):
     total = jnp.sum(stats[...], axis=0)
     mean = total[:frames] / cell_count
     inv = lax.rsqrt(total[frames:] / cell_count - mean * mean + 1e-05)
-    return spread(mean, channels), spread(inv, channels)
-
-
-def pairs(half, value):
+    both = spread(jnp.concatenate([mean, inv], axis=0), channels)
+    return both[:frames], both[frames:]
+
+
+def pairs(half):
     row = lax.broadcasted_iota(jnp.int32, (half, 2 * half), 0)
     col = lax.broadcasted_iota(jnp.int32, (half, 2 * half), 1)
-    return jnp.where((col == 2 * row) | (col == 2 * row + 1), value, 0.0)
+    return jnp.where((col == 2 * row) | (col == 2 * row + 1), 1.0, 0.0).astype(bf16)
 
 
 def pack(parts, wide, chunks, payload):
-    wide[...] = jnp.zeros_like(wide)
-    chunks[...] = jnp.zeros_like(chunks)
-    for at, part in parts:
-        wide[:, at : at + part.shape[1]] = part.astype(f32)
-    pixels = wide.shape[0]
-    for k in range(wide.shape[1] // LANES):
-        chunks[pl.ds(k, pixels, stride=PAYLOAD), :] = wide[:, k * LANES : (k + 1) * LANES]
+    used = 0
+    for part in parts:
+        wide[:, used : used + part.shape[1]] = part.astype(f32)
+        used += part.shape[1]
+    pixels, width = wide.shape
+    if used < width:
+        wide[:, used:] = jnp.zeros((pixels, width - used), f32)
+    for k in range(PAYLOAD):
+        here = pl.ds(k, pixels, stride=PAYLOAD)
+        if k * LANES < width:
+            chunks[here, :] = wide[:, k * LANES : (k + 1) * LANES]
+        else:
+            chunks[here, :] = jnp.zeros((pixels, LANES), f32)
     payload[...] = chunks[...].reshape(payload.shape).astype(bf16)
 
 
@@ -261,20 +283,11 @@
             silu, slope = activation(normed, gain[...])
             fine += cells[f, r].astype(f32) + silu
             sway += slope * normed
-    select = pairs(half, 1.0 / 16.0)
-    low = dot_exact(select, fine).astype(bf16)
+    select = pairs(half)
+    low = (dot_chosen(select, fine) * (1.0 / 16.0)).astype(bf16)
     pooled[...] = low
-    pack(
-        [
-            (0, low),
-            (SLOT, dot_exact(select, sway)),
-            (2 * SLOT, cot_in[...]),
-            (3 * SLOT, grad_heads[...]),
-        ],
-        wide,
-        chunks,
-        payload,
-    )
+    sway = dot_chosen(select, sway) * (1.0 / 16.0)
+    pack([low, sway, grad_heads[...], cot_in[...]], wide, chunks, payload)
 
 
 def slopes(
@@ -311,57 +324,60 @@
         slope_out[at] = slope_of(edge[:step].astype(f32), gain)
 
 
-def coarse(payload, merged, bias, out, wide, out_wide, chunks, bias_here, sems, *, heads, channels):
-    bias_copy = (bias, bias_here, sems.at[0])
-    start(bias_copy)
+def coarse(payload, merged, bias, out, wide, out_wide, chunks, placed, *, heads, channels):
     unpack(payload, wide, chunks)
     frames = payload.shape[0]
     pooled = wide[:, :channels].astype(bf16)
-    sway = wide[:, SLOT : SLOT + channels]
-    cot_in = wide[:, 2 * SLOT : 2 * SLOT + channels]
+    sway = wide[:, channels : 2 * channels]
     width = merged.shape[1] // 3
-    grad_heads = wide[:, 3 * SLOT : 3 * SLOT + width].astype(bf16)
+    grad_heads = wide[:, 2 * channels : 2 * channels + width].astype(bf16)
+    cot_in = wide[:, 2 * channels + width : 3 * channels + width]
     depth = width // heads
     factor = 1.0 / math.sqrt(depth)
     qkv = dot(pooled, merged[...]).astype(bf16)
     queries, keys, values = (qkv[:, i * width : (i + 1) * width] for i in range(3))
-    row = lax.broadcasted_iota(jnp.int32, (heads, frames, width), 0)
-    lane = lax.broadcasted_iota(jnp.int32, (heads, frames, width), 2)
-    own = (lane >= row * depth) & (lane < (row + 1) * depth)
-
-    def by_head(matrix):
-        tiled = jnp.broadcast_to(matrix.astype(f32)[None], (heads, frames, width))
-        return jnp.where(own, tiled, 0.0).astype(bf16).reshape(heads * frames, width)
+
+    def by_head(matrix, place):
+        place[...] = jnp.zeros_like(place)
+        for h in range(heads):
+            lanes = slice(h * depth, (h + 1) * depth)
+            place[h * frames : (h + 1) * frames, lanes] = matrix[:, lanes]
+        return place[...]
 
     def gather(product):
-        return jnp.sum(jnp.where(own, product.reshape(heads, frames, width), 0.0), axis=0)
-
-    query_rows = by_head(queries)
-    grad_rows = by_head(grad_heads)
-    wait(bias_copy)
-    scores = dot_nt(query_rows, keys) * factor + bias_here[...].reshape(heads * frames, frames)
-    expd = jnp.exp(scores - jnp.max(scores, axis=1, keepdims=True))
-    weights = expd / jnp.sum(expd, axis=1, keepdims=True)
+        return jnp.concatenate(
+            [
+                product[h * frames : (h + 1) * frames, h * depth : (h + 1) * depth]
+                for h in range(heads)
+            ],
+            axis=1,
+        )
+
+    grad_rows = by_head(grad_heads, placed.at[1])
+    query_rows = by_head(queries, placed.at[0])
+    scores = dot_nt(keys, query_rows) * factor + bias[...]
+    expd = jnp.exp(scores - jnp.max(scores, axis=0, keepdims=True))
+    weights = expd / jnp.sum(expd, axis=0, keepdims=True)
     rounded = weights.astype(bf16)
-    blended = gather(dot(rounded, values))
-    grad_weights = dot_nt(grad_rows, values)
-    grad_values = dot_tn(rounded, grad_rows)
-    centre = jnp.sum(weights * grad_weights, axis=1, keepdims=True)
+    grad_weights = dot_nt(values, grad_rows)
+    centre = jnp.sum(weights * grad_weights, axis=0, keepdims=True)
     grad_scores = (weights * (grad_weights - centre)).astype(bf16)
-    grad_queries = gather(dot(grad_scores, keys)) * factor
-    grad_keys = dot_tn(grad_scores, query_rows) * factor
+    blended = gather(dot_tn(rounded, values))
+    grad_values = dot(rounded, grad_rows)
+    grad_queries = gather(dot_tn(grad_scores, keys)) * factor
+    grad_keys = dot(grad_scores, query_rows) * factor
     grads = jnp.concatenate([grad_queries, grad_keys, grad_values], axis=1).astype(bf16)
-    grad_pooled = (cot_in + dot_nt(grads, merged[...])).astype(bf16)
+    grad_pooled = (cot_in + dot_nt(merged[...], grads).T).astype(bf16)
     low = grad_pooled.astype(f32)
     gain = jnp.sum(low * sway, axis=0, keepdims=True)
     outside = jnp.zeros((1, channels), f32)
     pack(
         [
-            (0, jnp.concatenate([outside, low[:-1]], axis=0)),
-            (channels, low),
-            (2 * channels, jnp.concatenate([low[1:], outside], axis=0)),
-            (3 * channels, jnp.broadcast_to(gain, (frames, channels))),
-            (4 * channels, blended),
+            jnp.concatenate([outside, low[:-1]], axis=0),
+            low,
+            jnp.concatenate([low[1:], outside], axis=0),
+            jnp.broadcast_to(gain, (frames, channels)),
+            blended,
         ],
         out_wide,
         chunks,
@@ -409,7 +425,7 @@
     count = 2 * (frames + 2)
     block = jnp.concatenate(
         [
-            dot_exact(jnp.concatenate(firsts + seconds, axis=0), members(channels)),
+            dot_sums(jnp.concatenate(firsts + seconds, axis=0), members(channels)),
             *[gain[:, k * LANES : (k + 1) * LANES] for k in range(SLOT // LANES)],
             jnp.zeros((stats.shape[1] - count - SLOT // LANES, LANES), f32),
         ],
@@ -426,7 +442,27 @@
     return dot(grow, grad_pooled)
 
 
-def norm_back(
+def norm_back(grown, cells_normed, cells_slope, scale, first, second):
+    repeated = jnp.concatenate([grown] * (cells_slope.shape[0] // grown.shape[0]), axis=0)
+    return scale * (
+        repeated * cells_slope.astype(f32) - first - cells_normed.astype(f32) * second
+    )
+
+
+def time_back(cells, time, grad, top, bottom):
+    frames, rows, columns, channels = grad.shape
+    step = rows * columns
+    size = frames * step
+    sums = dot_nt(cells[:size], time[2])
+    sums += dot_nt(cells[step : step + size], time[1])
+    sums += dot_nt(cells[2 * step : 2 * step + size], time[0])
+    spatial = sums.astype(bf16).reshape(grad.shape)
+    grad[...] = spatial
+    top[...] = spatial[:, 0]
+    bottom[...] = spatial[:, -1]
+
+
+def frames_back(
     stats,
     grad_pooled,
     normed,
@@ -436,64 +472,63 @@
     after,
     beside_slope,
     beside_inv,
-    weight,
+    time,
     grad,
     top,
     bottom,
     gain,
     cells,
-    time,
-    sems,
     *,
     cell_count,
 ):
-    copy = (weight, time, sems.at[0])
-    start(copy)
-    frames, rows, columns, channels = grad.shape
-    step = rows * columns
+    frames = inv.shape[0]
+    channels = normed.shape[1]
+    step = normed.shape[0] // frames
     count = frames + 2
     total = jnp.sum(stats[...], axis=0)
     for k in range(gain.shape[1] // LANES):
         gain[:, k * LANES : (k + 1) * LANES] = total[2 * count + k : 2 * count + k + 1]
     means = spread(total[: 2 * count] / cell_count, channels)
     at = lax.axis_index("frame")
-    last = lax.axis_size("frame") - 1
-
-    def back(f, low, cells_normed, cells_slope, scale):
-        grown = unpooled(low)
-        grown = jnp.concatenate([grown] * rows, axis=0)
-        return scale * (
-            grown * cells_slope.astype(f32)
-            - means[f : f + 1]
-            - cells_normed.astype(f32) * means[count + f : count + f + 1]
-        )
-
-    early = back(0, grad_pooled[0], before[:step], beside_slope[0], beside_inv[0:1])
+
+    def coefficients(f):
+        return means[f : f + 1], means[count + f : count + f + 1]
+
+    early = norm_back(
+        unpooled(grad_pooled[0]), before[:step], beside_slope[0], beside_inv[0:1], *coefficients(0)
+    )
     cells[:step] = jnp.where(at > 0, early, 0.0).astype(bf16)
+    grown = unpooled(grad_pooled[1])
     for f in range(frames):
         here = slice(f * step, (f + 1) * step)
-        value = back(f + 1, grad_pooled[1], normed[here], slope[here], inv[f : f + 1])
+        value = norm_back(grown, normed[here], slope[here], inv[f : f + 1], *coefficients(f + 1))
         cells[(f + 1) * step : (f + 2) * step] = value.astype(bf16)
-    late = back(
-        count - 1, grad_pooled[2], after[:step], beside_slope[1], beside_inv[1:2]
-    )
-    cells[(count - 1) * step :] = jnp.where(at < last, late, 0.0).astype(bf16)
-    size = frames * step
-    wait(copy)
-    sums = dot_nt(cells[:size], time[2])
-    sums += dot_nt(cells[step : step + size], time[1])
-    sums += dot_nt(cells[2 * step :], time[0])
-    spatial = sums.astype(bf16).reshape(grad.shape)
-    grad[...] = spatial
-    top[...] = spatial[:, :1]
-    bottom[...] = spatial[:, -1:]
-
-
-def space_back_finish(part, above, below, weight, grad_pooled, out):
+    late = norm_back(
+        unpooled(grad_pooled[2]),
+        after[:step],
+        beside_slope[1],
+        beside_inv[1:2],
+        *coefficients(count - 1),
+    )
+    there = at < lax.axis_size("frame") - 1
+    cells[(count - 1) * step :] = jnp.where(there, late, 0.0).astype(bf16)
+    time_back(cells, time, grad, top, bottom)
+
+
+def space_back(cells, weight_far, part, weight, sems):
+    space_own(cells, weight_far, part, weight, sems, back=True)
+
+
+def space_back_finish(part, above, below, weight, grad_pooled, out, block, sem):
     grown = unpooled(grad_pooled[1]) * (1.0 / 16.0)
-    for at, row in enumerate(space_edges(part, above, below, weight, True)):
-        row = row.reshape(out.shape[0], *out.shape[2:]) + grown[None]
-        out[:, at] = row.astype(bf16)
+    frames, rows, columns, channels = block.shape
+    copies = []
+    for r, (i, rim) in enumerate(zip((0, 2), inside(above[...], below[...]))):
+        row = part[r] + row_sum(taps(rim), weight, i, True)
+        block[:, r] = (row.reshape(frames, columns, channels) + grown[None]).astype(bf16)
+        copies.append((block.at[:, r], out.at[:, r], sem.at[r]))
+        start(copies[r])
+    wait(*copies)
 
 
 def project_cot(cot, proj_in, proj_out, grad_heads, cot_in, low, high, sems):
@@ -505,12 +540,15 @@
     grad_heads[...] = dot_nt(cot[...], high[...]).astype(bf16)
 
 
-def merge(proj_in, proj_query, proj_key, proj_value, merged, low, weights, sems):
+def merge(
+    proj_in, proj_query, proj_key, proj_value, bias, merged, bias_out, low, weights, bias_here, sems
+):
+    bias_copy = (bias, bias_here, sems.at[1, 3])
     depth, width = proj_query.shape
     parts = weights.shape[0]
     piece = depth // parts
     first = (proj_in, low, sems.at[0, 3])
-    start(first)
+    start(first, bias_copy)
     copies = []
     for k in range(parts):
         here = pl.ds(k * piece, piece)
@@ -528,16 +566,19 @@
         product = dot(low[:, k * piece : (k + 1) * piece], weights[k])
         sums = product if sums is None else sums + product
     merged[...] = sums.astype(bf16)
-
-
-def coarse_finish(pooled, proj_in, blended, proj_out, out, token, low, high, sems):
+    wait(bias_copy)
+    bias_out[...] = bias_here[...].reshape(-1, bias_here.shape[2]).T
+
+
+def coarse_finish(pooled, proj_in, blended, proj_out, time_far, out, time, low, high, sems):
+    time_copy = (time_far, time, sems.at[2])
     copies = ((proj_in, low, sems.at[0]), (proj_out, high, sems.at[1]))
-    start(*copies)
+    start(*copies, time_copy)
     wait(copies[0])
     base = dot(pooled[...], low[...]).astype(bf16).astype(f32)
     wait(copies[1])
     out[...] = (base + dot(blended[...], high[...])).astype(bf16)
-    token[...] = jnp.zeros_like(token)
+    wait(time_copy)
 
 
 def neighbours(tail, head, axis):
@@ -579,7 +620,7 @@
     band = shape(frames_in.shape, bf16)
     gain = norm_gain.reshape(1, channels)
     packing = (
-        pltpu.VMEM((half, 3 * SLOT + width), f32),
+        pltpu.VMEM((half, -(-(3 * channels + width) // LANES) * LANES), f32),
         pltpu.VMEM((half * PAYLOAD, LANES), f32),
     )
     payload = shape((half, PAYLOAD, LANES), bf16)
@@ -615,9 +656,9 @@
         spatial_outer, (edge, edge), part, outer_above, outer_below, weight, pin=(0, 1)
     )
     before, after = neighbours(last, first, "frame")
-    part, weight = call(
+    part, weight, inner_sums = call(
         spatial_inner,
-        (flat, shape(kernel_time.shape, bf16)),
+        (flat, shape(kernel_time.shape, bf16), shape((2 * frames, channels), f32)),
         part,
         inner_above,
         inner_below,
@@ -627,16 +668,19 @@
         kernel_time,
         scratch=(pltpu.VMEM(frames_in.shape, bf16), pltpu.SemaphoreType.DMA((1,))),
         far=(6,),
-        pin=(0, 1),
+        pin=(0, 1, 2),
     )
     temporal, stats = call(
-        lambda *refs: temporal_finish(*refs, frames=frames),
+        temporal_finish,
         (flat, shape((bands, 2 * frames, LANES), f32)),
         part,
         before,
         after,
         weight,
+        inner_sums,
+        scratch=(pltpu.VMEM((2 * frames, channels), f32),),
         pin=(0,),
+        alias={0: 0},
     )
     cot = cotangent.reshape(half, depth)
     token = shape((8, LANES), f32)
@@ -675,20 +719,22 @@
         pin=(0, 1, 2),
         after=(pooled,),
     )
-    merged = call(
+    merged, bias = call(
         merge,
-        shape((channels, 3 * width), bf16),
+        (shape((channels, 3 * width), bf16), shape((half, heads * half), f32)),
         proj_in,
         proj_query,
         proj_key,
         proj_value,
+        frame_bias,
         scratch=(
             low,
             pltpu.VMEM((5, depth // 5, 3 * width), bf16),
+            pltpu.VMEM(frame_bias.shape, f32),
             pltpu.SemaphoreType.DMA((5, 4)),
         ),
-        far=(0, 1, 2, 3),
-        pin=(0,),
+        far=(0, 1, 2, 3, 4),
+        pin=(0, 1),
         after=(slopes_token,),
     )
     before, after = neighbours(tail, head, "frame")
@@ -697,15 +743,13 @@
         payload,
         received,
         merged,
-        frame_bias,
+        bias,
         scratch=(
             packing[0],
             pltpu.VMEM((half, 4 * channels + width), f32),
             packing[1],
-            pltpu.VMEM(frame_bias.shape, f32),
-            pltpu.SemaphoreType.DMA((1,)),
+            pltpu.VMEM((2, heads * half, width), bf16),
         ),
-        far=(2,),
     )
     beside_slope, beside_inv = call(
         slopes_beside,
@@ -731,21 +775,23 @@
         beside_slope,
         scratch=(pltpu.VMEM((half, 4 * channels + width), f32), packing[1]),
     )
-    coarse_out, coarse_token = call(
+    coarse_out, time = call(
         coarse_finish,
-        (shape((half, depth), bf16), token),
+        (shape((half, depth), bf16), shape(kernel_time.shape, bf16)),
         pooled,
         proj_in,
         blended,
         proj_out,
-        scratch=(low, high, pltpu.SemaphoreType.DMA((2,))),
-        far=(1, 3),
+        kernel_time,
+        scratch=(low, high, pltpu.SemaphoreType.DMA((3,))),
+        far=(1, 3, 4),
+        pin=(1,),
         after=(stats,),
     )
     stats = exchange(stats, "space")
-    row_edge = shape((frames, 1, columns, channels), bf16)
+    row_edge = shape((frames, columns, channels), bf16)
     grad_spatial, top, bottom, grad_gain = call(
-        lambda *refs: norm_back(*refs, cell_count=cell_count),
+        lambda *refs: frames_back(*refs, cell_count=cell_count),
         (band, row_edge, row_edge, shape((1, SLOT), f32)),
         stats,
         grad_pooled,
@@ -756,18 +802,13 @@
         after,
         beside_slope,
         beside_inv,
-        kernel_time,
-        scratch=(
-            pltpu.VMEM(((frames + 2) * rows * columns, channels), bf16),
-            pltpu.VMEM(kernel_time.shape, bf16),
-            pltpu.SemaphoreType.DMA((1,)),
-        ),
-        far=(9,),
-        after=(coarse_token,),
+        time,
+        scratch=(pltpu.VMEM(((frames + 2) * rows * columns, channels), bf16),),
+        pin=(0, 1, 2, 3),
     )
     above, below = neighbours(bottom, top, "space")
     part, weight = call(
-        lambda *refs: space_own(*refs, back=True),
+        space_back,
         (partial, space_here),
         grad_spatial,
         kernel_space,
@@ -775,7 +816,17 @@
         far=(1,),
         pin=(0, 1),
     )
-    grad_frames = call(space_back_finish, band, part, above, below, weight, grad_pooled)
+    grad_frames = call(
+        space_back_finish,
+        band,
+        part,
+        above,
+        below,
+        weight,
+        grad_pooled,
+        scratch=(pltpu.VMEM(band.shape, bf16), pltpu.SemaphoreType.DMA((2,))),
+        far_out=(0,),
+    )
     return coarse_out.reshape(cotangent.shape), grad_frames, grad_gain[0, :channels]
 
 

time: 98.7 us -> 96.4 us (0.977)
  Pallas kernels: 33.4 us -> 31.1 us
    pallas_call x16, Pallas kernels: 33.4 us -> 31.1 us  [call(): pl.pallas_call(body, out_shape=shapes[0] if single else shapes, in_specs=...]
where the time goes in v5:
time: 96.4 us; the launch traced here: 95.7 us
  starting transfers between devices  44.7 us (46%)
  Pallas kernels  31.1 us (32%)
  waiting for transfers between devices  18.4 us (19%)
    pallas_call x16, Pallas kernels, call(): pl.pallas_call(body, out_shape=shapes[0] if single else shapes, in_specs=...  31.1 us
    all_to_all x4, starting transfers between devices, exchange(): lax.all_to_all(payload, axis, split_axis=0, concat_axis=0, tiled=True)  24.9 us
    ppermute x5, starting transfers between devices, neighbours(): lax.ppermute(head, axis, [((i + 1) % count, i) for i in range(count)])  10.6 us
    ppermute x5, starting transfers between devices, neighbours(): lax.ppermute(tail, axis, [(i, (i + 1) % count) for i in range(count)])  9.17 us
    all_to_all x4, waiting for transfers between devices, exchange(): lax.all_to_all(payload, axis, split_axis=0, concat_axis=0, tiled=True)  8.62 us
    ppermute x5, waiting for transfers between devices, neighbours(): lax.ppermute(tail, axis, [(i, (i + 1) % count) for i in range(count)])  5.95 us
    ppermute x5, waiting for transfers between devices, neighbours(): lax.ppermute(head, axis, [((i + 1) % count, i) for i in range(count)])  3.79 us
  transfers between devices with their start and end apart: 14, of which 8 were waited for; matrix products, arithmetic and copies ran while one was open for 1% of the time, Pallas kernels for 21%

profile of v5, /device:TPU:26, one launch (start us, length us, event | category | flops | bytes accessed | tf_op | source)
XLA Modules:
  0.0 95.7 jit_solution(12760935839706990931)
XLA Ops:
  1.7 2.0 %collective-permute-start.2 = (bf16[2,64,320]{2,1,0:T(8,128)(2,1)S(1)}, bf16[2,64,320]{2,1,0:T(8,128)(2,1)S(1)}, u32[]{:S(2)}, u32[]{:S(2)}) collective-permute-start(bf16[2,64,320]{2,1,0:T(8,128)(2,1)S(1)} %get-tuple-element.45), channel_id=1, source_target_pairs={{0,1},{1,2},{2,3},{3,4},{4,5},{5,6},{6,7},{7,0},{8,9},{9,10},{10,1... | collective-permute-start | bytes 245768 | tf_op jit(solution)/shard_map/ppermute | solution.py:587
  3.8 4.0 %collective-permute-start = (bf16[2,64,320]{2,1,0:T(8,128)(2,1)S(1)}, bf16[2,64,320]{2,1,0:T(8,128)(2,1)S(1)}, u32[]{:S(2)}, u32[]{:S(2)}) collective-permute-start(bf16[2,64,320]{2,1,0:T(8,128)(2,1)S(1)} %get-tuple-element.42), channel_id=1, source_target_pairs={{0,1},{1,2},{2,3},{3,4},{4,5},{5,6},{6,7},{7,0},{8,9},{9,10},{10,1... | collective-permute-start | bytes 245768 | tf_op jit(solution)/shard_map/ppermute | solution.py:587
  7.9 3.0 %shard_map.130 = (f32[2,256,320]{2,1,0:T(8,128)S(1)}, bf16[3,3,320,320]{3,2,1,0:T(8,128)(2,1)S(1)}) custom-call(bf16[4,2,64,320]{3,2,1,0:T(8,128)(2,1)} %refs_2_.4, bf16[3,3,320,320]{3,2,1,0:T(8,128)(2,1)} %refs_1_.9), custom_call_target="tpu_custom_call" | custom-call | tf_op jit(solution)/shard_map/pallas_call | solution.py:70
  11.6 5.3 %collective-permute-start.5 = (bf16[1,2,64,320]{3,2,1,0:T(8,128)(2,1)S(1)}, bf16[1,2,64,320]{3,2,1,0:T(8,128)(2,1)S(1)}, u32[]{:S(2)}, u32[]{:S(2)}) collective-permute-start(bf16[1,2,64,320]{3,2,1,0:T(8,128)(2,1)S(1)} %get-tuple-element.47.refs_4_), channel_id=1, source_target_pairs={{8,0},{16,8},{24,16},{32,24},{40,32},{48,40},{56,48},{64,56},{72,6... | collective-permute-start | bytes 245768 | tf_op jit(solution)/shard_map/ppermute | solution.py:588
  16.9 2.1 %shard_map.133 = (f32[512,320]{1,0:T(8,128)S(1)}, bf16[3,320,320]{2,1,0:T(8,128)(2,1)S(1)}, f32[8,320]{1,0:T(8,128)S(1)}) custom-call(f32[2,256,320]{2,1,0:T(8,128)S(1)} %get-tuple-element.41.refs_0_, bf16[2,64,320]{2,1,0:T(8,128)(2,1)S(1)} %collective-permute-done.refs_1_, bf16[2,64,320]{2,1,0:T(8,128)(2,1)S(1)} %collective-permute-done.1.refs_2_, ...), custom_call_target="tpu_custom_call" | custom-call | tf_op jit(solution)/shard_map/pallas_call | solution.py:70
  20.3 7.5 %all-to-all-start = ((f32[8,8,128]{2,1,0:T(8,128)}), f32[8,8,128]{2,1,0:T(8,128)S(1)}, u32[]{:S(2)}, u32[]{:S(2)}) async-start(f32[8,8,128]{2,1,0:T(8,128)} %get-tuple-element.53.refs_3_), calls=%async_computation | async-start | bytes 65536 | tf_op jit(solution)/shard_map/all_to_all | solution.py:593
  27.8 3.1 %shard_map.135 = (bf16[32,640]{1,0:T(8,128)(2,1)S(1)}, f32[32,320]{1,0:T(8,128)S(1)}) custom-call(bf16[32,1280]{1,0:T(8,128)(2,1)S(1)} %bitcast.2, bf16[320,1280]{1,0:T(8,128)(2,1)} %refs_1_.8, bf16[640,1280]{1,0:T(8,128)(2,1)} %refs_3_.3, f32[8,8,128]{2,1,0:T(8,128)} %get-tuple-element.53.refs_3_), custom_call_target="tpu_custom_call" | custom-call | tf_op jit(solution)/shard_map/pallas_call | solution.py:70
  31.2 1.5 %shard_map.136 = (bf16[32,16,128]{2,1,0:T(8,128)(2,1)}, bf16[32,320]{1,0:T(8,128)(2,1)S(1)}) custom-call(f32[512,320]{1,0:T(8,128)S(1)} %get-tuple-element.52.refs_0_, f32[8,8,128]{2,1,0:T(8,128)S(1)} %all-to-all-done.refs_1_, bf16[4,2,64,320]{3,2,1,0:T(8,128)(2,1)S(1)} %copy-done, f32[1,320]{1,0:T(1,128)S(1)} %reshape.15.refs_3_.refs_2_, ...), custom_call_target="tpu_custom_call" | custom-call | tf_op jit(solution)/shard_map/pallas_call | solution.py:70
  32.7 6.8 %all-to-all-start.1 = ((bf16[32,16,128]{2,1,0:T(8,128)(2,1)}), bf16[32,16,128]{2,1,0:T(8,128)(2,1)S(1)}, u32[]{:S(2)}, u32[]{:S(2)}) async-start(bf16[32,16,128]{2,1,0:T(8,128)(2,1)} %get-tuple-element.57), calls=%async_computation.1 | async-start | bytes 262144 | tf_op jit(solution)/shard_map/all_to_all | solution.py:593
  40.1 4.3 %shard_map.138 = (bf16[320,1920]{1,0:T(8,128)(2,1)S(1)}, f32[32,320]{1,0:T(8,128)S(1)}) custom-call(bf16[320,1280]{1,0:T(8,128)(2,1)} %refs_1_.8, bf16[1280,640]{1,0:T(8,128)(2,1)} %refs_1_.7, bf16[1280,640]{1,0:T(8,128)(2,1)} %refs_2_.5, bf16[1280,640]{1,0:T(8,128)(2,1)} %refs_3_.2, f32[10,32,32]{2,1,0:T(8,128)} %refs_4_.2, ...), custom_call_target="tpu_custom_call" | custom-call | tf_op jit(solution)/shard_map/pallas_call | solution.py:70
  44.4 6.9 %all-to-all-done.1.refs_0_ = bf16[32,16,128]{2,1,0:T(8,128)(2,1)S(1)} async-done(((bf16[32,16,128]{2,1,0:T(8,128)(2,1)}), bf16[32,16,128]{2,1,0:T(8,128)(2,1)S(1)}, u32[]{:S(2)}, u32[]{:S(2)}) %all-to-all-start.1) | async-done | bytes 131104 | tf_op jit(solution)/shard_map/all_to_all | solution.py:593
  51.3 2.5 %shard_map.139 = bf16[32,16,128]{2,1,0:T(8,128)(2,1)} custom-call(bf16[32,16,128]{2,1,0:T(8,128)(2,1)S(1)} %all-to-all-done.1.refs_0_, bf16[320,1920]{1,0:T(8,128)(2,1)S(1)} %get-tuple-element.59.refs_1_, f32[32,320]{1,0:T(8,128)S(1)} %get-tuple-element.60.refs_2_), custom_call_target="tpu_custom_call" | custom-call | tf_op jit(solution)/shard_map/pallas_call | solution.py:70
  53.8 3.9 %all-to-all-start.2 = ((bf16[32,16,128]{2,1,0:T(8,128)(2,1)}), bf16[32,16,128]{2,1,0:T(8,128)(2,1)S(1)}, u32[]{:S(2)}, u32[]{:S(2)}) async-start(bf16[32,16,128]{2,1,0:T(8,128)(2,1)} %shard_map.139), calls=%async_computation.2 | async-start | bytes 262144 | tf_op jit(solution)/shard_map/all_to_all | solution.py:593
  57.9 5.2 %collective-permute-start.7 = (bf16[144,320]{1,0:T(8,128)(2,1)S(1)}, bf16[144,320]{1,0:T(8,128)(2,1)S(1)}, u32[]{:S(2)}, u32[]{:S(2)}) collective-permute-start(bf16[144,320]{1,0:T(8,128)(2,1)S(1)} %get-tuple-element.64), channel_id=1, source_target_pairs={{8,0},{16,8},{24,16},{32,24},{40,32},{48,40},{56,48},{64,56},{72,6... | collective-permute-start | bytes 276488 | tf_op jit(solution)/shard_map/ppermute | solution.py:588
  63.1 5.0 %collective-permute-done.6.refs_0_.refs_3_.refs_5_ = bf16[144,320]{1,0:T(8,128)(2,1)S(1)} collective-permute-done((bf16[144,320]{1,0:T(8,128)(2,1)S(1)}, bf16[144,320]{1,0:T(8,128)(2,1)S(1)}, u32[]{:S(2)}, u32[]{:S(2)}) %collective-permute-start.6) | collective-permute-done | bytes 92192 | tf_op jit(solution)/shard_map/ppermute | solution.py:587
  68.2 1.6 %all-to-all-done.2.refs_0_ = bf16[32,16,128]{2,1,0:T(8,128)(2,1)S(1)} async-done(((bf16[32,16,128]{2,1,0:T(8,128)(2,1)}), bf16[32,16,128]{2,1,0:T(8,128)(2,1)S(1)}, u32[]{:S(2)}, u32[]{:S(2)}) %all-to-all-start.2) | async-done | bytes 131104 | tf_op jit(solution)/shard_map/all_to_all | solution.py:593
  69.8 1.3 %shard_map.141 = (f32[8,16,128]{2,1,0:T(8,128)}, bf16[3,32,320]{2,1,0:T(8,128)(2,1)S(1)}, bf16[32,640]{1,0:T(8,128)(2,1)S(1)}) custom-call(bf16[32,16,128]{2,1,0:T(8,128)(2,1)S(1)} %all-to-all-done.2.refs_0_, bf16[512,320]{1,0:T(8,128)(2,1)S(1)} %get-tuple-element.61.refs_1_.refs_2_, bf16[512,320]{1,0:T(8,128)(2,1)S(1)} %get-tuple-element.62.refs_2_.refs_3_, ...), custom_call_target="tpu_custom_call" | custom-call | tf_op jit(solution)/shard_map/pallas_call | solution.py:70
  71.1 6.8 %all-to-all-start.3 = ((f32[8,16,128]{2,1,0:T(8,128)}), f32[8,16,128]{2,1,0:T(8,128)S(1)}, u32[]{:S(2)}, u32[]{:S(2)}) async-start(f32[8,16,128]{2,1,0:T(8,128)} %get-tuple-element.67.refs_5_), calls=%async_computation.3 | async-start | bytes 131072 | tf_op jit(solution)/shard_map/all_to_all | solution.py:593
  77.9 3.6 %shard_map.142 = (bf16[32,1280]{1,0:T(8,128)(2,1)}, bf16[3,320,320]{2,1,0:T(8,128)(2,1)S(1)}) custom-call(bf16[32,320]{1,0:T(8,128)(2,1)S(1)} %get-tuple-element.56.refs_3_.refs_0_, bf16[320,1280]{1,0:T(8,128)(2,1)} %refs_1_.8, bf16[32,640]{1,0:T(8,128)(2,1)S(1)} %get-tuple-element.66.refs_2_, bf16[640,1280]{1,0:T(8,128)(2,1)} %refs_3_.3, ...), custom_call_target="tpu_custom_call" | custom-call | tf_op jit(solution)/shard_map/pallas_call | solution.py:70
  81.5 1.3 %shard_map.143 = (bf16[4,2,64,320]{3,2,1,0:T(8,128)(2,1)S(1)}, bf16[4,64,320]{2,1,0:T(8,128)(2,1)S(1)}, bf16[4,64,320]{2,1,0:T(8,128)(2,1)S(1)}, f32[1,384]{1,0:T(1,128)S(1)}) custom-call(f32[8,16,128]{2,1,0:T(8,128)S(1)} %all-to-all-done.3.refs_0_, bf16[3,32,320]{2,1,0:T(8,128)(2,1)S(1)} %get-tuple-element.69.refs_1_.refs_4_, ...), custom_call_target="tpu_custom_call" | custom-call | tf_op jit(solution)/shard_map/pallas_call | solution.py:70
  82.8 2.8 %collective-permute-start.8 = (bf16[4,64,320]{2,1,0:T(8,128)(2,1)S(1)}, bf16[4,64,320]{2,1,0:T(8,128)(2,1)S(1)}, u32[]{:S(2)}, u32[]{:S(2)}) collective-permute-start(bf16[4,64,320]{2,1,0:T(8,128)(2,1)S(1)} %get-tuple-element.75), channel_id=1, source_target_pairs={{0,1},{1,2},{2,3},{3,4},{4,5},{5,6},{6,7},{7,0},{8,9},{9,10},{10,1... | collective-permute-start | bytes 491528 | tf_op jit(solution)/shard_map/ppermute | solution.py:587
  85.6 3.2 %shard_map.144 = (f32[2,256,320]{2,1,0:T(8,128)S(1)}, bf16[3,3,320,320]{3,2,1,0:T(8,128)(2,1)S(1)}) custom-call(bf16[4,2,64,320]{3,2,1,0:T(8,128)(2,1)S(1)} %get-tuple-element.73.refs_0_, bf16[3,3,320,320]{3,2,1,0:T(8,128)(2,1)} %refs_1_.9), custom_call_target="tpu_custom_call" | custom-call | tf_op jit(solution)/shard_map/pallas_call | solution.py:70
  90.2 3.7 %collective-permute-done.9.refs_2_ = bf16[4,64,320]{2,1,0:T(8,128)(2,1)S(1)} collective-permute-done((bf16[4,64,320]{2,1,0:T(8,128)(2,1)S(1)}, bf16[4,64,320]{2,1,0:T(8,128)(2,1)S(1)}, u32[]{:S(2)}, u32[]{:S(2)}) %collective-permute-start.9) | collective-permute-done | bytes 163872 | tf_op jit(solution)/shard_map/ppermute | solution.py:588
  93.9 1.6 %shard_map.145 = bf16[4,2,64,320]{3,2,1,0:T(8,128)(2,1)} custom-call(f32[2,256,320]{2,1,0:T(8,128)S(1)} %get-tuple-element.74.refs_0_, bf16[4,64,320]{2,1,0:T(8,128)(2,1)S(1)} %collective-permute-done.8.refs_1_, bf16[4,64,320]{2,1,0:T(8,128)(2,1)S(1)} %collective-permute-done.9.refs_2_, bf16[3,3,320,320]{3,2,1,0:T(8,128)(2,1)S(1)} %get-tuple-element.77.refs_3_, ...), custom_call_target="tpu_custom_call" | custom-call | tf_op jit(solution)/shard_map/pallas_call | solution.py:70
  (28 shorter events, 5.7 us)
Async XLA Ops:
  1.7 9.1 %collective-permute-start.2 = (bf16[2,64,320]{2,1,0:T(8,128)(2,1)S(1)}, bf16[2,64,320]{2,1,0:T(8,128)(2,1)S(1)}, u32[]{:S(2)}, u32[]{:S(2)}) collective-permute-start(bf16[2,64,320]{2,1,0:T(8,128)(2,1)S(1)} %get-tuple-element.45), channel_id=1, source_target_pairs={{0,1},{1,2},{2,3},{3,4},{4,5},{5,6},{6,7},{7,0},{8,9},{9,10},{10,1... | collective-permute-start | bytes 245768 | tf_op jit(solution)/shard_map/ppermute | solution.py:587
  3.7 7.2 %collective-permute-start.3 = (bf16[2,64,320]{2,1,0:T(8,128)(2,1)S(1)}, bf16[2,64,320]{2,1,0:T(8,128)(2,1)S(1)}, u32[]{:S(2)}, u32[]{:S(2)}) collective-permute-start(bf16[2,64,320]{2,1,0:T(8,128)(2,1)S(1)} %get-tuple-element.46), channel_id=1, source_target_pairs={{1,0},{2,1},{3,2},{4,3},{5,4},{6,5},{7,6},{0,7},{9,8},{10,9},{11,1... | collective-permute-start | bytes 245768 | tf_op jit(solution)/shard_map/ppermute | solution.py:588
  3.8 13.1 %collective-permute-start = (bf16[2,64,320]{2,1,0:T(8,128)(2,1)S(1)}, bf16[2,64,320]{2,1,0:T(8,128)(2,1)S(1)}, u32[]{:S(2)}, u32[]{:S(2)}) collective-permute-start(bf16[2,64,320]{2,1,0:T(8,128)(2,1)S(1)} %get-tuple-element.42), channel_id=1, source_target_pairs={{0,1},{1,2},{2,3},{3,4},{4,5},{5,6},{6,7},{7,0},{8,9},{9,10},{10,1... | collective-permute-start | bytes 245768 | tf_op jit(solution)/shard_map/ppermute | solution.py:587
  7.9 9.1 %collective-permute-start.1 = (bf16[2,64,320]{2,1,0:T(8,128)(2,1)S(1)}, bf16[2,64,320]{2,1,0:T(8,128)(2,1)S(1)}, u32[]{:S(2)}, u32[]{:S(2)}) collective-permute-start(bf16[2,64,320]{2,1,0:T(8,128)(2,1)S(1)} %get-tuple-element.43), channel_id=1, source_target_pairs={{1,0},{2,1},{3,2},{4,3},{5,4},{6,5},{7,6},{0,7},{9,8},{10,9},{11,1... | collective-permute-start | bytes 245768 | tf_op jit(solution)/shard_map/ppermute | solution.py:588
  11.5 7.7 %collective-permute-start.4 = (bf16[1,2,64,320]{3,2,1,0:T(8,128)(2,1)S(1)}, bf16[1,2,64,320]{3,2,1,0:T(8,128)(2,1)S(1)}, u32[]{:S(2)}, u32[]{:S(2)}) collective-permute-start(bf16[1,2,64,320]{3,2,1,0:T(8,128)(2,1)S(1)} %get-tuple-element.48.refs_5_), channel_id=1, source_target_pairs={{0,8},{8,16},{16,24},{24,32},{32,40},{40,48},{48,56},{56,64},{64,7... | collective-permute-start | bytes 245768 | tf_op jit(solution)/shard_map/ppermute | solution.py:587
  11.6 7.6 %collective-permute-start.5 = (bf16[1,2,64,320]{3,2,1,0:T(8,128)(2,1)S(1)}, bf16[1,2,64,320]{3,2,1,0:T(8,128)(2,1)S(1)}, u32[]{:S(2)}, u32[]{:S(2)}) collective-permute-start(bf16[1,2,64,320]{3,2,1,0:T(8,128)(2,1)S(1)} %get-tuple-element.47.refs_4_), channel_id=1, source_target_pairs={{8,0},{16,8},{24,16},{32,24},{40,32},{48,40},{56,48},{64,56},{72,6... | collective-permute-start | bytes 245768 | tf_op jit(solution)/shard_map/ppermute | solution.py:588
  19.0 8.8 %copy-start.2 = (f32[320]{0:T(512)S(1)}, f32[320]{0:T(512)}, u32[]{:S(2)}) copy-start(f32[320]{0:T(512)} %param.14) | copy-start | bytes 3844
  19.0 8.8 %copy-start.1 = (bf16[1,1,32,1280]{3,2,1,0:T(8,128)(2,1)S(1)}, bf16[1,1,32,1280]{3,2,1,0:T(8,128)(2,1)}, u32[]{:S(2)}) copy-start(bf16[1,1,32,1280]{3,2,1,0:T(8,128)(2,1)} %param.21) | copy-start | bytes 245764
  20.3 10.8 %copy-start = (bf16[4,2,64,320]{3,2,1,0:T(8,128)(2,1)S(1)}, bf16[4,2,64,320]{3,2,1,0:T(8,128)(2,1)}, u32[]{:S(2)}) copy-start(bf16[4,2,64,320]{3,2,1,0:T(8,128)(2,1)} %refs_2_.4) | copy-start | bytes 983044
  20.3 10.8 %all-to-all-start = ((f32[8,8,128]{2,1,0:T(8,128)}), f32[8,8,128]{2,1,0:T(8,128)S(1)}, u32[]{:S(2)}, u32[]{:S(2)}) async-start(f32[8,8,128]{2,1,0:T(8,128)} %get-tuple-element.53.refs_3_), calls=%async_computation | async-start | bytes 65536 | tf_op jit(solution)/shard_map/all_to_all | solution.py:593
  32.7 18.5 %all-to-all-start.1 = ((bf16[32,16,128]{2,1,0:T(8,128)(2,1)}), bf16[32,16,128]{2,1,0:T(8,128)(2,1)S(1)}, u32[]{:S(2)}, u32[]{:S(2)}) async-start(bf16[32,16,128]{2,1,0:T(8,128)(2,1)} %get-tuple-element.57), calls=%async_computation.1 | async-start | bytes 262144 | tf_op jit(solution)/shard_map/all_to_all | solution.py:593
  53.8 16.0 %all-to-all-start.2 = ((bf16[32,16,128]{2,1,0:T(8,128)(2,1)}), bf16[32,16,128]{2,1,0:T(8,128)(2,1)S(1)}, u32[]{:S(2)}, u32[]{:S(2)}) async-start(bf16[32,16,128]{2,1,0:T(8,128)(2,1)} %shard_map.139), calls=%async_computation.2 | async-start | bytes 262144 | tf_op jit(solution)/shard_map/all_to_all | solution.py:593
  57.6 10.4 %collective-permute-start.6 = (bf16[144,320]{1,0:T(8,128)(2,1)S(1)}, bf16[144,320]{1,0:T(8,128)(2,1)S(1)}, u32[]{:S(2)}, u32[]{:S(2)}) collective-permute-start(bf16[144,320]{1,0:T(8,128)(2,1)S(1)} %get-tuple-element.63), channel_id=1, source_target_pairs={{0,8},{8,16},{16,24},{24,32},{32,40},{40,48},{48,56},{56,64},{64,7... | collective-permute-start | bytes 276488 | tf_op jit(solution)/shard_map/ppermute | solution.py:587
  57.9 10.2 %collective-permute-start.7 = (bf16[144,320]{1,0:T(8,128)(2,1)S(1)}, bf16[144,320]{1,0:T(8,128)(2,1)S(1)}, u32[]{:S(2)}, u32[]{:S(2)}) collective-permute-start(bf16[144,320]{1,0:T(8,128)(2,1)S(1)} %get-tuple-element.64), channel_id=1, source_target_pairs={{8,0},{16,8},{24,16},{32,24},{40,32},{48,40},{56,48},{64,56},{72,6... | collective-permute-start | bytes 276488 | tf_op jit(solution)/shard_map/ppermute | solution.py:588
  71.1 10.4 %all-to-all-start.3 = ((f32[8,16,128]{2,1,0:T(8,128)}), f32[8,16,128]{2,1,0:T(8,128)S(1)}, u32[]{:S(2)}, u32[]{:S(2)}) async-start(f32[8,16,128]{2,1,0:T(8,128)} %get-tuple-element.67.refs_5_), calls=%async_computation.3 | async-start | bytes 131072 | tf_op jit(solution)/shard_map/all_to_all | solution.py:593
  82.8 7.4 %collective-permute-start.8 = (bf16[4,64,320]{2,1,0:T(8,128)(2,1)S(1)}, bf16[4,64,320]{2,1,0:T(8,128)(2,1)S(1)}, u32[]{:S(2)}, u32[]{:S(2)}) collective-permute-start(bf16[4,64,320]{2,1,0:T(8,128)(2,1)S(1)} %get-tuple-element.75), channel_id=1, source_target_pairs={{0,1},{1,2},{2,3},{3,4},{4,5},{5,6},{6,7},{7,0},{8,9},{9,10},{10,1... | collective-permute-start | bytes 491528 | tf_op jit(solution)/shard_map/ppermute | solution.py:587
  85.6 8.3 %collective-permute-start.9 = (bf16[4,64,320]{2,1,0:T(8,128)(2,1)S(1)}, bf16[4,64,320]{2,1,0:T(8,128)(2,1)S(1)}, u32[]{:S(2)}, u32[]{:S(2)}) collective-permute-start(bf16[4,64,320]{2,1,0:T(8,128)(2,1)S(1)} %get-tuple-element.76), channel_id=1, source_target_pairs={{1,0},{2,1},{3,2},{4,3},{5,4},{6,5},{7,6},{0,7},{9,8},{10,9},{11,1... | collective-permute-start | bytes 491528 | tf_op jit(solution)/shard_map/ppermute | solution.py:588

commit v6 on v5

--- a/solution.py
+++ b/solution.py
@@ -122,15 +122,18 @@
     wait(*copies)
 
 
-def space_first(cells_far, weight_far, part, weight, cells, sems, cells_sem):
-    copy = (cells_far, cells, cells_sem.at[0])
+def space_first(cells_far, weight_far, time_far, part, weight, time, cells, sems, more_sems):
+    copy = (cells_far, cells, more_sems.at[0])
+    time_copy = (time_far, time, more_sems.at[1])
     start(copy)
-    space_own(cells, weight_far, part, weight, sems, back=False, copy=copy)
-
-
-def space_own(cells, weight_far, part, weight, sems, *, back, copy=None):
+    space_own(cells, weight_far, part, weight, sems, back=False, copy=copy, last=time_copy)
+
+
+def space_own(cells, weight_far, part, weight, sems, *, back, copy=None, last=None):
     copies = [(weight_far.at[i], weight.at[i], sems.at[i]) for i in range(3)]
     start(*copies)
+    if last:
+        start(last)
     if copy:
         wait(copy)
     first = taps(cells[:, 0])
@@ -138,6 +141,8 @@
     wait(*copies)
     part[0] = row_sum(first, weight, 1, back) + row_sum(second, weight, 2, back)
     part[1] = row_sum(second, weight, 1, back) + row_sum(first, weight, 0, back)
+    if last:
+        wait(last)
 
 
 def inside(above, below):
@@ -158,9 +163,7 @@
         last[0, r] = row[columns:]
 
 
-def spatial_inner(part, above, below, weight, first, last, time_far, sums, time, moments_out, cells, sems):
-    copy = (time_far, time, sems.at[0])
-    start(copy)
+def spatial_inner(part, above, below, weight, first, last, time, sums, moments_out, cells):
     columns = above.shape[1]
     frames, rows = cells.shape[:2]
     for r, (i, rim) in enumerate(zip((0, 2), inside(above[...], below[...]))):
@@ -168,7 +171,6 @@
         cells[1 : frames - 1, r] = row.astype(bf16).reshape(frames - 2, *cells.shape[2:])
     cells[0] = first[0]
     cells[frames - 1] = last[0]
-    wait(copy)
     time_own(cells, time, sums)
     step = sums.shape[0] // frames
     for f in range(1, frames - 1):
@@ -639,36 +641,36 @@
     outer_above, outer_below = neighbours(outer_bottom, outer_top, "space")
     inner_above, inner_below = neighbours(inner_bottom, inner_top, "space")
     space_here = shape(kernel_space.shape, bf16)
-    part, weight = call(
+    part, weight, time = call(
         space_first,
-        (partial, space_here),
+        (partial, space_here, shape(kernel_time.shape, bf16)),
         frames_in,
         kernel_space,
+        kernel_time,
         scratch=(
             pltpu.VMEM(frames_in.shape, bf16),
             pltpu.SemaphoreType.DMA((3,)),
-            pltpu.SemaphoreType.DMA((1,)),
+            pltpu.SemaphoreType.DMA((2,)),
         ),
-        far=(0, 1),
-        pin=(0, 1),
+        far=(0, 1, 2),
+        pin=(0, 1, 2),
     )
     first, last = call(
         spatial_outer, (edge, edge), part, outer_above, outer_below, weight, pin=(0, 1)
     )
     before, after = neighbours(last, first, "frame")
-    part, weight, inner_sums = call(
+    part, inner_sums = call(
         spatial_inner,
-        (flat, shape(kernel_time.shape, bf16), shape((2 * frames, channels), f32)),
+        (flat, shape((2 * frames, channels), f32)),
         part,
         inner_above,
         inner_below,
         weight,
         first,
         last,
-        kernel_time,
-        scratch=(pltpu.VMEM(frames_in.shape, bf16), pltpu.SemaphoreType.DMA((1,))),
-        far=(6,),
-        pin=(0, 1, 2),
+        time,
+        scratch=(pltpu.VMEM(frames_in.shape, bf16),),
+        pin=(0, 1),
     )
     temporal, stats = call(
         temporal_finish,
@@ -676,7 +678,7 @@
         part,
         before,
         after,
-        weight,
+        time,
         inner_sums,
         scratch=(pltpu.VMEM((2 * frames, channels), f32),),
         pin=(0,),

time: 96.4 us -> 96.3 us (level)
  no operation moved by 1% of the time
where the time goes in v6:
time: 96.3 us; the launch traced here: 95.7 us
  starting transfers between devices  44.7 us (46%)
  Pallas kernels  30.2 us (31%)
  waiting for transfers between devices  19.2 us (20%)
    pallas_call x16, Pallas kernels, call(): pl.pallas_call(body, out_shape=shapes[0] if single else shapes, in_specs=...  30.2 us
    all_to_all x4, starting transfers between devices, exchange(): lax.all_to_all(payload, axis, split_axis=0, concat_axis=0, tiled=True)  24.9 us
    ppermute x5, starting transfers between devices, neighbours(): lax.ppermute(head, axis, [((i + 1) % count, i) for i in range(count)])  10.6 us
    ppermute x5, starting transfers between devices, neighbours(): lax.ppermute(tail, axis, [(i, (i + 1) % count) for i in range(count)])  9.17 us
    all_to_all x4, waiting for transfers between devices, exchange(): lax.all_to_all(payload, axis, split_axis=0, concat_axis=0, tiled=True)  8.61 us
    ppermute x5, waiting for transfers between devices, neighbours(): lax.ppermute(tail, axis, [(i, (i + 1) % count) for i in range(count)])  6.84 us
    ppermute x5, waiting for transfers between devices, neighbours(): lax.ppermute(head, axis, [((i + 1) % count, i) for i in range(count)])  3.78 us
  transfers between devices with their start and end apart: 14, of which 8 were waited for; matrix products, arithmetic and copies ran while one was open for 1% of the time, Pallas kernels for 21%

profile of v6, /device:TPU:26, one launch (start us, length us, event | category | flops | bytes accessed | tf_op | source)
XLA Modules:
  0.0 95.7 jit_solution(2136706103195474446)
XLA Ops:
  1.7 2.0 %collective-permute-start.2 = (bf16[2,64,320]{2,1,0:T(8,128)(2,1)S(1)}, bf16[2,64,320]{2,1,0:T(8,128)(2,1)S(1)}, u32[]{:S(2)}, u32[]{:S(2)}) collective-permute-start(bf16[2,64,320]{2,1,0:T(8,128)(2,1)S(1)} %get-tuple-element.45), channel_id=1, source_target_pairs={{0,1},{1,2},{2,3},{3,4},{4,5},{5,6},{6,7},{7,0},{8,9},{9,10},{10,1... | collective-permute-start | bytes 245768 | tf_op jit(solution)/shard_map/ppermute | solution.py:589
  3.8 4.0 %collective-permute-start = (bf16[2,64,320]{2,1,0:T(8,128)(2,1)S(1)}, bf16[2,64,320]{2,1,0:T(8,128)(2,1)S(1)}, u32[]{:S(2)}, u32[]{:S(2)}) collective-permute-start(bf16[2,64,320]{2,1,0:T(8,128)(2,1)S(1)} %get-tuple-element.42), channel_id=1, source_target_pairs={{0,1},{1,2},{2,3},{3,4},{4,5},{5,6},{6,7},{7,0},{8,9},{9,10},{10,1... | collective-permute-start | bytes 245768 | tf_op jit(solution)/shard_map/ppermute | solution.py:589
  7.9 3.0 %shard_map.130 = (f32[2,256,320]{2,1,0:T(8,128)S(1)}, bf16[3,3,320,320]{3,2,1,0:T(8,128)(2,1)S(1)}, bf16[3,320,320]{2,1,0:T(8,128)(2,1)S(1)}) custom-call(bf16[4,2,64,320]{3,2,1,0:T(8,128)(2,1)} %refs_2_.6, bf16[3,3,320,320]{3,2,1,0:T(8,128)(2,1)} %refs_1_.9, bf16[3,320,320]{2,1,0:T(8,128)(2,1)} %refs_4_.3), custom_call_target="tpu_custom_call" | custom-call | tf_op jit(solution)/shard_map/pallas_call | solution.py:70
  11.6 5.3 %collective-permute-start.5 = (bf16[1,2,64,320]{3,2,1,0:T(8,128)(2,1)S(1)}, bf16[1,2,64,320]{3,2,1,0:T(8,128)(2,1)S(1)}, u32[]{:S(2)}, u32[]{:S(2)}) collective-permute-start(bf16[1,2,64,320]{3,2,1,0:T(8,128)(2,1)S(1)} %get-tuple-element.47.refs_4_), channel_id=1, source_target_pairs={{8,0},{16,8},{24,16},{32,24},{40,32},{48,40},{56,48},{64,56},{72,6... | collective-permute-start | bytes 245768 | tf_op jit(solution)/shard_map/ppermute | solution.py:590
  16.9 1.2 %shard_map.133 = (f32[512,320]{1,0:T(8,128)S(1)}, f32[8,320]{1,0:T(8,128)S(1)}) custom-call(f32[2,256,320]{2,1,0:T(8,128)S(1)} %get-tuple-element.41.refs_0_, bf16[2,64,320]{2,1,0:T(8,128)(2,1)S(1)} %collective-permute-done.refs_1_, bf16[2,64,320]{2,1,0:T(8,128)(2,1)S(1)} %collective-permute-done.1.refs_2_, ...), custom_call_target="tpu_custom_call" | custom-call | tf_op jit(solution)/shard_map/pallas_call | solution.py:70
  20.3 7.5 %all-to-all-start = ((f32[8,8,128]{2,1,0:T(8,128)}), f32[8,8,128]{2,1,0:T(8,128)S(1)}, u32[]{:S(2)}, u32[]{:S(2)}) async-start(f32[8,8,128]{2,1,0:T(8,128)} %get-tuple-element.53.refs_3_), calls=%async_computation | async-start | bytes 65536 | tf_op jit(solution)/shard_map/all_to_all | solution.py:595
  27.9 3.1 %shard_map.135 = (bf16[32,640]{1,0:T(8,128)(2,1)S(1)}, f32[32,320]{1,0:T(8,128)S(1)}) custom-call(bf16[32,1280]{1,0:T(8,128)(2,1)S(1)} %bitcast.2, bf16[320,1280]{1,0:T(8,128)(2,1)} %refs_1_.8, bf16[640,1280]{1,0:T(8,128)(2,1)} %refs_3_.3, f32[8,8,128]{2,1,0:T(8,128)} %get-tuple-element.53.refs_3_), custom_call_target="tpu_custom_call" | custom-call | tf_op jit(solution)/shard_map/pallas_call | solution.py:70
  31.2 1.5 %shard_map.136 = (bf16[32,16,128]{2,1,0:T(8,128)(2,1)}, bf16[32,320]{1,0:T(8,128)(2,1)S(1)}) custom-call(f32[512,320]{1,0:T(8,128)S(1)} %get-tuple-element.52.refs_0_, f32[8,8,128]{2,1,0:T(8,128)S(1)} %all-to-all-done.refs_1_, bf16[4,2,64,320]{3,2,1,0:T(8,128)(2,1)S(1)} %copy-done, f32[1,320]{1,0:T(1,128)S(1)} %reshape.15.refs_3_.refs_2_, ...), custom_call_target="tpu_custom_call" | custom-call | tf_op jit(solution)/shard_map/pallas_call | solution.py:70
  32.7 6.7 %all-to-all-start.1 = ((bf16[32,16,128]{2,1,0:T(8,128)(2,1)}), bf16[32,16,128]{2,1,0:T(8,128)(2,1)S(1)}, u32[]{:S(2)}, u32[]{:S(2)}) async-start(bf16[32,16,128]{2,1,0:T(8,128)(2,1)} %get-tuple-element.57), calls=%async_computation.1 | async-start | bytes 262144 | tf_op jit(solution)/shard_map/all_to_all | solution.py:595
  40.1 4.3 %shard_map.138 = (bf16[320,1920]{1,0:T(8,128)(2,1)S(1)}, f32[32,320]{1,0:T(8,128)S(1)}) custom-call(bf16[320,1280]{1,0:T(8,128)(2,1)} %refs_1_.8, bf16[1280,640]{1,0:T(8,128)(2,1)} %refs_1_.7, bf16[1280,640]{1,0:T(8,128)(2,1)} %refs_2_.7, bf16[1280,640]{1,0:T(8,128)(2,1)} %refs_3_.2, f32[10,32,32]{2,1,0:T(8,128)} %refs_4_.2, ...), custom_call_target="tpu_custom_call" | custom-call | tf_op jit(solution)/shard_map/pallas_call | solution.py:70
  44.4 6.9 %all-to-all-done.1.refs_0_ = bf16[32,16,128]{2,1,0:T(8,128)(2,1)S(1)} async-done(((bf16[32,16,128]{2,1,0:T(8,128)(2,1)}), bf16[32,16,128]{2,1,0:T(8,128)(2,1)S(1)}, u32[]{:S(2)}, u32[]{:S(2)}) %all-to-all-start.1) | async-done | bytes 131104 | tf_op jit(solution)/shard_map/all_to_all | solution.py:595
  51.3 2.5 %shard_map.139 = bf16[32,16,128]{2,1,0:T(8,128)(2,1)} custom-call(bf16[32,16,128]{2,1,0:T(8,128)(2,1)S(1)} %all-to-all-done.1.refs_0_, bf16[320,1920]{1,0:T(8,128)(2,1)S(1)} %get-tuple-element.59.refs_1_, f32[32,320]{1,0:T(8,128)S(1)} %get-tuple-element.60.refs_2_), custom_call_target="tpu_custom_call" | custom-call | tf_op jit(solution)/shard_map/pallas_call | solution.py:70
  53.8 3.9 %all-to-all-start.2 = ((bf16[32,16,128]{2,1,0:T(8,128)(2,1)}), bf16[32,16,128]{2,1,0:T(8,128)(2,1)S(1)}, u32[]{:S(2)}, u32[]{:S(2)}) async-start(bf16[32,16,128]{2,1,0:T(8,128)(2,1)} %shard_map.139), calls=%async_computation.2 | async-start | bytes 262144 | tf_op jit(solution)/shard_map/all_to_all | solution.py:595
  57.9 5.2 %collective-permute-start.7 = (bf16[144,320]{1,0:T(8,128)(2,1)S(1)}, bf16[144,320]{1,0:T(8,128)(2,1)S(1)}, u32[]{:S(2)}, u32[]{:S(2)}) collective-permute-start(bf16[144,320]{1,0:T(8,128)(2,1)S(1)} %get-tuple-element.64), channel_id=1, source_target_pairs={{8,0},{16,8},{24,16},{32,24},{40,32},{48,40},{56,48},{64,56},{72,6... | collective-permute-start | bytes 276488 | tf_op jit(solution)/shard_map/ppermute | solution.py:590
  63.1 5.0 %collective-permute-done.6.refs_0_.refs_3_.refs_5_ = bf16[144,320]{1,0:T(8,128)(2,1)S(1)} collective-permute-done((bf16[144,320]{1,0:T(8,128)(2,1)S(1)}, bf16[144,320]{1,0:T(8,128)(2,1)S(1)}, u32[]{:S(2)}, u32[]{:S(2)}) %collective-permute-start.6) | collective-permute-done | bytes 92192 | tf_op jit(solution)/shard_map/ppermute | solution.py:589
  68.2 1.6 %all-to-all-done.2.refs_0_ = bf16[32,16,128]{2,1,0:T(8,128)(2,1)S(1)} async-done(((bf16[32,16,128]{2,1,0:T(8,128)(2,1)}), bf16[32,16,128]{2,1,0:T(8,128)(2,1)S(1)}, u32[]{:S(2)}, u32[]{:S(2)}) %all-to-all-start.2) | async-done | bytes 131104 | tf_op jit(solution)/shard_map/all_to_all | solution.py:595
  69.8 1.3 %shard_map.141 = (f32[8,16,128]{2,1,0:T(8,128)}, bf16[3,32,320]{2,1,0:T(8,128)(2,1)S(1)}, bf16[32,640]{1,0:T(8,128)(2,1)S(1)}) custom-call(bf16[32,16,128]{2,1,0:T(8,128)(2,1)S(1)} %all-to-all-done.2.refs_0_, bf16[512,320]{1,0:T(8,128)(2,1)S(1)} %get-tuple-element.61.refs_1_.refs_2_, bf16[512,320]{1,0:T(8,128)(2,1)S(1)} %get-tuple-element.62.refs_2_.refs_3_, ...), custom_call_target="tpu_custom_call" | custom-call | tf_op jit(solution)/shard_map/pallas_call | solution.py:70
  71.1 6.8 %all-to-all-start.3 = ((f32[8,16,128]{2,1,0:T(8,128)}), f32[8,16,128]{2,1,0:T(8,128)S(1)}, u32[]{:S(2)}, u32[]{:S(2)}) async-start(f32[8,16,128]{2,1,0:T(8,128)} %get-tuple-element.67.refs_5_), calls=%async_computation.3 | async-start | bytes 131072 | tf_op jit(solution)/shard_map/all_to_all | solution.py:595
  77.9 3.6 %shard_map.142 = (bf16[32,1280]{1,0:T(8,128)(2,1)}, bf16[3,320,320]{2,1,0:T(8,128)(2,1)S(1)}) custom-call(bf16[32,320]{1,0:T(8,128)(2,1)S(1)} %get-tuple-element.56.refs_3_.refs_0_, bf16[320,1280]{1,0:T(8,128)(2,1)} %refs_1_.8, bf16[32,640]{1,0:T(8,128)(2,1)S(1)} %get-tuple-element.66.refs_2_, bf16[640,1280]{1,0:T(8,128)(2,1)} %refs_3_.3, ...), custom_call_target="tpu_custom_call" | custom-call | tf_op jit(solution)/shard_map/pallas_call | solution.py:70
  81.5 1.3 %shard_map.143 = (bf16[4,2,64,320]{3,2,1,0:T(8,128)(2,1)S(1)}, bf16[4,64,320]{2,1,0:T(8,128)(2,1)S(1)}, bf16[4,64,320]{2,1,0:T(8,128)(2,1)S(1)}, f32[1,384]{1,0:T(1,128)S(1)}) custom-call(f32[8,16,128]{2,1,0:T(8,128)S(1)} %all-to-all-done.3.refs_0_, bf16[3,32,320]{2,1,0:T(8,128)(2,1)S(1)} %get-tuple-element.69.refs_1_.refs_4_, ...), custom_call_target="tpu_custom_call" | custom-call | tf_op jit(solution)/shard_map/pallas_call | solution.py:70
  82.8 2.8 %collective-permute-start.8 = (bf16[4,64,320]{2,1,0:T(8,128)(2,1)S(1)}, bf16[4,64,320]{2,1,0:T(8,128)(2,1)S(1)}, u32[]{:S(2)}, u32[]{:S(2)}) collective-permute-start(bf16[4,64,320]{2,1,0:T(8,128)(2,1)S(1)} %get-tuple-element.75), channel_id=1, source_target_pairs={{0,1},{1,2},{2,3},{3,4},{4,5},{5,6},{6,7},{7,0},{8,9},{9,10},{10,1... | collective-permute-start | bytes 491528 | tf_op jit(solution)/shard_map/ppermute | solution.py:589
  85.6 3.2 %shard_map.144 = (f32[2,256,320]{2,1,0:T(8,128)S(1)}, bf16[3,3,320,320]{3,2,1,0:T(8,128)(2,1)S(1)}) custom-call(bf16[4,2,64,320]{3,2,1,0:T(8,128)(2,1)S(1)} %get-tuple-element.73.refs_0_, bf16[3,3,320,320]{3,2,1,0:T(8,128)(2,1)} %refs_1_.9), custom_call_target="tpu_custom_call" | custom-call | tf_op jit(solution)/shard_map/pallas_call | solution.py:70
  90.2 3.7 %collective-permute-done.9.refs_2_ = bf16[4,64,320]{2,1,0:T(8,128)(2,1)S(1)} collective-permute-done((bf16[4,64,320]{2,1,0:T(8,128)(2,1)S(1)}, bf16[4,64,320]{2,1,0:T(8,128)(2,1)S(1)}, u32[]{:S(2)}, u32[]{:S(2)}) %collective-permute-start.9) | collective-permute-done | bytes 163872 | tf_op jit(solution)/shard_map/ppermute | solution.py:590
  93.9 1.6 %shard_map.145 = bf16[4,2,64,320]{3,2,1,0:T(8,128)(2,1)} custom-call(f32[2,256,320]{2,1,0:T(8,128)S(1)} %get-tuple-element.74.refs_0_, bf16[4,64,320]{2,1,0:T(8,128)(2,1)S(1)} %collective-permute-done.8.refs_1_, bf16[4,64,320]{2,1,0:T(8,128)(2,1)S(1)} %collective-permute-done.9.refs_2_, bf16[3,3,320,320]{3,2,1,0:T(8,128)(2,1)S(1)} %get-tuple-element.77.refs_3_, ...), custom_call_target="tpu_custom_call" | custom-call | tf_op jit(solution)/shard_map/pallas_call | solution.py:70
  (28 shorter events, 6.6 us)
Async XLA Ops:
  1.7 9.2 %collective-permute-start.2 = (bf16[2,64,320]{2,1,0:T(8,128)(2,1)S(1)}, bf16[2,64,320]{2,1,0:T(8,128)(2,1)S(1)}, u32[]{:S(2)}, u32[]{:S(2)}) collective-permute-start(bf16[2,64,320]{2,1,0:T(8,128)(2,1)S(1)} %get-tuple-element.45), channel_id=1, source_target_pairs={{0,1},{1,2},{2,3},{3,4},{4,5},{5,6},{6,7},{7,0},{8,9},{9,10},{10,1... | collective-permute-start | bytes 245768 | tf_op jit(solution)/shard_map/ppermute | solution.py:589
  3.7 7.2 %collective-permute-start.3 = (bf16[2,64,320]{2,1,0:T(8,128)(2,1)S(1)}, bf16[2,64,320]{2,1,0:T(8,128)(2,1)S(1)}, u32[]{:S(2)}, u32[]{:S(2)}) collective-permute-start(bf16[2,64,320]{2,1,0:T(8,128)(2,1)S(1)} %get-tuple-element.46), channel_id=1, source_target_pairs={{1,0},{2,1},{3,2},{4,3},{5,4},{6,5},{7,6},{0,7},{9,8},{10,9},{11,1... | collective-permute-start | bytes 245768 | tf_op jit(solution)/shard_map/ppermute | solution.py:590
  3.8 13.1 %collective-permute-start = (bf16[2,64,320]{2,1,0:T(8,128)(2,1)S(1)}, bf16[2,64,320]{2,1,0:T(8,128)(2,1)S(1)}, u32[]{:S(2)}, u32[]{:S(2)}) collective-permute-start(bf16[2,64,320]{2,1,0:T(8,128)(2,1)S(1)} %get-tuple-element.42), channel_id=1, source_target_pairs={{0,1},{1,2},{2,3},{3,4},{4,5},{5,6},{6,7},{7,0},{8,9},{9,10},{10,1... | collective-permute-start | bytes 245768 | tf_op jit(solution)/shard_map/ppermute | solution.py:589
  7.9 9.1 %collective-permute-start.1 = (bf16[2,64,320]{2,1,0:T(8,128)(2,1)S(1)}, bf16[2,64,320]{2,1,0:T(8,128)(2,1)S(1)}, u32[]{:S(2)}, u32[]{:S(2)}) collective-permute-start(bf16[2,64,320]{2,1,0:T(8,128)(2,1)S(1)} %get-tuple-element.43), channel_id=1, source_target_pairs={{1,0},{2,1},{3,2},{4,3},{5,4},{6,5},{7,6},{0,7},{9,8},{10,9},{11,1... | collective-permute-start | bytes 245768 | tf_op jit(solution)/shard_map/ppermute | solution.py:590
  11.5 7.7 %collective-permute-start.4 = (bf16[1,2,64,320]{3,2,1,0:T(8,128)(2,1)S(1)}, bf16[1,2,64,320]{3,2,1,0:T(8,128)(2,1)S(1)}, u32[]{:S(2)}, u32[]{:S(2)}) collective-permute-start(bf16[1,2,64,320]{3,2,1,0:T(8,128)(2,1)S(1)} %get-tuple-element.48.refs_5_), channel_id=1, source_target_pairs={{0,8},{8,16},{16,24},{24,32},{32,40},{40,48},{48,56},{56,64},{64,7... | collective-permute-start | bytes 245768 | tf_op jit(solution)/shard_map/ppermute | solution.py:589
  11.6 7.6 %collective-permute-start.5 = (bf16[1,2,64,320]{3,2,1,0:T(8,128)(2,1)S(1)}, bf16[1,2,64,320]{3,2,1,0:T(8,128)(2,1)S(1)}, u32[]{:S(2)}, u32[]{:S(2)}) collective-permute-start(bf16[1,2,64,320]{3,2,1,0:T(8,128)(2,1)S(1)} %get-tuple-element.47.refs_4_), channel_id=1, source_target_pairs={{8,0},{16,8},{24,16},{32,24},{40,32},{48,40},{56,48},{64,56},{72,6... | collective-permute-start | bytes 245768 | tf_op jit(solution)/shard_map/ppermute | solution.py:590
  18.1 9.7 %copy-start.2 = (f32[320]{0:T(512)S(1)}, f32[320]{0:T(512)}, u32[]{:S(2)}) copy-start(f32[320]{0:T(512)} %param.14) | copy-start | bytes 3844
  18.1 9.7 %copy-start.1 = (bf16[1,1,32,1280]{3,2,1,0:T(8,128)(2,1)S(1)}, bf16[1,1,32,1280]{3,2,1,0:T(8,128)(2,1)}, u32[]{:S(2)}) copy-start(bf16[1,1,32,1280]{3,2,1,0:T(8,128)(2,1)} %param.21) | copy-start | bytes 245764
  20.3 10.9 %copy-start = (bf16[4,2,64,320]{3,2,1,0:T(8,128)(2,1)S(1)}, bf16[4,2,64,320]{3,2,1,0:T(8,128)(2,1)}, u32[]{:S(2)}) copy-start(bf16[4,2,64,320]{3,2,1,0:T(8,128)(2,1)} %refs_2_.6) | copy-start | bytes 983044
  20.3 10.8 %all-to-all-start = ((f32[8,8,128]{2,1,0:T(8,128)}), f32[8,8,128]{2,1,0:T(8,128)S(1)}, u32[]{:S(2)}, u32[]{:S(2)}) async-start(f32[8,8,128]{2,1,0:T(8,128)} %get-tuple-element.53.refs_3_), calls=%async_computation | async-start | bytes 65536 | tf_op jit(solution)/shard_map/all_to_all | solution.py:595
  32.7 18.5 %all-to-all-start.1 = ((bf16[32,16,128]{2,1,0:T(8,128)(2,1)}), bf16[32,16,128]{2,1,0:T(8,128)(2,1)S(1)}, u32[]{:S(2)}, u32[]{:S(2)}) async-start(bf16[32,16,128]{2,1,0:T(8,128)(2,1)} %get-tuple-element.57), calls=%async_computation.1 | async-start | bytes 262144 | tf_op jit(solution)/shard_map/all_to_all | solution.py:595
  53.8 16.0 %all-to-all-start.2 = ((bf16[32,16,128]{2,1,0:T(8,128)(2,1)}), bf16[32,16,128]{2,1,0:T(8,128)(2,1)S(1)}, u32[]{:S(2)}, u32[]{:S(2)}) async-start(bf16[32,16,128]{2,1,0:T(8,128)(2,1)} %shard_map.139), calls=%async_computation.2 | async-start | bytes 262144 | tf_op jit(solution)/shard_map/all_to_all | solution.py:595
  57.6 10.4 %collective-permute-start.6 = (bf16[144,320]{1,0:T(8,128)(2,1)S(1)}, bf16[144,320]{1,0:T(8,128)(2,1)S(1)}, u32[]{:S(2)}, u32[]{:S(2)}) collective-permute-start(bf16[144,320]{1,0:T(8,128)(2,1)S(1)} %get-tuple-element.63), channel_id=1, source_target_pairs={{0,8},{8,16},{16,24},{24,32},{32,40},{40,48},{48,56},{56,64},{64,7... | collective-permute-start | bytes 276488 | tf_op jit(solution)/shard_map/ppermute | solution.py:589
  57.9 10.2 %collective-permute-start.7 = (bf16[144,320]{1,0:T(8,128)(2,1)S(1)}, bf16[144,320]{1,0:T(8,128)(2,1)S(1)}, u32[]{:S(2)}, u32[]{:S(2)}) collective-permute-start(bf16[144,320]{1,0:T(8,128)(2,1)S(1)} %get-tuple-element.64), channel_id=1, source_target_pairs={{8,0},{16,8},{24,16},{32,24},{40,32},{48,40},{56,48},{64,56},{72,6... | collective-permute-start | bytes 276488 | tf_op jit(solution)/shard_map/ppermute | solution.py:590
  71.1 10.4 %all-to-all-start.3 = ((f32[8,16,128]{2,1,0:T(8,128)}), f32[8,16,128]{2,1,0:T(8,128)S(1)}, u32[]{:S(2)}, u32[]{:S(2)}) async-start(f32[8,16,128]{2,1,0:T(8,128)} %get-tuple-element.67.refs_5_), calls=%async_computation.3 | async-start | bytes 131072 | tf_op jit(solution)/shard_map/all_to_all | solution.py:595
  82.8 7.4 %collective-permute-start.8 = (bf16[4,64,320]{2,1,0:T(8,128)(2,1)S(1)}, bf16[4,64,320]{2,1,0:T(8,128)(2,1)S(1)}, u32[]{:S(2)}, u32[]{:S(2)}) collective-permute-start(bf16[4,64,320]{2,1,0:T(8,128)(2,1)S(1)} %get-tuple-element.75), channel_id=1, source_target_pairs={{0,1},{1,2},{2,3},{3,4},{4,5},{5,6},{6,7},{7,0},{8,9},{9,10},{10,1... | collective-permute-start | bytes 491528 | tf_op jit(solution)/shard_map/ppermute | solution.py:589
  85.6 8.3 %collective-permute-start.9 = (bf16[4,64,320]{2,1,0:T(8,128)(2,1)S(1)}, bf16[4,64,320]{2,1,0:T(8,128)(2,1)S(1)}, u32[]{:S(2)}, u32[]{:S(2)}) collective-permute-start(bf16[4,64,320]{2,1,0:T(8,128)(2,1)S(1)} %get-tuple-element.76), channel_id=1, source_target_pairs={{1,0},{2,1},{3,2},{4,3},{5,4},{6,5},{7,6},{0,7},{9,8},{10,9},{11,1... | collective-permute-start | bytes 491528 | tf_op jit(solution)/shard_map/ppermute | solution.py:590

commit v7 on v5

--- a/solution.py
+++ b/solution.py
@@ -203,8 +203,8 @@
 
 
 def spread(statistic, channels):
-    group = lax.broadcasted_iota(jnp.int32, (LANES, channels), 0)
-    channel = lax.broadcasted_iota(jnp.int32, (LANES, channels), 1)
+    group = lax.broadcasted_iota(jnp.int32, (statistic.shape[1], channels), 0)
+    channel = lax.broadcasted_iota(jnp.int32, (statistic.shape[1], channels), 1)
     return dot_sums(statistic, belong(channel, group, channels))
 
 
@@ -422,10 +422,14 @@
         add(grown[1], slope[here], normed[here])
     add(grown[2], beside_slope[1], after[:step])
     gain = jnp.concatenate([gain, jnp.zeros((1, SLOT - channels), f32)], axis=1)
-    count = 2 * (frames + 2)
+    sums = dot_sums(jnp.concatenate(firsts + seconds, axis=0), members(channels))
+    beside = LANES // GROUPS
+    count = sums.shape[0] // beside
     block = jnp.concatenate(
         [
-            dot_sums(jnp.concatenate(firsts + seconds, axis=0), members(channels)),
+            jnp.concatenate(
+                [sums[q * count : (q + 1) * count, :GROUPS] for q in range(beside)], axis=1
+            ),
             *[gain[:, k * LANES : (k + 1) * LANES] for k in range(SLOT // LANES)],
             jnp.zeros((stats.shape[1] - count - SLOT // LANES, LANES), f32),
         ],
@@ -486,9 +490,14 @@
     step = normed.shape[0] // frames
     count = frames + 2
     total = jnp.sum(stats[...], axis=0)
+    beside = LANES // GROUPS
+    held = 2 * count // beside
     for k in range(gain.shape[1] // LANES):
-        gain[:, k * LANES : (k + 1) * LANES] = total[2 * count + k : 2 * count + k + 1]
-    means = spread(total[: 2 * count] / cell_count, channels)
+        gain[:, k * LANES : (k + 1) * LANES] = total[held + k : held + k + 1]
+    sums = jnp.concatenate(
+        [total[:held, q * GROUPS : (q + 1) * GROUPS] for q in range(beside)], axis=0
+    )
+    means = spread(sums / cell_count, channels)
     at = lax.axis_index("frame")
 
     def coefficients(f):
@@ -763,7 +772,7 @@
     stats, grad_pooled, blended = call(
         lambda *refs: totals(*refs, frames=frames),
         (
-            shape((bands, 16, LANES), f32),
+            shape((bands, 8, LANES), f32),
             shape((3, half, channels), bf16),
             shape((half, width), bf16),
         ),

time: 96.4 us -> 96.4 us (level)
  no operation moved by 1% of the time
where the time goes in v7:
time: 96.4 us; the launch traced here: 95.7 us
  starting transfers between devices  44.7 us (46%)
  Pallas kernels  31.1 us (32%)
  waiting for transfers between devices  18.3 us (19%)
    pallas_call x16, Pallas kernels, call(): pl.pallas_call(body, out_shape=shapes[0] if single else shapes, in_specs=...  31.1 us
    all_to_all x4, starting transfers between devices, exchange(): lax.all_to_all(payload, axis, split_axis=0, concat_axis=0, tiled=True)  24.9 us
    ppermute x5, starting transfers between devices, neighbours(): lax.ppermute(head, axis, [((i + 1) % count, i) for i in range(count)])  10.6 us
    ppermute x5, starting transfers between devices, neighbours(): lax.ppermute(tail, axis, [(i, (i + 1) % count) for i in range(count)])  9.17 us
    all_to_all x4, waiting for transfers between devices, exchange(): lax.all_to_all(payload, axis, split_axis=0, concat_axis=0, tiled=True)  8.62 us
    ppermute x5, waiting for transfers between devices, neighbours(): lax.ppermute(tail, axis, [(i, (i + 1) % count) for i in range(count)])  5.96 us
    ppermute x5, waiting for transfers between devices, neighbours(): lax.ppermute(head, axis, [((i + 1) % count, i) for i in range(count)])  3.77 us
  transfers between devices with their start and end apart: 14, of which 8 were waited for; matrix products, arithmetic and copies ran while one was open for 1% of the time, Pallas kernels for 21%

profile of v7, /device:TPU:26, one launch (start us, length us, event | category | flops | bytes accessed | tf_op | source)
XLA Modules:
  0.0 95.7 jit_solution(15932428615405137475)
XLA Ops:
  1.7 2.0 %collective-permute-start.2 = (bf16[2,64,320]{2,1,0:T(8,128)(2,1)S(1)}, bf16[2,64,320]{2,1,0:T(8,128)(2,1)S(1)}, u32[]{:S(2)}, u32[]{:S(2)}) collective-permute-start(bf16[2,64,320]{2,1,0:T(8,128)(2,1)S(1)} %get-tuple-element.45), channel_id=1, source_target_pairs={{0,1},{1,2},{2,3},{3,4},{4,5},{5,6},{6,7},{7,0},{8,9},{9,10},{10,1... | collective-permute-start | bytes 245768 | tf_op jit(solution)/shard_map/ppermute | solution.py:596
  3.8 4.0 %collective-permute-start = (bf16[2,64,320]{2,1,0:T(8,128)(2,1)S(1)}, bf16[2,64,320]{2,1,0:T(8,128)(2,1)S(1)}, u32[]{:S(2)}, u32[]{:S(2)}) collective-permute-start(bf16[2,64,320]{2,1,0:T(8,128)(2,1)S(1)} %get-tuple-element.42), channel_id=1, source_target_pairs={{0,1},{1,2},{2,3},{3,4},{4,5},{5,6},{6,7},{7,0},{8,9},{9,10},{10,1... | collective-permute-start | bytes 245768 | tf_op jit(solution)/shard_map/ppermute | solution.py:596
  7.9 3.0 %shard_map.130 = (f32[2,256,320]{2,1,0:T(8,128)S(1)}, bf16[3,3,320,320]{3,2,1,0:T(8,128)(2,1)S(1)}) custom-call(bf16[4,2,64,320]{3,2,1,0:T(8,128)(2,1)} %refs_2_.4, bf16[3,3,320,320]{3,2,1,0:T(8,128)(2,1)} %refs_1_.9), custom_call_target="tpu_custom_call" | custom-call | tf_op jit(solution)/shard_map/pallas_call | solution.py:70
  11.6 5.3 %collective-permute-start.5 = (bf16[1,2,64,320]{3,2,1,0:T(8,128)(2,1)S(1)}, bf16[1,2,64,320]{3,2,1,0:T(8,128)(2,1)S(1)}, u32[]{:S(2)}, u32[]{:S(2)}) collective-permute-start(bf16[1,2,64,320]{3,2,1,0:T(8,128)(2,1)S(1)} %get-tuple-element.47.refs_4_), channel_id=1, source_target_pairs={{8,0},{16,8},{24,16},{32,24},{40,32},{48,40},{56,48},{64,56},{72,6... | collective-permute-start | bytes 245768 | tf_op jit(solution)/shard_map/ppermute | solution.py:597
  16.9 2.1 %shard_map.133 = (f32[512,320]{1,0:T(8,128)S(1)}, bf16[3,320,320]{2,1,0:T(8,128)(2,1)S(1)}, f32[8,320]{1,0:T(8,128)S(1)}) custom-call(f32[2,256,320]{2,1,0:T(8,128)S(1)} %get-tuple-element.41.refs_0_, bf16[2,64,320]{2,1,0:T(8,128)(2,1)S(1)} %collective-permute-done.refs_1_, bf16[2,64,320]{2,1,0:T(8,128)(2,1)S(1)} %collective-permute-done.1.refs_2_, ...), custom_call_target="tpu_custom_call" | custom-call | tf_op jit(solution)/shard_map/pallas_call | solution.py:70
  20.3 7.5 %all-to-all-start = ((f32[8,8,128]{2,1,0:T(8,128)}), f32[8,8,128]{2,1,0:T(8,128)S(1)}, u32[]{:S(2)}, u32[]{:S(2)}) async-start(f32[8,8,128]{2,1,0:T(8,128)} %get-tuple-element.53.refs_3_), calls=%async_computation | async-start | bytes 65536 | tf_op jit(solution)/shard_map/all_to_all | solution.py:602
  27.8 3.1 %shard_map.135 = (bf16[32,640]{1,0:T(8,128)(2,1)S(1)}, f32[32,320]{1,0:T(8,128)S(1)}) custom-call(bf16[32,1280]{1,0:T(8,128)(2,1)S(1)} %bitcast.2, bf16[320,1280]{1,0:T(8,128)(2,1)} %refs_1_.8, bf16[640,1280]{1,0:T(8,128)(2,1)} %refs_3_.3, f32[8,8,128]{2,1,0:T(8,128)} %get-tuple-element.53.refs_3_), custom_call_target="tpu_custom_call" | custom-call | tf_op jit(solution)/shard_map/pallas_call | solution.py:70
  31.2 1.5 %shard_map.136 = (bf16[32,16,128]{2,1,0:T(8,128)(2,1)}, bf16[32,320]{1,0:T(8,128)(2,1)S(1)}) custom-call(f32[512,320]{1,0:T(8,128)S(1)} %get-tuple-element.52.refs_0_, f32[8,8,128]{2,1,0:T(8,128)S(1)} %all-to-all-done.refs_1_, bf16[4,2,64,320]{3,2,1,0:T(8,128)(2,1)S(1)} %copy-done, f32[1,320]{1,0:T(1,128)S(1)} %reshape.15.refs_3_.refs_2_, ...), custom_call_target="tpu_custom_call" | custom-call | tf_op jit(solution)/shard_map/pallas_call | solution.py:70
  32.7 6.8 %all-to-all-start.1 = ((bf16[32,16,128]{2,1,0:T(8,128)(2,1)}), bf16[32,16,128]{2,1,0:T(8,128)(2,1)S(1)}, u32[]{:S(2)}, u32[]{:S(2)}) async-start(bf16[32,16,128]{2,1,0:T(8,128)(2,1)} %get-tuple-element.57), calls=%async_computation.1 | async-start | bytes 262144 | tf_op jit(solution)/shard_map/all_to_all | solution.py:602
  40.1 4.3 %shard_map.138 = (bf16[320,1920]{1,0:T(8,128)(2,1)S(1)}, f32[32,320]{1,0:T(8,128)S(1)}) custom-call(bf16[320,1280]{1,0:T(8,128)(2,1)} %refs_1_.8, bf16[1280,640]{1,0:T(8,128)(2,1)} %refs_1_.7, bf16[1280,640]{1,0:T(8,128)(2,1)} %refs_2_.5, bf16[1280,640]{1,0:T(8,128)(2,1)} %refs_3_.2, f32[10,32,32]{2,1,0:T(8,128)} %refs_4_.2, ...), custom_call_target="tpu_custom_call" | custom-call | tf_op jit(solution)/shard_map/pallas_call | solution.py:70
  44.4 6.9 %all-to-all-done.1.refs_0_ = bf16[32,16,128]{2,1,0:T(8,128)(2,1)S(1)} async-done(((bf16[32,16,128]{2,1,0:T(8,128)(2,1)}), bf16[32,16,128]{2,1,0:T(8,128)(2,1)S(1)}, u32[]{:S(2)}, u32[]{:S(2)}) %all-to-all-start.1) | async-done | bytes 131104 | tf_op jit(solution)/shard_map/all_to_all | solution.py:602
  51.3 2.5 %shard_map.139 = bf16[32,16,128]{2,1,0:T(8,128)(2,1)} custom-call(bf16[32,16,128]{2,1,0:T(8,128)(2,1)S(1)} %all-to-all-done.1.refs_0_, bf16[320,1920]{1,0:T(8,128)(2,1)S(1)} %get-tuple-element.59.refs_1_, f32[32,320]{1,0:T(8,128)S(1)} %get-tuple-element.60.refs_2_), custom_call_target="tpu_custom_call" | custom-call | tf_op jit(solution)/shard_map/pallas_call | solution.py:70
  53.8 3.9 %all-to-all-start.2 = ((bf16[32,16,128]{2,1,0:T(8,128)(2,1)}), bf16[32,16,128]{2,1,0:T(8,128)(2,1)S(1)}, u32[]{:S(2)}, u32[]{:S(2)}) async-start(bf16[32,16,128]{2,1,0:T(8,128)(2,1)} %shard_map.139), calls=%async_computation.2 | async-start | bytes 262144 | tf_op jit(solution)/shard_map/all_to_all | solution.py:602
  57.9 5.2 %collective-permute-start.7 = (bf16[144,320]{1,0:T(8,128)(2,1)S(1)}, bf16[144,320]{1,0:T(8,128)(2,1)S(1)}, u32[]{:S(2)}, u32[]{:S(2)}) collective-permute-start(bf16[144,320]{1,0:T(8,128)(2,1)S(1)} %get-tuple-element.64), channel_id=1, source_target_pairs={{8,0},{16,8},{24,16},{32,24},{40,32},{48,40},{56,48},{64,56},{72,6... | collective-permute-start | bytes 276488 | tf_op jit(solution)/shard_map/ppermute | solution.py:597
  63.1 5.0 %collective-permute-done.6.refs_0_.refs_3_.refs_5_ = bf16[144,320]{1,0:T(8,128)(2,1)S(1)} collective-permute-done((bf16[144,320]{1,0:T(8,128)(2,1)S(1)}, bf16[144,320]{1,0:T(8,128)(2,1)S(1)}, u32[]{:S(2)}, u32[]{:S(2)}) %collective-permute-start.6) | collective-permute-done | bytes 92192 | tf_op jit(solution)/shard_map/ppermute | solution.py:596
  68.2 1.6 %all-to-all-done.2.refs_0_ = bf16[32,16,128]{2,1,0:T(8,128)(2,1)S(1)} async-done(((bf16[32,16,128]{2,1,0:T(8,128)(2,1)}), bf16[32,16,128]{2,1,0:T(8,128)(2,1)S(1)}, u32[]{:S(2)}, u32[]{:S(2)}) %all-to-all-start.2) | async-done | bytes 131104 | tf_op jit(solution)/shard_map/all_to_all | solution.py:602
  69.8 1.3 %shard_map.141 = (f32[8,8,128]{2,1,0:T(8,128)}, bf16[3,32,320]{2,1,0:T(8,128)(2,1)S(1)}, bf16[32,640]{1,0:T(8,128)(2,1)S(1)}) custom-call(bf16[32,16,128]{2,1,0:T(8,128)(2,1)S(1)} %all-to-all-done.2.refs_0_, bf16[512,320]{1,0:T(8,128)(2,1)S(1)} %get-tuple-element.61.refs_1_.refs_2_, bf16[512,320]{1,0:T(8,128)(2,1)S(1)} %get-tuple-element.62.refs_2_.refs_3_, ...), custom_call_target="tpu_custom_call" | custom-call | tf_op jit(solution)/shard_map/pallas_call | solution.py:70
  71.1 6.8 %all-to-all-start.3 = ((f32[8,8,128]{2,1,0:T(8,128)}), f32[8,8,128]{2,1,0:T(8,128)S(1)}, u32[]{:S(2)}, u32[]{:S(2)}) async-start(f32[8,8,128]{2,1,0:T(8,128)} %get-tuple-element.67.refs_5_), calls=%async_computation.3 | async-start | bytes 65536 | tf_op jit(solution)/shard_map/all_to_all | solution.py:602
  77.9 3.5 %shard_map.142 = (bf16[32,1280]{1,0:T(8,128)(2,1)}, bf16[3,320,320]{2,1,0:T(8,128)(2,1)S(1)}) custom-call(bf16[32,320]{1,0:T(8,128)(2,1)S(1)} %get-tuple-element.56.refs_3_.refs_0_, bf16[320,1280]{1,0:T(8,128)(2,1)} %refs_1_.8, bf16[32,640]{1,0:T(8,128)(2,1)S(1)} %get-tuple-element.66.refs_2_, bf16[640,1280]{1,0:T(8,128)(2,1)} %refs_3_.3, ...), custom_call_target="tpu_custom_call" | custom-call | tf_op jit(solution)/shard_map/pallas_call | solution.py:70
  81.4 1.4 %shard_map.143 = (bf16[4,2,64,320]{3,2,1,0:T(8,128)(2,1)S(1)}, bf16[4,64,320]{2,1,0:T(8,128)(2,1)S(1)}, bf16[4,64,320]{2,1,0:T(8,128)(2,1)S(1)}, f32[1,384]{1,0:T(1,128)S(1)}) custom-call(f32[8,8,128]{2,1,0:T(8,128)S(1)} %all-to-all-done.3.refs_0_, bf16[3,32,320]{2,1,0:T(8,128)(2,1)S(1)} %get-tuple-element.69.refs_1_.refs_4_, ...), custom_call_target="tpu_custom_call" | custom-call | tf_op jit(solution)/shard_map/pallas_call | solution.py:70
  82.8 2.8 %collective-permute-start.8 = (bf16[4,64,320]{2,1,0:T(8,128)(2,1)S(1)}, bf16[4,64,320]{2,1,0:T(8,128)(2,1)S(1)}, u32[]{:S(2)}, u32[]{:S(2)}) collective-permute-start(bf16[4,64,320]{2,1,0:T(8,128)(2,1)S(1)} %get-tuple-element.75), channel_id=1, source_target_pairs={{0,1},{1,2},{2,3},{3,4},{4,5},{5,6},{6,7},{7,0},{8,9},{9,10},{10,1... | collective-permute-start | bytes 491528 | tf_op jit(solution)/shard_map/ppermute | solution.py:596
  85.6 3.2 %shard_map.144 = (f32[2,256,320]{2,1,0:T(8,128)S(1)}, bf16[3,3,320,320]{3,2,1,0:T(8,128)(2,1)S(1)}) custom-call(bf16[4,2,64,320]{3,2,1,0:T(8,128)(2,1)S(1)} %get-tuple-element.73.refs_0_, bf16[3,3,320,320]{3,2,1,0:T(8,128)(2,1)} %refs_1_.9), custom_call_target="tpu_custom_call" | custom-call | tf_op jit(solution)/shard_map/pallas_call | solution.py:70
  90.2 3.7 %collective-permute-done.9.refs_2_ = bf16[4,64,320]{2,1,0:T(8,128)(2,1)S(1)} collective-permute-done((bf16[4,64,320]{2,1,0:T(8,128)(2,1)S(1)}, bf16[4,64,320]{2,1,0:T(8,128)(2,1)S(1)}, u32[]{:S(2)}, u32[]{:S(2)}) %collective-permute-start.9) | collective-permute-done | bytes 163872 | tf_op jit(solution)/shard_map/ppermute | solution.py:597
  93.9 1.6 %shard_map.145 = bf16[4,2,64,320]{3,2,1,0:T(8,128)(2,1)} custom-call(f32[2,256,320]{2,1,0:T(8,128)S(1)} %get-tuple-element.74.refs_0_, bf16[4,64,320]{2,1,0:T(8,128)(2,1)S(1)} %collective-permute-done.8.refs_1_, bf16[4,64,320]{2,1,0:T(8,128)(2,1)S(1)} %collective-permute-done.9.refs_2_, bf16[3,3,320,320]{3,2,1,0:T(8,128)(2,1)S(1)} %get-tuple-element.77.refs_3_, ...), custom_call_target="tpu_custom_call" | custom-call | tf_op jit(solution)/shard_map/pallas_call | solution.py:70
  (28 shorter events, 5.7 us)
Async XLA Ops:
  1.7 9.1 %collective-permute-start.2 = (bf16[2,64,320]{2,1,0:T(8,128)(2,1)S(1)}, bf16[2,64,320]{2,1,0:T(8,128)(2,1)S(1)}, u32[]{:S(2)}, u32[]{:S(2)}) collective-permute-start(bf16[2,64,320]{2,1,0:T(8,128)(2,1)S(1)} %get-tuple-element.45), channel_id=1, source_target_pairs={{0,1},{1,2},{2,3},{3,4},{4,5},{5,6},{6,7},{7,0},{8,9},{9,10},{10,1... | collective-permute-start | bytes 245768 | tf_op jit(solution)/shard_map/ppermute | solution.py:596
  3.7 7.2 %collective-permute-start.3 = (bf16[2,64,320]{2,1,0:T(8,128)(2,1)S(1)}, bf16[2,64,320]{2,1,0:T(8,128)(2,1)S(1)}, u32[]{:S(2)}, u32[]{:S(2)}) collective-permute-start(bf16[2,64,320]{2,1,0:T(8,128)(2,1)S(1)} %get-tuple-element.46), channel_id=1, source_target_pairs={{1,0},{2,1},{3,2},{4,3},{5,4},{6,5},{7,6},{0,7},{9,8},{10,9},{11,1... | collective-permute-start | bytes 245768 | tf_op jit(solution)/shard_map/ppermute | solution.py:597
  3.8 13.1 %collective-permute-start = (bf16[2,64,320]{2,1,0:T(8,128)(2,1)S(1)}, bf16[2,64,320]{2,1,0:T(8,128)(2,1)S(1)}, u32[]{:S(2)}, u32[]{:S(2)}) collective-permute-start(bf16[2,64,320]{2,1,0:T(8,128)(2,1)S(1)} %get-tuple-element.42), channel_id=1, source_target_pairs={{0,1},{1,2},{2,3},{3,4},{4,5},{5,6},{6,7},{7,0},{8,9},{9,10},{10,1... | collective-permute-start | bytes 245768 | tf_op jit(solution)/shard_map/ppermute | solution.py:596
  7.9 9.1 %collective-permute-start.1 = (bf16[2,64,320]{2,1,0:T(8,128)(2,1)S(1)}, bf16[2,64,320]{2,1,0:T(8,128)(2,1)S(1)}, u32[]{:S(2)}, u32[]{:S(2)}) collective-permute-start(bf16[2,64,320]{2,1,0:T(8,128)(2,1)S(1)} %get-tuple-element.43), channel_id=1, source_target_pairs={{1,0},{2,1},{3,2},{4,3},{5,4},{6,5},{7,6},{0,7},{9,8},{10,9},{11,1... | collective-permute-start | bytes 245768 | tf_op jit(solution)/shard_map/ppermute | solution.py:597
  11.5 7.7 %collective-permute-start.4 = (bf16[1,2,64,320]{3,2,1,0:T(8,128)(2,1)S(1)}, bf16[1,2,64,320]{3,2,1,0:T(8,128)(2,1)S(1)}, u32[]{:S(2)}, u32[]{:S(2)}) collective-permute-start(bf16[1,2,64,320]{3,2,1,0:T(8,128)(2,1)S(1)} %get-tuple-element.48.refs_5_), channel_id=1, source_target_pairs={{0,8},{8,16},{16,24},{24,32},{32,40},{40,48},{48,56},{56,64},{64,7... | collective-permute-start | bytes 245768 | tf_op jit(solution)/shard_map/ppermute | solution.py:596
  11.6 7.6 %collective-permute-start.5 = (bf16[1,2,64,320]{3,2,1,0:T(8,128)(2,1)S(1)}, bf16[1,2,64,320]{3,2,1,0:T(8,128)(2,1)S(1)}, u32[]{:S(2)}, u32[]{:S(2)}) collective-permute-start(bf16[1,2,64,320]{3,2,1,0:T(8,128)(2,1)S(1)} %get-tuple-element.47.refs_4_), channel_id=1, source_target_pairs={{8,0},{16,8},{24,16},{32,24},{40,32},{48,40},{56,48},{64,56},{72,6... | collective-permute-start | bytes 245768 | tf_op jit(solution)/shard_map/ppermute | solution.py:597
  19.0 8.8 %copy-start.2 = (f32[320]{0:T(512)S(1)}, f32[320]{0:T(512)}, u32[]{:S(2)}) copy-start(f32[320]{0:T(512)} %param.14) | copy-start | bytes 3844
  19.0 8.8 %copy-start.1 = (bf16[1,1,32,1280]{3,2,1,0:T(8,128)(2,1)S(1)}, bf16[1,1,32,1280]{3,2,1,0:T(8,128)(2,1)}, u32[]{:S(2)}) copy-start(bf16[1,1,32,1280]{3,2,1,0:T(8,128)(2,1)} %param.21) | copy-start | bytes 245764
  20.3 10.8 %copy-start = (bf16[4,2,64,320]{3,2,1,0:T(8,128)(2,1)S(1)}, bf16[4,2,64,320]{3,2,1,0:T(8,128)(2,1)}, u32[]{:S(2)}) copy-start(bf16[4,2,64,320]{3,2,1,0:T(8,128)(2,1)} %refs_2_.4) | copy-start | bytes 983044
  20.3 10.8 %all-to-all-start = ((f32[8,8,128]{2,1,0:T(8,128)}), f32[8,8,128]{2,1,0:T(8,128)S(1)}, u32[]{:S(2)}, u32[]{:S(2)}) async-start(f32[8,8,128]{2,1,0:T(8,128)} %get-tuple-element.53.refs_3_), calls=%async_computation | async-start | bytes 65536 | tf_op jit(solution)/shard_map/all_to_all | solution.py:602
  32.7 18.5 %all-to-all-start.1 = ((bf16[32,16,128]{2,1,0:T(8,128)(2,1)}), bf16[32,16,128]{2,1,0:T(8,128)(2,1)S(1)}, u32[]{:S(2)}, u32[]{:S(2)}) async-start(bf16[32,16,128]{2,1,0:T(8,128)(2,1)} %get-tuple-element.57), calls=%async_computation.1 | async-start | bytes 262144 | tf_op jit(solution)/shard_map/all_to_all | solution.py:602
  53.8 16.0 %all-to-all-start.2 = ((bf16[32,16,128]{2,1,0:T(8,128)(2,1)}), bf16[32,16,128]{2,1,0:T(8,128)(2,1)S(1)}, u32[]{:S(2)}, u32[]{:S(2)}) async-start(bf16[32,16,128]{2,1,0:T(8,128)(2,1)} %shard_map.139), calls=%async_computation.2 | async-start | bytes 262144 | tf_op jit(solution)/shard_map/all_to_all | solution.py:602
  57.6 10.4 %collective-permute-start.6 = (bf16[144,320]{1,0:T(8,128)(2,1)S(1)}, bf16[144,320]{1,0:T(8,128)(2,1)S(1)}, u32[]{:S(2)}, u32[]{:S(2)}) collective-permute-start(bf16[144,320]{1,0:T(8,128)(2,1)S(1)} %get-tuple-element.63), channel_id=1, source_target_pairs={{0,8},{8,16},{16,24},{24,32},{32,40},{40,48},{48,56},{56,64},{64,7... | collective-permute-start | bytes 276488 | tf_op jit(solution)/shard_map/ppermute | solution.py:596
  57.9 10.2 %collective-permute-start.7 = (bf16[144,320]{1,0:T(8,128)(2,1)S(1)}, bf16[144,320]{1,0:T(8,128)(2,1)S(1)}, u32[]{:S(2)}, u32[]{:S(2)}) collective-permute-start(bf16[144,320]{1,0:T(8,128)(2,1)S(1)} %get-tuple-element.64), channel_id=1, source_target_pairs={{8,0},{16,8},{24,16},{32,24},{40,32},{48,40},{56,48},{64,56},{72,6... | collective-permute-start | bytes 276488 | tf_op jit(solution)/shard_map/ppermute | solution.py:597
  71.1 10.3 %all-to-all-start.3 = ((f32[8,8,128]{2,1,0:T(8,128)}), f32[8,8,128]{2,1,0:T(8,128)S(1)}, u32[]{:S(2)}, u32[]{:S(2)}) async-start(f32[8,8,128]{2,1,0:T(8,128)} %get-tuple-element.67.refs_5_), calls=%async_computation.3 | async-start | bytes 65536 | tf_op jit(solution)/shard_map/all_to_all | solution.py:602
  82.8 7.4 %collective-permute-start.8 = (bf16[4,64,320]{2,1,0:T(8,128)(2,1)S(1)}, bf16[4,64,320]{2,1,0:T(8,128)(2,1)S(1)}, u32[]{:S(2)}, u32[]{:S(2)}) collective-permute-start(bf16[4,64,320]{2,1,0:T(8,128)(2,1)S(1)} %get-tuple-element.75), channel_id=1, source_target_pairs={{0,1},{1,2},{2,3},{3,4},{4,5},{5,6},{6,7},{7,0},{8,9},{9,10},{10,1... | collective-permute-start | bytes 491528 | tf_op jit(solution)/shard_map/ppermute | solution.py:596
  85.6 8.3 %collective-permute-start.9 = (bf16[4,64,320]{2,1,0:T(8,128)(2,1)S(1)}, bf16[4,64,320]{2,1,0:T(8,128)(2,1)S(1)}, u32[]{:S(2)}, u32[]{:S(2)}) collective-permute-start(bf16[4,64,320]{2,1,0:T(8,128)(2,1)S(1)} %get-tuple-element.76), channel_id=1, source_target_pairs={{1,0},{2,1},{3,2},{4,3},{5,4},{6,5},{7,6},{0,7},{9,8},{10,9},{11,1... | collective-permute-start | bytes 491528 | tf_op jit(solution)/shard_map/ppermute | solution.py:597
